TPU v7x, 32 devices: a whole 2x2x4 slice. The times are simulated.
32 devices in a mesh: section: 2 (over x), dp: 8 (over z, core), tensor: 2 (over y).
Axes of the slice: x: 2, y: 2, z: 4, core: 2. Of those that a mesh axis runs over, the one named last changes fastest.
Arguments:
- layer_input: bfloat16 [2, 2048, 2048], P(None, ('dp', 'tensor')), may hold values from -6 to 6
- segment_ids: int32 [2, 2048], P(None, 'dp'), may hold values from 0 to 2, as said below
- output_grad: bfloat16 [2, 2048, 2048], P(None, ('dp', 'tensor')), may hold values from -6 to 6
- query_weight: bfloat16 [2, 2048, 2048], P('section', 'dp', 'tensor'), may hold values from -0.125 to 0.125
- key_weight: bfloat16 [2, 2048, 2048], P('section', 'dp', 'tensor'), may hold values from -0.125 to 0.125
- value_weight: bfloat16 [2, 2048, 4096], P('section', 'dp', 'tensor'), may hold values from -0.125 to 0.125
- swish_weight: bfloat16 [2, 2048, 4096], P('section', 'dp', 'tensor'), may hold values from -0.125 to 0.125
- output_weight: bfloat16 [2, 4096, 2048], P('section', 'tensor', 'dp'), may hold values from -0.09375 to 0.09375
- gate_weight: bfloat16 [2, 2048, 4096], P('section', 'dp', 'tensor'), may hold values from -0.125 to 0.125
- up_weight: bfloat16 [2, 2048, 4096], P('section', 'dp', 'tensor'), may hold values from -0.125 to 0.125
- down_weight: bfloat16 [2, 4096, 2048], P('section', 'tensor', 'dp'), may hold values from -0.09375 to 0.09375
- mixer_gain: float32 [2, 2048], P('section'), may hold values from 0.25 to 1.75
- ffn_gain: float32 [2, 2048], P('section'), may hold values from 0.25 to 1.75
Outputs:
- layer_outputs: bfloat16 [2, 2, 2048, 2048], P('section', None, ('dp', 'tensor'))
- input_grads: bfloat16 [2, 2, 2048, 2048], P('section', None, ('dp', 'tensor'))
- grad_query: float32 [2, 2048, 2048], P('section', 'dp', 'tensor')
- grad_key: float32 [2, 2048, 2048], P('section', 'dp', 'tensor')
- grad_value: float32 [2, 2048, 4096], P('section', 'dp', 'tensor')
- grad_swish: float32 [2, 2048, 4096], P('section', 'dp', 'tensor')
- grad_output: float32 [2, 4096, 2048], P('section', 'tensor', 'dp')
- grad_gate: float32 [2, 2048, 4096], P('section', 'dp', 'tensor')
- grad_up: float32 [2, 2048, 4096], P('section', 'dp', 'tensor')
- grad_down: float32 [2, 4096, 2048], P('section', 'tensor', 'dp')
- grad_mixer_gain: float32 [2, 2048], P('section')
- grad_ffn_gain: float32 [2, 2048], P('section')
Inputs may be any that keep to these rules, and one draw needn't show every extreme that they name: `segment_ids`: within each sequence of 256 tokens the numbers start at 0 and rise by one at each of exactly two document boundaries: one among positions 64 to 95, one among positions 160 to 192.
All inputs are finite; a program needn't handle non-finite values.
Results may differ from a plain program's by a relative error of at most 0.03.
Values may be sent and summed in bfloat16 or wider, within the bound.
A program may use at most 576 MiB of HBM per device.

v0:
```python
import jax
import jax.numpy as jnp
from jax import lax
from jax.sharding import PartitionSpec as P

HEAD_K = 256
HEAD_V = 512


epsilon = 1e-05
group_guard = 1.0


def passed_along(shard, axis, by):
    length = lax.axis_size(axis)
    pairs = [(i, i + by) for i in range(length) if 0 <= i + by < length]
    return lax.ppermute(shard, axis, pairs)


def layer_norm(values, gain):
    centred = values - jnp.mean(values, axis=-1, keepdims=True)
    spread = jnp.mean(centred * centred, axis=-1, keepdims=True)
    return centred * lax.rsqrt(spread + epsilon) * gain


def group_norm(mixed):
    centred = mixed - jnp.mean(mixed, axis=-1, keepdims=True)
    spread = jnp.mean(centred * centred, axis=-1, keepdims=True)
    return centred * lax.rsqrt(spread + group_guard)


def rotation_tables(length, half_width):
    pair_index = jnp.arange(half_width).astype(jnp.float32)
    position = jnp.arange(length).astype(jnp.float32)[:, None]
    angle = position * jnp.exp(-jnp.log(10000.0) * pair_index / half_width)
    zeta = (pair_index / half_width + 0.4) / 1.4
    growth = jnp.exp(position / 512.0 * jnp.log(zeta))
    return (jnp.cos(angle), jnp.sin(angle), growth)


def rotate(values, cosine, sine, growth):
    half_width = values.shape[-1] // 2
    first_half = values[..., :half_width]
    second_half = values[..., half_width:]
    cos_table = cosine[:, None, :]
    sin_table = sine[:, None, :]
    scale_table = growth[:, None, :]
    return jnp.concatenate(
        [
            (first_half * cos_table - second_half * sin_table) * scale_table,
            (first_half * sin_table + second_half * cos_table) * scale_table,
        ],
        axis=-1,
    )


def unrotate(grads, cosine, sine, growth):
    half_width = grads.shape[-1] // 2
    cos_table = cosine[:, None, :]
    sin_table = sine[:, None, :]
    scale_table = growth[:, None, :]
    first_half = grads[..., :half_width] * scale_table
    second_half = grads[..., half_width:] * scale_table
    return jnp.concatenate(
        [
            first_half * cos_table + second_half * sin_table,
            second_half * cos_table - first_half * sin_table,
        ],
        axis=-1,
    )


def decay_mask(segments, first_head, heads):
    length = segments.shape[-1]
    position = jnp.arange(length)
    earlier = position[:, None] >= position[None, :]
    same_doc = (segments[:, None] == segments[None, :]) & earlier
    distance = jnp.maximum(position[:, None] - position[None, :], 0).astype(jnp.float32)
    head_index = (first_head + jnp.arange(heads)).astype(jnp.float32)
    log_rate = jnp.log(1.0 - jnp.exp2(-5.0 - head_index))
    return jnp.where(same_doc[None], jnp.exp(log_rate[:, None, None] * distance[None]), 0.0)


def gelu_product(gate, up_part):
    return jax.nn.gelu(gate) * up_part


def weight_terms(pairs):
    return tuple(
        (
            jnp.einsum("tc,te->ce", left_rows, right_rows, preferred_element_type=jnp.float32)
            for left_rows, right_rows in pairs
        )
    )


def pack_terms(terms):
    columns = [
        one_term.T if member in (4, 7) else one_term for member, one_term in enumerate(terms)
    ]
    return jnp.concatenate(columns, axis=1)


def unpack_terms(packed, widths):
    pieces = []
    offset = 0
    for member, count in enumerate(widths):
        piece = packed[:, offset : offset + count]
        offset = offset + count
        pieces.append(piece.T if member in (4, 7) else piece)
    return tuple(pieces)


def on_device(
    layer_input,
    segment_ids,
    output_grad,
    query_weight,
    key_weight,
    value_weight,
    swish_weight,
    output_weight,
    gate_weight,
    up_weight,
    down_weight,
    mixer_gain,
    ffn_gain,
):
    section_first = lax.axis_index("section") == 0
    gathered = (
        lax.all_gather(query_weight[0], "dp", axis=0, tiled=True),
        lax.all_gather(key_weight[0], "dp", axis=0, tiled=True),
        lax.all_gather(value_weight[0], "dp", axis=0, tiled=True),
        lax.all_gather(swish_weight[0], "dp", axis=0, tiled=True),
        lax.all_gather(output_weight[0], "dp", axis=1, tiled=True),
        lax.all_gather(gate_weight[0], "dp", axis=0, tiled=True),
        lax.all_gather(up_weight[0], "dp", axis=0, tiled=True),
        lax.all_gather(down_weight[0], "dp", axis=1, tiled=True),
    )
    query_full, key_full, value_full, swish_full, output_full, gate_full, up_full, down_full = (
        gathered
    )
    widths = (
        query_full.shape[1],
        key_full.shape[1],
        value_full.shape[1],
        swish_full.shape[1],
        output_full.shape[0],
        gate_full.shape[1],
        up_full.shape[1],
        down_full.shape[0],
    )
    mixer_scale = mixer_gain[0]
    ffn_scale = ffn_gain[0]
    batches = layer_input.shape[0]
    rows_here = layer_input.shape[1]
    width = layer_input.shape[2]
    length = segment_ids.shape[1]
    heads_here = query_full.shape[1] // HEAD_K
    first_head = lax.axis_index("tensor") * heads_here
    cosine, sine, growth = rotation_tables(length, HEAD_K // 2)
    shrink = 1.0 / growth
    score_scale = HEAD_K ** (-0.5)

    def select(first_value, second_value):
        return jax.tree.map(
            lambda one_side, other_side: jnp.where(section_first, one_side, other_side),
            first_value,
            second_value,
        )

    def backward(grad_out, saved, masks):
        (
            hidden_in,
            middle,
            normed_in,
            query_rot,
            key_rot,
            value,
            gate_pre,
            mixed,
            merged,
            normed_mid,
            gate,
            up_part,
            hidden,
        ) = saved
        grad_down = lax.all_gather(grad_out.astype(jnp.bfloat16), "tensor", axis=0, tiled=True)
        grad_hidden = jnp.einsum(
            "td,fd->tf", grad_down, down_full, preferred_element_type=jnp.float32
        )
        _, act_pull = jax.vjp(gelu_product, gate, up_part)
        grad_gate, grad_up = act_pull(grad_hidden)
        grad_gate = grad_gate.astype(jnp.bfloat16)
        grad_up = grad_up.astype(jnp.bfloat16)
        grad_mid_norm = jnp.einsum(
            "tf,df->td", grad_gate, gate_full, preferred_element_type=jnp.float32
        ) + jnp.einsum("tf,df->td", grad_up, up_full, preferred_element_type=jnp.float32)
        grad_mid_norm = lax.psum_scatter(grad_mid_norm, "tensor", scatter_dimension=0, tiled=True)
        _, norm_pull = jax.vjp(layer_norm, middle, ffn_scale)
        grad_through, ffn_term = norm_pull(grad_mid_norm)
        grad_middle = grad_out + grad_through
        grad_branch = lax.all_gather(grad_middle.astype(jnp.bfloat16), "tensor", axis=0, tiled=True)
        grad_merged = jnp.einsum(
            "td,vd->tv", grad_branch, output_full, preferred_element_type=jnp.float32
        )

        def gated_norm(mixed_part, gate_part):
            return group_norm(mixed_part).reshape(length, -1) * jax.nn.silu(gate_part)

        _, gate_pull = jax.vjp(gated_norm, mixed, gate_pre)
        grad_mixed, grad_gate_pre = gate_pull(grad_merged)
        grad_mixed = grad_mixed.astype(jnp.bfloat16)
        grad_gate_pre = grad_gate_pre.astype(jnp.bfloat16)
        product = jnp.einsum("thd,shd->hts", query_rot, key_rot, preferred_element_type=jnp.float32)
        weight = (product * score_scale * masks).astype(jnp.bfloat16)
        grad_weight = jnp.einsum(
            "thv,shv->hts", grad_mixed, value, preferred_element_type=jnp.float32
        )
        grad_product = (grad_weight * score_scale * masks).astype(jnp.bfloat16)
        grad_value = (
            jnp.einsum("hts,thv->shv", weight, grad_mixed, preferred_element_type=jnp.float32)
            .astype(jnp.bfloat16)
            .reshape(length, -1)
        )
        grad_qrot = jnp.einsum(
            "hts,shd->thd", grad_product, key_rot, preferred_element_type=jnp.float32
        )
        grad_krot = jnp.einsum(
            "hts,thd->shd", grad_product, query_rot, preferred_element_type=jnp.float32
        )
        grad_query = (
            unrotate(grad_qrot, cosine, sine, growth).astype(jnp.bfloat16).reshape(length, -1)
        )
        grad_key = (
            unrotate(grad_krot, cosine, sine, shrink).astype(jnp.bfloat16).reshape(length, -1)
        )
        grad_normed = (
            jnp.einsum("tc,dc->td", grad_query, query_full, preferred_element_type=jnp.float32)
            + jnp.einsum("tc,dc->td", grad_key, key_full, preferred_element_type=jnp.float32)
            + jnp.einsum("tc,dc->td", grad_value, value_full, preferred_element_type=jnp.float32)
            + jnp.einsum("tc,dc->td", grad_gate_pre, swish_full, preferred_element_type=jnp.float32)
        )
        grad_normed = lax.psum_scatter(grad_normed, "tensor", scatter_dimension=0, tiled=True)
        _, first_pull = jax.vjp(layer_norm, hidden_in, mixer_scale)
        grad_first, mixer_term = first_pull(grad_normed)
        grad_input = grad_middle + grad_first
        pairs = (
            (normed_in, grad_query),
            (normed_in, grad_key),
            (normed_in, grad_value),
            (normed_in, grad_gate_pre),
            (merged, grad_branch),
            (normed_mid, grad_gate),
            (normed_mid, grad_up),
            (hidden, grad_down),
        )
        return (grad_input, pairs, mixer_term, ffn_term)

    received = jnp.zeros((rows_here, width), jnp.bfloat16)
    results = []
    caches = []
    tick_masks = []
    for turn_index in range(batches + 1):
        own_rows = layer_input[min(turn_index, batches - 1)]
        ids_here = jnp.where(
            section_first,
            segment_ids[min(turn_index, batches - 1)],
            segment_ids[max(turn_index - 1, 0)],
        )
        masks = decay_mask(ids_here, first_head, heads_here)
        forward_hidden_in = jnp.where(section_first, own_rows, received).astype(jnp.float32)
        forward_normed_in = lax.all_gather(
            layer_norm(forward_hidden_in, mixer_scale).astype(jnp.bfloat16),
            "tensor",
            axis=0,
            tiled=True,
        )
        query = jnp.dot(forward_normed_in, query_full, preferred_element_type=jnp.float32).reshape(
            length, heads_here, HEAD_K
        )
        key_proj = jnp.dot(forward_normed_in, key_full, preferred_element_type=jnp.float32).reshape(
            length, heads_here, HEAD_K
        )
        forward_value = (
            jnp.dot(forward_normed_in, value_full, preferred_element_type=jnp.float32)
            .astype(jnp.bfloat16)
            .reshape(length, heads_here, HEAD_V)
        )
        forward_gate_pre = jnp.dot(
            forward_normed_in, swish_full, preferred_element_type=jnp.float32
        )
        forward_query_rot = rotate(query, cosine, sine, growth).astype(jnp.bfloat16)
        forward_key_rot = rotate(key_proj, cosine, sine, shrink).astype(jnp.bfloat16)
        forward_product = jnp.einsum(
            "thd,shd->hts", forward_query_rot, forward_key_rot, preferred_element_type=jnp.float32
        )
        forward_weight = (forward_product * score_scale * masks).astype(jnp.bfloat16)
        forward_mixed = jnp.einsum(
            "hts,shv->thv", forward_weight, forward_value, preferred_element_type=jnp.float32
        )
        forward_merged = (
            group_norm(forward_mixed).reshape(length, -1) * jax.nn.silu(forward_gate_pre)
        ).astype(jnp.bfloat16)
        branch = jnp.dot(forward_merged, output_full, preferred_element_type=jnp.float32)
        forward_middle = forward_hidden_in + lax.psum_scatter(
            branch, "tensor", scatter_dimension=0, tiled=True
        )
        forward_normed_mid = lax.all_gather(
            layer_norm(forward_middle, ffn_scale).astype(jnp.bfloat16), "tensor", axis=0, tiled=True
        )
        forward_gate = jnp.dot(forward_normed_mid, gate_full, preferred_element_type=jnp.float32)
        forward_up_part = jnp.dot(forward_normed_mid, up_full, preferred_element_type=jnp.float32)
        forward_hidden = gelu_product(forward_gate, forward_up_part).astype(jnp.bfloat16)
        feed = jnp.dot(forward_hidden, down_full, preferred_element_type=jnp.float32)
        result = forward_middle + lax.psum_scatter(feed, "tensor", scatter_dimension=0, tiled=True)
        forward_saved = (
            forward_hidden_in,
            forward_middle,
            forward_normed_in,
            forward_query_rot,
            forward_key_rot,
            forward_value,
            forward_gate_pre,
            forward_mixed,
            forward_merged,
            forward_normed_mid,
            forward_gate,
            forward_up_part,
            forward_hidden,
        )
        result, saved = (result, forward_saved)
        sent = result.astype(jnp.bfloat16)
        if turn_index < batches:
            received = passed_along(sent, "section", 1)
        results.append(sent)
        caches.append(saved)
        tick_masks.append(masks)
    returned = jnp.zeros((rows_here, width), jnp.bfloat16)
    grads_in = []
    stored = []
    packed_total = None
    mixer_total = jnp.zeros((width,), jnp.float32)
    ffn_total = jnp.zeros((width,), jnp.float32)
    for turn_index in range(batches + 1):
        later_tick = min(turn_index + 1, batches)
        earlier_tick = max(turn_index - 1, 0)
        saved = select(caches[earlier_tick], caches[later_tick])
        masks = jnp.where(section_first, tick_masks[earlier_tick], tick_masks[later_tick])
        grad_out = jnp.where(
            section_first, returned, output_grad[min(turn_index, batches - 1)]
        ).astype(jnp.float32)
        usable = jnp.where(section_first, turn_index >= 1, turn_index < batches)
        grad_input, pairs, mixer_term, ffn_term = backward(grad_out, saved, masks)
        mixer_total = mixer_total + jnp.where(usable, mixer_term, 0.0)
        ffn_total = ffn_total + jnp.where(usable, ffn_term, 0.0)
        sent_back = grad_input.astype(jnp.bfloat16)
        if turn_index < batches:
            returned = passed_along(sent_back, "section", -1)
        grads_in.append(sent_back)
        stored.append(pairs)
    chosen = [select(stored[index + 1], stored[index]) for index in range(batches)]
    joined = tuple(
        (
            (
                jnp.concatenate([entry[member][0] for entry in chosen], axis=0),
                jnp.concatenate([entry[member][1] for entry in chosen], axis=0),
            )
            for member in range(8)
        )
    )
    packed_total = lax.psum_scatter(
        pack_terms(weight_terms(joined)).astype(jnp.bfloat16), "dp", scatter_dimension=0, tiled=True
    ).astype(jnp.float32)
    shard_totals = unpack_terms(packed_total, widths)
    mixer_sum, ffn_sum = lax.psum((mixer_total, ffn_total), ("dp", "tensor"))
    layer_outputs = jnp.stack(
        [jnp.where(section_first, results[index], results[index + 1]) for index in range(batches)]
    )[None]
    input_grads = jnp.stack(
        [jnp.where(section_first, grads_in[index + 1], grads_in[index]) for index in range(batches)]
    )[None]
    return (
        layer_outputs,
        input_grads,
        shard_totals[0][None],
        shard_totals[1][None],
        shard_totals[2][None],
        shard_totals[3][None],
        shard_totals[4][None],
        shard_totals[5][None],
        shard_totals[6][None],
        shard_totals[7][None],
        mixer_sum[None],
        ffn_sum[None],
    )


def solution(mesh):
    in_specs = (
        P(None, ("dp", "tensor"), None),
        P(None, "dp"),
        P(None, ("dp", "tensor"), None),
        P("section", "dp", "tensor"),
        P("section", "dp", "tensor"),
        P("section", "dp", "tensor"),
        P("section", "dp", "tensor"),
        P("section", "tensor", "dp"),
        P("section", "dp", "tensor"),
        P("section", "dp", "tensor"),
        P("section", "tensor", "dp"),
        P("section", None),
        P("section", None),
    )
    out_specs = (
        P("section", None, ("dp", "tensor"), None),
        P("section", None, ("dp", "tensor"), None),
        P("section", "dp", "tensor"),
        P("section", "dp", "tensor"),
        P("section", "dp", "tensor"),
        P("section", "dp", "tensor"),
        P("section", "tensor", "dp"),
        P("section", "dp", "tensor"),
        P("section", "dp", "tensor"),
        P("section", "tensor", "dp"),
        P("section", None),
        P("section", None),
    )
    return jax.shard_map(
        on_device, mesh=mesh, in_specs=in_specs, out_specs=out_specs, check_vma=False
    )
```

profile of v0, /device:TPU:5, one launch (start us, length us, event | category | flops | bytes accessed | tf_op | source)
XLA Modules:
  0.0 2218.2 jit_solution(3032113394214278732)
XLA Ops:
  16.8 16.8 all-gather.30.cloned.1.call-done
  33.6 50.2 %all-gather.56.cloned.1.call-done = bf16[1,2048,1024]{2,1,0:T(8,128)(2,1)} async-done(((bf16[1,256,1024]{2,1,0:T(8,128)(2,1)}), bf16[1,2048,1024]{2,1,0:T(8,128)(2,1)}) %all-gather.56.cloned.1.call-update) | async-done | bytes 4194320 | tf_op jit(solution)/shard_map/all_gather | solution.py:132
  88.0 43.2 %all-gather.54.cloned.1.call-done = bf16[1,2048,1024]{2,1,0:T(8,128)(2,1)} async-done(((bf16[1,256,1024]{2,1,0:T(8,128)(2,1)}), bf16[1,2048,1024]{2,1,0:T(8,128)(2,1)}) %all-gather.54.cloned.1.call-update) | async-done | bytes 4194320 | tf_op jit(solution)/shard_map/all_gather | solution.py:131
  136.2 77.3 %all-gather.52.cloned.1.call-done = bf16[1,2048,2048]{2,1,0:T(8,128)(2,1)} async-done(((bf16[1,256,2048]{2,1,0:T(8,128)(2,1)}), bf16[1,2048,2048]{2,1,0:T(8,128)(2,1)}) %all-gather.52.cloned.1.call-update) | async-done | bytes 8388624 | tf_op jit(solution)/shard_map/all_gather | solution.py:133
  227.1 68.5 %all-gather.58.cloned.1.call-done = bf16[1,2048,2048]{2,1,0:T(8,128)(2,1)} async-done(((bf16[1,256,2048]{2,1,0:T(8,128)(2,1)}), bf16[1,2048,2048]{2,1,0:T(8,128)(2,1)}) %all-gather.58.cloned.1.call-update) | async-done | bytes 8388624 | tf_op jit(solution)/shard_map/all_gather | solution.py:134
  303.4 74.7 %all-gather.60.cloned.1.call-done = bf16[1,2048,2048]{2,1,0:T(8,128)(2,1)} async-done(((bf16[1,2048,256]{2,1,0:T(8,128)(2,1)}), bf16[1,2048,2048]{2,1,0:T(8,128)(2,1)}) %all-gather.60.cloned.1.call-update) | async-done | bytes 8388624 | tf_op jit(solution)/shard_map/all_gather | solution.py:135
  386.3 27.9 %reduce-scatter.14.cloned.1.call-done = f32[128,2048]{1,0:T(8,128)} async-done(((f32[256,2048]{1,0:T(8,128)}), f32[128,2048]{1,0:T(8,128)}) %reduce-scatter.14.cloned.1.call-update) | async-done | bytes 1048592 | tf_op jit(solution)/shard_map/reduce_scatter | solution.py:306
  418.7 80.8 %all-gather.62.cloned.1.call-done = bf16[1,2048,2048]{2,1,0:T(8,128)(2,1)} async-done(((bf16[1,256,2048]{2,1,0:T(8,128)(2,1)}), bf16[1,2048,2048]{2,1,0:T(8,128)(2,1)}) %all-gather.62.cloned.1.call-update) | async-done | bytes 8388624 | tf_op jit(solution)/shard_map/all_gather | solution.py:136
  499.5 20.6 all-gather.32.cloned.1.call-done
  527.5 77.7 %all-gather.64.cloned.1.call-done = bf16[1,2048,2048]{2,1,0:T(8,128)(2,1)} async-done(((bf16[1,256,2048]{2,1,0:T(8,128)(2,1)}), bf16[1,2048,2048]{2,1,0:T(8,128)(2,1)}) %all-gather.64.cloned.1.call-update) | async-done | bytes 8388624 | tf_op jit(solution)/shard_map/all_gather | solution.py:137
  613.8 74.2 %all-gather.66.cloned.1.call-done = bf16[1,2048,2048]{2,1,0:T(8,128)(2,1)} async-done(((bf16[1,2048,256]{2,1,0:T(8,128)(2,1)}), bf16[1,2048,2048]{2,1,0:T(8,128)(2,1)}) %all-gather.66.cloned.1.call-update) | async-done | bytes 8388624 | tf_op jit(solution)/shard_map/all_gather | solution.py:138
  695.4 28.7 %reduce-scatter.16.cloned.1.call-done = f32[128,2048]{1,0:T(8,128)} async-done(((f32[256,2048]{1,0:T(8,128)}), f32[128,2048]{1,0:T(8,128)}) %reduce-scatter.16.cloned.1.call-update) | async-done | bytes 1048592 | tf_op jit(solution)/shard_map/reduce_scatter | solution.py:316
  742.1 22.6 %all-gather.34.cloned.1.call-done = bf16[256,2048]{1,0:T(8,128)(2,1)} async-done(((bf16[128,2048]{1,0:T(8,128)(2,1)}), bf16[256,2048]{1,0:T(8,128)(2,1)}) %all-gather.34.cloned.1.call-update) | async-done | bytes 1048592 | tf_op jit(solution)/shard_map/all_gather | solution.py:273
  810.1 31.9 %reduce-scatter.18.cloned.1.call-done = f32[128,2048]{1,0:T(8,128)} async-done(((f32[256,2048]{1,0:T(8,128)}), f32[128,2048]{1,0:T(8,128)}) %reduce-scatter.18.cloned.1.call-update) | async-done | bytes 1048592 | tf_op jit(solution)/shard_map/reduce_scatter | solution.py:306
  848.0 19.3 all-gather.36.cloned.1.call-done
  890.2 12.0 fusion.147
  917.8 29.5 %reduce-scatter.26.cloned.1.call-done = f32[128,2048]{1,0:T(8,128)} async-done(((f32[256,2048]{1,0:T(8,128)}), f32[128,2048]{1,0:T(8,128)}) %reduce-scatter.26.cloned.1.call-update) | async-done | bytes 1048592 | tf_op jit(solution)/shard_map/reduce_scatter | solution.py:199
  959.9 13.9 all-gather.42.cloned.1.call-done
  1044.4 12.4 reduce-scatter.28.cloned.1.call-done
  1063.5 20.6 all-gather.38.cloned.1.call-done
  1133.8 31.1 %reduce-scatter.22.cloned.1.call-done = f32[128,2048]{1,0:T(8,128)} async-done(((f32[256,2048]{1,0:T(8,128)}), f32[128,2048]{1,0:T(8,128)}) %reduce-scatter.22.cloned.1.call-update) | async-done | bytes 1048592 | tf_op jit(solution)/shard_map/reduce_scatter | solution.py:306
  1176.6 13.7 collective-permute-done.2
  1217.5 10.6 broadcast_select_fusion.2
  1243.6 30.6 %reduce-scatter.30.cloned.1.call-done = f32[128,2048]{1,0:T(8,128)} async-done(((f32[256,2048]{1,0:T(8,128)}), f32[128,2048]{1,0:T(8,128)}) %reduce-scatter.30.cloned.1.call-update) | async-done | bytes 1048592 | tf_op jit(solution)/shard_map/reduce_scatter | solution.py:199
  1279.4 20.8 all-gather.46.cloned.1.call-done
  1351.4 31.7 %reduce-scatter.32.cloned.1.call-done = f32[128,2048]{1,0:T(8,128)} async-done(((f32[256,2048]{1,0:T(8,128)}), f32[128,2048]{1,0:T(8,128)}) %reduce-scatter.32.cloned.1.call-update) | async-done | bytes 1048592 | tf_op jit(solution)/shard_map/reduce_scatter | solution.py:244
  1390.2 13.6 collective-permute-done.3
  1404.7 21.2 all-gather.48.cloned.1.call-done
  1425.9 10.8 broadcast_select_fusion.1
  1457.0 24.4 %reduce-scatter.34.cloned.1.call-done = f32[128,2048]{1,0:T(8,128)} async-done(((f32[256,2048]{1,0:T(8,128)}), f32[128,2048]{1,0:T(8,128)}) %reduce-scatter.34.cloned.1.call-update) | async-done | bytes 1048592 | tf_op jit(solution)/shard_map/reduce_scatter | solution.py:199
  1620.8 57.9 %all-reduce = (f32[1,2048]{1,0:T(1,128)}, f32[1,2048]{1,0:T(1,128)}) all-reduce(f32[1,2048]{1,0:T(1,128)S(1)} %bitcast.466, f32[1,2048]{1,0:T(1,128)S(1)} %bitcast.465), channel_id=1, replica_groups=mesh['section'=2,'dp'=8,'tensor'=2] {'dp','tensor'}, use_global_device_ids=true, to_apply=%region_70.71 | all-reduce | flops 4096 | bytes 32768 | tf_op jit(solution)/shard_map/psum | solution.py:376
  1682.5 495.4 %reduce-scatter.38.cloned.1.call-done = bf16[256,14336]{0,1:T(8,128)(2,1)} async-done(((bf16[2048,14336]{0,1:T(8,128)(2,1)}), bf16[256,14336]{0,1:T(8,128)(2,1)}) %reduce-scatter.38.cloned.1.call-update) | async-done | bytes 7340048 | tf_op jit(solution)/shard_map/reduce_scatter | solution.py:372
  (772 shorter events, 636.1 us)
Async XLA Ops:
  11.9 71.9 %all-gather.56.cloned.1.call-start = ((), (), s32[]{:S(2)}) async-start(), calls=%async_computation.39 | async-start | bytes 4718592 | tf_op jit(solution)/shard_map/all_gather | solution.py:132
  12.7 118.6 %all-gather.54.cloned.1.call-start = ((), (), s32[]{:S(2)}) async-start(), calls=%async_computation.38 | async-start | bytes 4718592 | tf_op jit(solution)/shard_map/all_gather | solution.py:131
  13.4 200.2 %all-gather.52.cloned.1.call-start = ((), (), s32[]{:S(2)}) async-start(), calls=%async_computation.37 | async-start | bytes 9437184 | tf_op jit(solution)/shard_map/all_gather | solution.py:133
  14.0 281.7 %all-gather.58.cloned.1.call-start = ((), (), s32[]{:S(2)}) async-start(), calls=%async_computation.40 | async-start | bytes 9437184 | tf_op jit(solution)/shard_map/all_gather | solution.py:134
  14.6 363.6 %all-gather.60.cloned.1.call-start = ((), (), s32[]{:S(2)}) async-start(), calls=%async_computation.41 | async-start | bytes 9437184 | tf_op jit(solution)/shard_map/all_gather | solution.py:135
  15.1 399.2 %reduce-scatter.14.cloned.1.call-start = ((), (), s32[]{:S(2)}) async-start(), calls=%async_computation.14 | async-start | bytes 3145728 | tf_op jit(solution)/shard_map/reduce_scatter | solution.py:306
  385.5 114.0 %all-gather.62.cloned.1.call-start = ((), (), s32[]{:S(2)}) async-start(), calls=%async_computation.42 | async-start | bytes 9437184 | tf_op jit(solution)/shard_map/all_gather | solution.py:136
  386.3 133.8 %all-gather.32.cloned.1.call-start = ((), (), s32[]{:S(2)}) async-start(), calls=%async_computation.15 | async-start | bytes 1572864 | tf_op jit(solution)/shard_map/all_gather | solution.py:309
  417.0 188.2 %all-gather.64.cloned.1.call-start = ((), (), s32[]{:S(2)}) async-start(), calls=%async_computation.43 | async-start | bytes 9437184 | tf_op jit(solution)/shard_map/all_gather | solution.py:137
  417.6 270.3 %all-gather.66.cloned.1.call-start = ((), (), s32[]{:S(2)}) async-start(), calls=%async_computation.44 | async-start | bytes 9437184 | tf_op jit(solution)/shard_map/all_gather | solution.py:138
  418.4 305.7 %reduce-scatter.16.cloned.1.call-start = ((), (), s32[]{:S(2)}) async-start(), calls=%async_computation.16 | async-start | bytes 3145728 | tf_op jit(solution)/shard_map/reduce_scatter | solution.py:316
  695.3 69.4 %all-gather.34.cloned.1.call-start = ((), (), s32[]{:S(2)}) async-start(), calls=%async_computation.17 | async-start | bytes 1572864 | tf_op jit(solution)/shard_map/all_gather | solution.py:273
  741.5 100.5 %reduce-scatter.18.cloned.1.call-start = ((), (), s32[]{:S(2)}) async-start(), calls=%async_computation.18 | async-start | bytes 3145728 | tf_op jit(solution)/shard_map/reduce_scatter | solution.py:306
  810.0 57.3 %all-gather.36.cloned.1.call-start = ((), (), s32[]{:S(2)}) async-start(), calls=%async_computation.19 | async-start | bytes 1572864 | tf_op jit(solution)/shard_map/all_gather | solution.py:309
  845.9 44.3 %all-gather.68.cloned.1.call-start = ((), (), s32[]{:S(2)}) async-start(), calls=%async_computation.45 | async-start | bytes 1572864 | tf_op jit(solution)/shard_map/all_gather | solution.py:188
  847.8 99.5 %reduce-scatter.26.cloned.1.call-start = ((), (), s32[]{:S(2)}) async-start(), calls=%async_computation.25 | async-start | bytes 3145728 | tf_op jit(solution)/shard_map/reduce_scatter | solution.py:199
  916.2 57.6 %all-gather.42.cloned.1.call-start = ((), (), s32[]{:S(2)}) async-start(), calls=%async_computation.26 | async-start | bytes 1572864 | tf_op jit(solution)/shard_map/all_gather | solution.py:203
  952.4 72.6 %reduce-scatter.20.cloned.1.call-start = ((), (), s32[]{:S(2)}) async-start(), calls=%async_computation.20 | async-start | bytes 3145728 | tf_op jit(solution)/shard_map/reduce_scatter | solution.py:316
  959.9 97.0 %reduce-scatter.28.cloned.1.call-start = ((), (), s32[]{:S(2)}) async-start(), calls=%async_computation.27 | async-start | bytes 3145728 | tf_op jit(solution)/shard_map/reduce_scatter | solution.py:244
  1024.9 59.1 %all-gather.38.cloned.1.call-start = ((), (), s32[]{:S(2)}) async-start(), calls=%async_computation.21 | async-start | bytes 1572864 | tf_op jit(solution)/shard_map/all_gather | solution.py:273
  1062.5 102.3 %reduce-scatter.22.cloned.1.call-start = ((), (), s32[]{:S(2)}) async-start(), calls=%async_computation.22 | async-start | bytes 3145728 | tf_op jit(solution)/shard_map/reduce_scatter | solution.py:306
  1132.6 62.0 %all-gather.40.cloned.1.call-start = ((), (), s32[]{:S(2)}) async-start(), calls=%async_computation.23 | async-start | bytes 1572864 | tf_op jit(solution)/shard_map/all_gather | solution.py:309
  1173.2 44.3 %all-gather.44.cloned.1.call-start = ((), (), s32[]{:S(2)}) async-start(), calls=%async_computation.28 | async-start | bytes 1572864 | tf_op jit(solution)/shard_map/all_gather | solution.py:188
  1191.2 83.0 %reduce-scatter.30.cloned.1.call-start = ((), (), s32[]{:S(2)}) async-start(), calls=%async_computation.29 | async-start | bytes 3145728 | tf_op jit(solution)/shard_map/reduce_scatter | solution.py:199
  1242.1 58.1 %all-gather.46.cloned.1.call-start = ((), (), s32[]{:S(2)}) async-start(), calls=%async_computation.30 | async-start | bytes 1572864 | tf_op jit(solution)/shard_map/all_gather | solution.py:203
  1278.7 104.4 %reduce-scatter.32.cloned.1.call-start = ((), (), s32[]{:S(2)}) async-start(), calls=%async_computation.31 | async-start | bytes 3145728 | tf_op jit(solution)/shard_map/reduce_scatter | solution.py:244
  1350.9 75.1 %all-gather.48.cloned.1.call-start = ((), (), s32[]{:S(2)}) async-start(), calls=%async_computation.32 | async-start | bytes 1572864 | tf_op jit(solution)/shard_map/all_gather | solution.py:188
  1404.7 76.7 %reduce-scatter.34.cloned.1.call-start = ((), (), s32[]{:S(2)}) async-start(), calls=%async_computation.33 | async-start | bytes 3145728 | tf_op jit(solution)/shard_map/reduce_scatter | solution.py:199
  1449.7 57.5 %all-gather.50.cloned.1.call-start = ((), (), s32[]{:S(2)}) async-start(), calls=%async_computation.34 | async-start | bytes 1572864 | tf_op jit(solution)/shard_map/all_gather | solution.py:203
  1485.7 130.2 %reduce-scatter.24.cloned.1.call-start = ((), (), s32[]{:S(2)}) async-start(), calls=%async_computation.24 | async-start | bytes 3145728 | tf_op jit(solution)/shard_map/reduce_scatter | solution.py:316
  1497.4 121.7 %reduce-scatter.36.cloned.1.call-start = ((), (), s32[]{:S(2)}) async-start(), calls=%async_computation.35 | async-start | bytes 3145728 | tf_op jit(solution)/shard_map/reduce_scatter | solution.py:244
  1561.3 616.6 %reduce-scatter.38.cloned.1.call-start = ((), (), s32[]{:S(2)}) async-start(), calls=%async_computation.36 | async-start | bytes 66060288 | tf_op jit(solution)/shard_map/reduce_scatter | solution.py:372
  (230 other events, 5749.1 us)
Sparse Core Ops, SparseCore 0:
  12.0 21.5 all-gather.29
  35.2 48.5 all-gather.55
  85.4 45.8 all-gather.53
  132.7 80.8 all-gather.51
  215.0 80.5 all-gather.57
  297.1 80.9 all-gather.59
  385.6 28.5 reduce-scatter.13
  416.0 83.4 all-gather.61
  521.7 83.5 all-gather.63
  606.9 80.9 all-gather.65
  695.4 28.5 reduce-scatter.15
  741.6 23.0 all-gather.33
  810.2 31.8 reduce-scatter.17
  846.0 21.2 all-gather.35
  868.8 21.2 all-gather.67
  916.4 30.9 reduce-scatter.25
  952.5 21.2 all-gather.41
  976.1 31.8 reduce-scatter.19
  1025.1 31.7 reduce-scatter.27
  1062.7 21.3 all-gather.37
  1132.8 32.0 reduce-scatter.21
  1173.3 21.2 all-gather.39
  1196.1 21.2 all-gather.43
  1242.2 31.8 reduce-scatter.29
  1278.9 21.3 all-gather.45
  1351.0 32.1 reduce-scatter.31
  1404.8 21.0 all-gather.47
  1449.8 31.5 reduce-scatter.33
  1485.8 21.2 all-gather.49
  1510.0 31.8 reduce-scatter.23
  1561.4 32.9 reduce-scatter.35
  1615.3 562.5 reduce-scatter.37
  (1 shorter events, 18.3 us)
where the time goes:
time: 2230 us; the launch traced here: 2220 us
  waiting for transfers between devices  1520 us (68%)
  matrix products  383 us (17%)
  other arithmetic  134 us (6%)
  local copies, waits for them, and re-layouts  90.1 us (4%)
  blocking collectives  57.9 us (3%)
    reduce_scatter x1, waiting for transfers between devices, on_device(): lax.psum_scatter(pack_terms(weight_terms(joined)).astype(jnp.bfloat16), '...  495 us
    reduce_scatter x3, waiting for transfers between devices, on_device(): lax.psum_scatter(branch, 'tensor', scatter_dimension=0, tiled=True)  91 us
    reduce_scatter x3, waiting for transfers between devices, backward(): lax.psum_scatter(grad_mid_norm, 'tensor', scatter_dimension=0, tiled=True)  84.5 us
    all_gather x1, waiting for transfers between devices, on_device(): lax.all_gather(gate_weight[0], 'dp', axis=0, tiled=True)  80.8 us
    all_gather x1, waiting for transfers between devices, on_device(): lax.all_gather(up_weight[0], 'dp', axis=0, tiled=True)  77.7 us
    all_gather x1, waiting for transfers between devices, on_device(): lax.all_gather(value_weight[0], 'dp', axis=0, tiled=True)  77.3 us
    all_gather x1, waiting for transfers between devices, on_device(): lax.all_gather(output_weight[0], 'dp', axis=1, tiled=True)  74.7 us
    all_gather x1, waiting for transfers between devices, on_device(): lax.all_gather(down_weight[0], 'dp', axis=1, tiled=True)  74.2 us
  transfers between devices with their start and end apart: 37, of which 34 were waited for; matrix products, arithmetic and copies ran while one was open for 13% of the time, Pallas kernels for 0%

commit v1 on v0

v1 whole, which is shorter than its diff:
```python
import functools

import jax
import jax.numpy as jnp
from jax import lax
from jax.experimental import pallas as pl
from jax.experimental.pallas import tpu as pltpu
from jax.sharding import PartitionSpec as P

HEAD_K = 256
HEAD_V = 512
MESH = pl.DeviceIdType.MESH

epsilon = 1e-05
group_guard = 1.0
bf16 = jnp.bfloat16
f32 = jnp.float32


def rotation_tables(length, half_width):
    pair_index = jnp.arange(half_width).astype(f32)
    position = jnp.arange(length).astype(f32)[:, None]
    angle = position * jnp.exp(-jnp.log(10000.0) * pair_index / half_width)
    zeta = (pair_index / half_width + 0.4) / 1.4
    growth = jnp.exp(position / 512.0 * jnp.log(zeta))
    return (jnp.cos(angle), jnp.sin(angle), growth)


def decay_mask(segments, first_head, heads):
    length = segments.shape[-1]
    position = jnp.arange(length)
    earlier = position[:, None] >= position[None, :]
    same_doc = (segments[:, :, None] == segments[:, None, :]) & earlier[None]
    distance = jnp.maximum(position[:, None] - position[None, :], 0).astype(f32)
    head_index = (first_head + jnp.arange(heads)).astype(f32)
    log_rate = jnp.log(1.0 - jnp.exp2(-5.0 - head_index))
    decay = jnp.exp(log_rate[:, None, None] * distance[None])
    return jnp.where(same_doc[:, None], decay[None], 0.0)


class Place:
    def __init__(self, dp_size):
        self.groups = dp_size // 4
        self.section = lax.axis_index("section")
        self.dp = lax.axis_index("dp")
        self.tensor = lax.axis_index("tensor")
        self.core = self.dp % 2
        self.low = (self.dp // 2) % 2
        self.group = self.dp // 4

    def dp_at(self, group_step, low_step):
        group = (self.group + group_step + self.groups) % self.groups
        return (group * 2 + (self.low + low_step) % 2) * 2 + self.core

    def sibling(self):
        return self.dp + 1 - 2 * self.core


SQUARE = ((0, 1), (1, 0), (1, 1))
TILE = 512
VMEM_LIMIT = 63 * 1024 * 1024


def mm(left, right):
    return lax.dot_general(left, right, (((1,), (0,)), ((), ())), preferred_element_type=f32)


def mm_nt(left, right):
    return lax.dot_general(left, right, (((1,), (1,)), ((), ())), preferred_element_type=f32)


def mm_tn(left, right):
    return lax.dot_general(left, right, (((0,), (0,)), ((), ())), preferred_element_type=f32)


class Square:
    def __init__(self, dp_size, rows):
        self.at = Place(dp_size)
        self.rows = rows
        self.own = self.at.low
        self.next = 1 - self.at.low

    def device(self, low_step, tensor_step):
        return (self.at.section, self.at.dp_at(0, low_step), (self.at.tensor + tensor_step) % 2)

    def barrier(self):
        barrier = pltpu.get_barrier_semaphore()
        for step in SQUARE:
            pl.semaphore_signal(barrier, inc=1, device_id=self.device(*step), device_id_type=MESH)
        pl.semaphore_wait(barrier, len(SQUARE))

    def chunk(self, ref, low_step=0, tensor_step=0):
        start = pl.multiple_of((self.at.tensor + tensor_step) % 2 * self.rows, self.rows)
        return ref.at[(self.at.low + low_step) % 2, pl.ds(start, self.rows)]

    def copy(self, src, dst, send, recv, step):
        return pltpu.make_async_remote_copy(
            src_ref=src,
            dst_ref=dst,
            send_sem=send,
            recv_sem=recv,
            device_id=self.device(*step),
            device_id_type=MESH,
        )

    def spread(self, ref, send, recv):
        pushes = []
        for j, step in enumerate(SQUARE):
            push = self.copy(self.chunk(ref), self.chunk(ref), send.at[j], recv.at[j], step)
            push.start()
            pushes.append(push)
        return pushes

    def spread_from(self, own, ref, send, recv, here):
        local = pltpu.make_async_copy(own, self.chunk(ref), here)
        local.start()
        pushes = [local]
        for j, step in enumerate(SQUARE):
            push = self.copy(own, self.chunk(ref), send.at[j], recv.at[j], step)
            push.start()
            pushes.append(push)
        return pushes

    def give(self, parts, landed, send, recv, j):
        push = self.copy(self.chunk(parts, *SQUARE[j]), landed.at[j], send.at[j], recv.at[j], SQUARE[j])
        push.start()
        return push


def row_blocks(rows, body, block=32):
    block = min(block, rows)

    @pl.loop(0, rows // block)
    def _(i):
        body(pl.ds(pl.multiple_of(i * block, block), block))


def norm_parts(values):
    centred = values - jnp.mean(values, axis=-1, keepdims=True)
    scale = lax.rsqrt(jnp.mean(centred * centred, axis=-1, keepdims=True) + epsilon)
    return centred * scale, scale


def norm_grad(normed, scale, upstream, gain):
    through = upstream * gain
    return scale * (
        through
        - jnp.mean(through, axis=-1, keepdims=True)
        - normed * jnp.mean(through * normed, axis=-1, keepdims=True)
    )


def turn(values, cosine, sine, scale):
    half = values.shape[-1] // 2
    a, b = values[:, :half], values[:, half:]
    return jnp.concatenate([(a * cosine - b * sine) * scale, (a * sine + b * cosine) * scale], axis=-1)


def turn_back(values, cosine, sine, scale):
    half = values.shape[-1] // 2
    a, b = values[:, :half] * scale, values[:, half:] * scale
    return jnp.concatenate([a * cosine + b * sine, b * cosine - a * sine], axis=-1)


def transpose_into(target, source):
    _, length, width = source.shape
    for s in range(2):
        for start in range(0, width, TILE):
            target[start : start + TILE, s * length : (s + 1) * length] = source[s, :, start : start + TILE].T


def forward_kernel(dp_size, layer, *refs):
    streams = layer == 0
    v = Refs()
    if streams:
        (v.x, v.own_gains, v.tables, v.masks, v.out_grad, *refs) = refs
        shards, refs = refs[:8], refs[8:]
        stored, refs = refs[:4], refs[4:]
        (v.gains, *refs) = refs
    else:
        (v.x, v.gains, v.tables, v.masks, *refs) = refs
        stored, refs = refs[:4], refs[4:]
    (middle, normed_in_t, query_rot, key_rot, value, unit, inverse, opened, slope_open, merged, normed_mid_t, act, slope,
     hidden, *refs) = refs
    if streams:
        (v.grad_down, result, *refs) = refs
    held, refs = refs[:4], refs[4:]
    (w_sem, normed_in, normed_mid, parts, landed, s_send, s_recv, g_send, g_recv, *refs) = refs
    x, tables, masks = v.x, v.tables, v.masks
    rows, width = x.shape
    sq = Square(dp_size, rows)
    at = sq.at
    qkvs, out_t, gate_up, down_t = held
    wide_k = query_rot.shape[-1]
    wide_v = value.shape[-1]
    wide_f = hidden.shape[-1]
    heads = wide_k // HEAD_K
    slices = dp_size // 2
    other = 1 - at.section
    groups = [(0, 0, wide_k), (0, wide_k, wide_k), (0, 2 * wide_k, wide_v), (0, 2 * wide_k + wide_v, wide_v),
              (1, 0, wide_v), (2, 0, wide_f), (2, wide_f, wide_f), (3, 0, wide_f)]
    loads = {}

    def load(i):
        which, first, size = groups[i]
        columns = pl.ds(first, size)
        loads[i] = pltpu.make_async_copy(
            stored[which].at[layer, :, :, :, columns], held[which].at[:, :, :, columns], w_sem.at[i]
        )
        loads[i].start()

    def weight(which, first, size):
        return held[which][:, :, :, first : first + size].reshape(width, size)

    def first_norm(block):
        unit_rows, _ = norm_parts(x[block].astype(f32))
        sq.chunk(normed_in)[block] = (unit_rows * v.gains[layer, 0:1]).astype(bf16)

    def project(i, s):
        loads_wait(i)
        first, size = groups[i][1:]
        tokens = normed_in[s]
        for start in range(0, size, TILE):
            wide = mm(tokens, weight(0, first + start, TILE))
            cols = slice(start, start + TILE)
            if i < 2:
                dest = (query_rot, key_rot)[i]
                for head in range(TILE // HEAD_K):
                    part = wide[:, head * HEAD_K : (head + 1) * HEAD_K]
                    dest[s, :, start + head * HEAD_K : start + (head + 1) * HEAD_K] = turn(
                        part, tables[0], tables[1], tables[2 + i]
                    ).astype(bf16)
            elif i == 2:
                value[s, :, cols] = wide.astype(bf16)
            else:
                sigmoid = 1.0 / (1.0 + jnp.exp(-wide))
                opened[s, :, cols] = (wide * sigmoid).astype(bf16)
                slope_open[s, :, cols] = (sigmoid * (1.0 + wide * (1.0 - sigmoid))).astype(bf16)

    waited = []

    def loads_wait(i):
        if i not in waited:
            waited.append(i)
            loads[i].wait()

    def retain(s):
        for head in range(heads):
            cols_k = slice(head * HEAD_K, (head + 1) * HEAD_K)
            cols_v = slice(head * HEAD_V, (head + 1) * HEAD_V)
            product = mm_nt(query_rot[s, :, cols_k], key_rot[s, :, cols_k])
            weights = (product * masks[s, head]).astype(bf16)
            mixed = mm(weights, value[s, :, cols_v])
            centred = mixed - jnp.mean(mixed, axis=-1, keepdims=True)
            scale = lax.rsqrt(jnp.mean(centred * centred, axis=-1, keepdims=True) + group_guard)
            unit_rows = centred * scale
            inverse[s, head] = scale
            unit[s, :, cols_v] = unit_rows.astype(bf16)
            merged[s, :, cols_v] = (unit_rows * opened[s, :, cols_v].astype(f32)).astype(bf16)

    def give_back(s, source, weight_t):
        tokens = source[s]
        step = width // slices
        for i in range(slices):
            parts[s, :, i * step : (i + 1) * step] = mm_nt(tokens, weight_t[i].reshape(step, -1)).astype(bf16)

    def collected(block, which):
        total = sq.chunk(parts)[block].astype(f32)
        for j in range(len(SQUARE)):
            total = total + landed[which, j, block].astype(f32)
        return total

    def give(s, which):
        send, recv = g_send.at[which], g_recv.at[which]
        return [sq.give(parts, landed.at[which], send, recv, j) for j in ((1, 2) if s == 1 else (0,))]

    def second_norm(block):
        middle_rows = x[block].astype(f32) + collected(block, 0)
        middle[block] = middle_rows
        unit_rows, _ = norm_parts(middle_rows)
        sq.chunk(normed_mid)[block] = (unit_rows * v.gains[layer, 1:2]).astype(bf16)

    def feed(s):
        loads_wait(5)
        loads_wait(6)
        tokens = normed_mid[s]
        for start in range(0, wide_f, TILE):
            cols = slice(start, start + TILE)
            gate = mm(tokens, weight(2, start, TILE))
            up = mm(tokens, weight(2, wide_f + start, TILE))
            square = gate * gate
            bend = jnp.tanh(0.7978845608028654 * gate * (1.0 + 0.044715 * square))
            half = 0.5 * (1.0 + bend)
            gelu = gate * half
            slope_gelu = half + 0.5 * gate * (1.0 - bend * bend) * (
                0.7978845608028654 * (1.0 + 3 * 0.044715 * square)
            )
            act[s, :, cols] = gelu.astype(bf16)
            slope[s, :, cols] = (slope_gelu * up).astype(bf16)
            hidden[s, :, cols] = (gelu * up).astype(bf16)

    if not streams:
        for i in range(7):
            load(i)
        row_blocks(rows, first_norm)
        sq.barrier()
        ins = sq.spread(normed_in, s_send.at[0], s_recv.at[0])
        ins[0].wait_recv()
        for i in range(4):
            project(i, sq.own)
        ins[1].wait_recv()
        ins[2].wait_recv()
        for i in range(4):
            project(i, sq.next)
        retain(sq.next)
        loads_wait(4)
        give_back(sq.next, merged, out_t)
        gives = give(1, 0)
        retain(sq.own)
        give_back(sq.own, merged, out_t)
        gives += give(0, 0)
        transpose_into(normed_in_t, normed_in)
        for push in gives:
            push.wait_recv()
        row_blocks(rows, second_norm)
        mids = sq.spread(normed_mid, s_send.at[1], s_recv.at[1])
        mids[0].wait_recv()
        feed(sq.own)
        mids[1].wait_recv()
        mids[2].wait_recv()
        feed(sq.next)
        transpose_into(normed_mid_t, normed_mid)
        for push in ins + mids + gives:
            push.wait_send()
        return

    (z_send, z_recv, x_send, x_recv, c_send, c_recv, o_send, o_recv, here_sem, gain_send, gain_recv, d_send, d_recv,
     d_sem) = refs
    steps = [(k, b) for k in range(at.groups) for b in range(2)][1:]

    def place(section=None, dp=None):
        return (at.section if section is None else section, at.dp if dp is None else dp, at.tensor)

    def copy(src, dst, send, recv, device):
        return pltpu.make_async_remote_copy(
            src_ref=src, dst_ref=dst, send_sem=send, recv_sem=recv, device_id=device, device_id_type=MESH
        )

    partners = [sq.device(*step) for step in SQUARE] + [place(dp=at.sibling()), place(section=other)]
    partners += [place(dp=at.dp_at(k, b)) for k, b in steps if (k, b) != (0, 1)]
    barrier = pltpu.get_barrier_semaphore()
    for partner in partners:
        pl.semaphore_signal(barrier, inc=1, device_id=partner, device_id_type=MESH)
    pl.semaphore_wait(barrier, len(partners))

    gain_copy = copy(v.own_gains, v.gains.at[at.section], gain_send, gain_recv, place(section=other))
    gain_copy.start()
    v.gains[at.section] = v.own_gains[...]

    def slot(i, section, dp):
        which, first, size = groups[i]
        return stored[which].at[section, dp // 2, dp % 2, :, pl.ds(first, size)]

    def block(i, section, core):
        which, first, size = groups[i]
        return stored[which].at[section, :, core, :, pl.ds(first, size)]

    def part(i, b):
        size = groups[i][2]
        return shards[i].at[:, pl.ds(pl.multiple_of((at.low + b) % 2 * size, size), size)]

    z_copies, x_copies, here, core_own, core_other = {}, {}, {}, {}, {}

    def push_own(i):
        mine = slot(i, at.section, at.dp)
        for j, (k, b) in enumerate(steps):
            z_copies[i, j] = copy(part(i, b), mine, z_send.at[i, j], z_recv.at[i, j], place(dp=at.dp_at(k, b)))
            z_copies[i, j].start()
        x_copies[i, 0] = copy(part(i, 0), mine, x_send.at[i, 0], x_recv.at[i, 0], place(section=other))
        x_copies[i, 0].start()
        here[i] = pltpu.make_async_copy(part(i, 0), mine, here_sem.at[i])
        here[i].start()

    def pass_on(i):
        for j, (k, b) in enumerate(steps):
            z_copies[i, j].wait_recv()
            arrived = slot(i, at.section, at.dp_at(-k, b))
            x_copies[i, j + 1] = copy(arrived, arrived, x_send.at[i, j + 1], x_recv.at[i, j + 1], place(section=other))
            x_copies[i, j + 1].start()
        here[i].wait()
        mine = block(i, at.section, at.core)
        core_own[i] = copy(mine, mine, c_send.at[i], c_recv.at[i], place(dp=at.sibling()))
        core_own[i].start()

    def share_other(i):
        for j in range(slices):
            x_copies[i, j].wait_recv()
        theirs = block(i, other, at.core)
        core_other[i] = copy(theirs, theirs, o_send.at[i], o_recv.at[i], place(dp=at.sibling()))
        core_other[i].start()

    def arrive(i):
        @pl.when(at.section == 0)
        def _():
            core_own[i].wait_recv()

        @pl.when(at.section == 1)
        def _():
            core_other[i].wait_recv()

        load(i)

    ahead = 3
    for i in range(ahead):
        push_own(i)
    gain_copy.wait_recv()
    row_blocks(rows, first_norm)
    ins = sq.spread(normed_in, s_send.at[0], s_recv.at[0])

    def advance(i):
        pass_on(i)
        if i + ahead < 8:
            push_own(i + ahead)
        if i > 0:
            share_other(i - 1)
            arrive(i - 1)

    advance(0)
    downs = sq.spread_from(v.out_grad, v.grad_down, d_send, d_recv, d_sem)
    advance(1)
    for push in ins:
        push.wait_recv()
    transpose_into(normed_in_t, normed_in)
    for i in range(2, 5):
        advance(i)
        for s in (sq.own, sq.next):
            project(i - 2, s)
    advance(5)
    for s in (sq.own, sq.next):
        project(3, s)
    retain(sq.next)
    loads_wait(4)
    give_back(sq.next, merged, out_t)
    gives = give(1, 0)
    retain(sq.own)
    give_back(sq.own, merged, out_t)
    gives += give(0, 0)
    advance(6)
    for push in gives:
        push.wait_recv()
    row_blocks(rows, second_norm)
    mids = sq.spread(normed_mid, s_send.at[1], s_recv.at[1])
    advance(7)
    for push in mids:
        push.wait_recv()
    transpose_into(normed_mid_t, normed_mid)
    feed(sq.next)
    feed(sq.own)
    for push in gives:
        push.wait_send()

    def last_group():
        for j in range(slices):
            x_copies[7, j].wait_recv()
        core_other[7].start()

    theirs = block(7, other, at.core)
    core_other[7] = copy(theirs, theirs, o_send.at[7], o_recv.at[7], place(dp=at.sibling()))

    @pl.when(at.section == 1)
    def _():
        last_group()

    arrive(7)
    loads_wait(7)
    give_back(sq.next, hidden, down_t)
    ends = give(1, 1)
    give_back(sq.own, hidden, down_t)
    ends += give(0, 1)

    @pl.when(at.section == 0)
    def _():
        last_group()

    for push in ends:
        push.wait_recv()

    def last(block):
        result[block] = (middle[block] + collected(block, 1)).astype(bf16)

    row_blocks(rows, last)

    @pl.when(at.section == 0)
    def _():
        for i in range(8):
            core_other[i].wait_recv()

    @pl.when(at.section == 1)
    def _():
        for i in range(8):
            core_own[i].wait_recv()

    for push in downs:
        push.wait()
    for push in ins + mids + ends + list(z_copies.values()) + list(x_copies.values()):
        push.wait_send()
    for i in range(8):
        core_own[i].wait_send()
        core_other[i].wait_send()
    gain_copy.wait_send()


def forward_layer(layer, x, gains, tables, masks, weights, dp_size, out_grad=None):
    rows, width = x.shape
    length = masks.shape[-1]
    heads = masks.shape[1]
    streams = layer == 0
    slices = dp_size // 2
    quarter_k = heads * HEAD_K
    quarter_v = heads * HEAD_V
    quarter_f = weights[-1].shape[-1] // 2 if streams else weights[-1].shape[-1]
    vmem = pl.BlockSpec(memory_space=pltpu.VMEM)
    any_spec = pl.BlockSpec(memory_space=pl.ANY)
    wides = (2 * quarter_k + 2 * quarter_v, quarter_v, 2 * quarter_f, quarter_f)

    def tokens(wide, kind=bf16):
        return jax.ShapeDtypeStruct((2, length, wide), kind)

    turned = jax.ShapeDtypeStruct((width, 2 * length), bf16)
    dma = pltpu.SemaphoreType.DMA
    out_shape = [
        jax.ShapeDtypeStruct((rows, width), f32),
        turned,
        tokens(quarter_k),
        tokens(quarter_k),
        tokens(quarter_v),
        tokens(quarter_v),
        jax.ShapeDtypeStruct((2, heads, length, 1), f32),
        tokens(quarter_v),
        tokens(quarter_v),
        tokens(quarter_v),
        turned,
        tokens(quarter_f),
        tokens(quarter_f),
        tokens(quarter_f),
    ]
    out_specs = [vmem] * len(out_shape)
    scratch = [pltpu.VMEM((slices, 2, width // dp_size, wide), bf16) for wide in wides] + [
        dma((8,)),
        pltpu.VMEM((2, length, width), bf16),
        pltpu.VMEM((2, length, width), bf16),
        pltpu.VMEM((2, length, width), bf16),
        pltpu.VMEM((2, 3, rows, width), bf16),
        dma((2, 3)),
        dma((2, 3)),
        dma((2, 3)),
        dma((2, 3)),
    ]
    if streams:
        out_shape = (
            [jax.ShapeDtypeStruct((2, slices, 2, width // dp_size, wide), bf16) for wide in wides]
            + [jax.ShapeDtypeStruct((2,) + gains.shape, f32)]
            + out_shape
            + [tokens(width), jax.ShapeDtypeStruct((rows, width), bf16)]
        )
        out_specs = [any_spec] * 4 + [vmem] + out_specs + [any_spec, vmem]
        scratch += [
            dma((8, slices - 1)),
            dma((8, slices - 1)),
            dma((8, slices)),
            dma((8, slices)),
            dma((8,)),
            dma((8,)),
            dma((8,)),
            dma((8,)),
            dma((8,)),
            dma,
            dma,
            dma((3,)),
            dma((3,)),
            dma,
        ]
    operands = [x, gains, tables, masks] + ([out_grad] if streams else [])
    return pl.pallas_call(
        functools.partial(forward_kernel, dp_size, layer),
        out_shape=out_shape,
        in_specs=[vmem] * len(operands) + [any_spec] * len(weights),
        out_specs=out_specs,
        scratch_shapes=scratch,
        compiler_params=pltpu.CompilerParams(
            collective_id=1 + layer, has_side_effects=True, vmem_limit_bytes=VMEM_LIMIT
        ),
        name="forward_layer",
    )(*operands, *weights)


class Refs:
    pass


GROUPS = 7


def backward_kernel(dp_size, layer, *refs):
    final_layer = layer == 0
    v = Refs()
    (v.grad_out, v.gains, v.tables, v.masks, v.x, v.middle, v.normed_in_t, v.query_rot, v.key_rot, v.value, v.unit,
     v.inverse, v.opened, v.slope_open, v.merged, v.normed_mid_t, v.act, v.slope, v.hidden,
     v.qkvs_all, v.out_all, v.gate_up_all, v.down_all, v.down_in, *refs) = refs
    if final_layer:
        v.later_chip, v.later_terms, v.first_rows, v.second_rows, *refs = refs
    v.grad_in, v.chip, v.core_land, *refs = refs
    if final_layer:
        v.x_land, v.final, v.gain_sums, v.taken_rows, v.taken_grads, *refs = refs
    else:
        v.terms, v.result, v.next_down, *refs = refs
    (v.big, v.out_t, v.query_v, v.key_v, v.value_v, v.wide_a, v.wide_b, v.wide_c, v.inverse_v, v.x_v, v.middle_v,
     v.normed_t, v.outer, v.grad_down, v.grad_gate_up, v.grad_branch, v.grad_qkvs, v.turned, v.parts, v.landed,
     v.grad_middle, v.stage_given, v.stage_own, v.core_part, v.load_sem, v.s_send, v.s_recv, v.g_send, v.g_recv,
     v.c_send, v.c_recv, v.local_sem, *refs) = refs
    if final_layer:
        (v.left, v.right, v.sums, v.r_sem, v.x_send, v.x_recv, v.z_send, v.z_recv, v.terms, v.held, v.hop_land,
         v.t_send, v.t_recv, v.row_send, v.row_recv) = refs
    else:
        v.parts_y, v.landed_y, v.d_send, v.d_recv, v.d_sem = refs
    at = Place(dp_size)
    rows, width = v.x.shape
    sq = Square(dp_size, rows)
    masks, tables, gains = v.masks, v.tables, v.gains
    query_v, key_v, value_v = v.query_v, v.key_v, v.value_v
    wide_a, wide_b, wide_c = v.wide_a, v.wide_b, v.wide_c
    grad_down, grad_gate_up, grad_branch, grad_qkvs = v.grad_down, v.grad_gate_up, v.grad_branch, v.grad_qkvs
    big, out_t, outer, parts, landed, terms = v.big, v.out_t, v.outer, v.parts, v.landed, v.terms
    wide_k = query_v.shape[-1]
    wide_v = value_v.shape[-1]
    wide_f = outer.shape[-1]
    heads = wide_k // HEAD_K
    slices = dp_size // 2
    slice_rows = width // dp_size
    gain_in = gains[layer, 0:1]
    gain_mid = gains[layer, 1:2]
    other = 1 - at.section
    steps = [(k, b) for k in range(at.groups) for b in range(2)]
    steps = steps[1:] + steps[:1]

    def load(index, source, target):
        copy = pltpu.make_async_copy(source, target, v.load_sem.at[index])
        copy.start()
        return copy

    def remote(src, dst, send, recv, device):
        return pltpu.make_async_remote_copy(
            src_ref=src, dst_ref=dst, send_sem=send, recv_sem=recv, device_id=device, device_id_type=MESH
        )

    def place(section=None, dp=None, tensor=None):
        return (
            at.section if section is None else section,
            at.dp if dp is None else dp,
            at.tensor if tensor is None else tensor,
        )

    sibling = place(dp=at.sibling())
    across = place(section=other)

    token_load = load(14, v.down_in, grad_down)
    down_load = load(0, v.down_all.at[layer], big.at[:, pl.ds(2 * wide_f, wide_f)])
    act_load = load(1, v.act, wide_a)
    slope_load = load(2, v.slope, wide_b)
    gate_load = load(3, v.gate_up_all.at[layer], big.at[:, pl.ds(0, 2 * wide_f)])
    hidden_load = load(4, v.hidden, outer)
    mid_load = load(5, v.normed_mid_t, v.normed_t)
    early = [
        load(6, v.middle, v.middle_v),
        load(7, v.x, v.x_v),
        load(8, v.out_all.at[layer], out_t),
        load(9, v.query_rot, query_v),
        load(10, v.key_rot, key_v),
        load(11, v.value, value_v),
        load(12, v.inverse, v.inverse_v),
        load(13, v.opened, wide_c),
    ]
    terms[...] = jnp.zeros_like(terms)

    partners = [sq.device(*step) for step in SQUARE] + [sibling]
    if final_layer:
        partners.append(across)
        partners += [place(dp=at.dp_at(k, b)) for k, b in steps[:-1] if (k, b) != (0, 1)]
    barrier = pltpu.get_barrier_semaphore()
    for partner in partners:
        pl.semaphore_signal(barrier, inc=1, device_id=partner, device_id_type=MESH)
    pl.semaphore_wait(barrier, len(partners))

    def x_copy(e, j, source):
        block = source.at[e, j]
        return remote(block, v.x_land.at[e, j], v.x_send.at[e, j], v.x_recv.at[e, j], across)

    def start_x(e, source):
        @pl.loop(0, slices)
        def _(j):
            x_copy(e, j, source).start()

    row_copies = []
    if final_layer:

        @pl.when(at.section == 0)
        def _():
            remote(v.second_rows, v.taken_rows, v.row_send.at[0], v.row_recv.at[0], across).start()

            @pl.loop(0, GROUPS)
            def _(e):
                start_x(e, v.later_chip)

            remote(v.grad_out, v.taken_grads, v.row_send.at[1], v.row_recv.at[1], across).start()

        @pl.when(at.section == 1)
        def _():
            remote(v.first_rows, v.taken_rows, v.row_send.at[0], v.row_recv.at[0], across).start()

    def through_down(s):
        tokens = grad_down[s]
        for start in range(0, wide_f, TILE):
            cols = slice(start, start + TILE)
            grad_hidden = mm(tokens, big[:, 2 * wide_f + start : 2 * wide_f + start + TILE])
            grad_gate_up[s, :, cols] = (grad_hidden * wide_b[s, :, cols].astype(f32)).astype(bf16)
            grad_gate_up[s, :, wide_f + start : wide_f + start + TILE] = (
                grad_hidden * wide_a[s, :, cols].astype(f32)
            ).astype(bf16)

    def give_back(s, source, weight, first, size, target):
        tokens = source[s]
        for start in range(0, width, TILE):
            target[s, :, start : start + TILE] = mm_nt(
                tokens, weight[start : start + TILE, first : first + size]
            ).astype(bf16)

    def collected(block, given, land):
        total = sq.chunk(given)[block].astype(f32)
        for j in range(len(SQUARE)):
            total = total + land[j, block].astype(f32)
        return total

    def exchange(source, weight, first, size, target, land, which):
        give_back(sq.next, source, weight, first, size, target)
        send, recv = v.g_send.at[which], v.g_recv.at[which]
        pushes = [sq.give(target, land, send, recv, j) for j in (1, 2)]
        give_back(sq.own, source, weight, first, size, target)
        pushes.append(sq.give(target, land, send, recv, 0))
        return pushes

    members = [
        (v.turned, outer, 0, wide_f),
        (v.normed_t, grad_gate_up, 0, wide_f),
        (v.normed_t, grad_gate_up, wide_f, wide_f),
        (v.turned, outer, 0, wide_v),
        (v.normed_t, grad_qkvs, 0, 2 * wide_k),
        (v.normed_t, grad_qkvs, 2 * wide_k, wide_v),
        (v.normed_t, grad_qkvs, 2 * wide_k + wide_v, wide_v),
    ]
    given_copies, own_copies, fetches = {}, {}, {}

    def product(e, dp):
        left, right, first, size = members[e]
        start = pl.multiple_of(dp * slice_rows, slice_rows)
        wide = right[:, :, first : first + size].reshape(-1, size)
        return mm(left[pl.ds(start, slice_rows), :], wide)

    def given(e):
        if e >= 2:
            given_copies[e - 2].wait_send()
        stage = v.stage_given.at[e % 2]

        @pl.loop(0, slices)
        def _(j):
            stage[j] = product(e, j * 2 + 1 - at.core).astype(bf16)

        given_copies[e] = remote(stage, v.core_land.at[e], v.c_send.at[e], v.c_recv.at[e], sibling)
        given_copies[e].start()

    def fetch(e):
        given_copies[e].wait_recv()
        fetches[e] = pltpu.make_async_copy(v.core_land.at[e], v.core_part, v.local_sem.at[0])
        fetches[e].start()

    def settle(e):
        if e in settled:
            return
        settled.append(e)
        own_copies[e].wait()
        if final_layer:

            @pl.when(at.section == 1)
            def _():
                start_x(e, v.chip)

    def own(e):
        if e >= 1:
            settle(e - 1)
        fetches[e].wait()

        @pl.loop(0, slices)
        def _(j):
            v.stage_own[j] = (product(e, j * 2 + at.core) + v.core_part[j].astype(f32)).astype(bf16)

        own_copies[e] = pltpu.make_async_copy(v.stage_own, v.chip.at[e], v.local_sem.at[1])
        own_copies[e].start()

    settled = []

    def index(k, b):
        return ((at.group + k) % at.groups) * 2 + (at.low + b) % 2

    def z_copy(e, j):
        k, b = steps[j]
        return remote(
            v.sums.at[j], v.final.at[e, k, at.low], v.z_send.at[e, j], v.z_recv.at[e, j], place(dp=at.dp_at(k, b))
        )

    def home_copy(e):
        return pltpu.make_async_copy(v.sums.at[slices - 1], v.final.at[e, 0, at.low], v.r_sem.at[2, 0])

    def reduce_group(e, source, wait_previous):
        def loads(j):
            here = index(*steps[j])
            return (
                pltpu.make_async_copy(source.at[e, here], v.left.at[j % 2], v.r_sem.at[0, j % 2]),
                pltpu.make_async_copy(v.x_land.at[e, here], v.right.at[j % 2], v.r_sem.at[1, j % 2]),
            )

        def begin(j):
            x_copy(e, index(*steps[j]), source).wait_recv()
            for copy in loads(j):
                copy.start()

        begin(0)
        for j in range(slices):
            if j + 1 < slices:
                begin(j + 1)
            for copy in loads(j):
                copy.wait()
            if wait_previous is not None:
                last = j == slices - 1

                @pl.when(wait_previous)
                def _():
                    if last:
                        home_copy(e).wait()
                    else:
                        z_copy(e - 1, j).wait_send()

            v.sums[j] = (v.left[j % 2].astype(f32) + v.right[j % 2].astype(f32)).astype(bf16)
            if j == slices - 1:
                home_copy(e).start()
            else:
                z_copy(e, j).start()

    def reduce_for(section, source, first, stop):
        @pl.when(at.section == section)
        def _():
            @pl.loop(first, stop)
            def _(e):
                reduce_group(e, source, e > 0)

    token_load.wait()
    if final_layer:
        hidden_load.wait()
        transpose_into(v.turned, grad_down)
        given(0)
    down_load.wait()
    act_load.wait()
    slope_load.wait()
    through_down(sq.next)
    through_down(sq.own)
    unit_load = load(1, v.unit, wide_a)
    bend_load = load(2, v.slope_open, wide_b)
    gate_load.wait()
    gives = exchange(grad_gate_up, big, 0, 2 * wide_f, parts, landed, 0)
    if not final_layer:
        hidden_load.wait()
        transpose_into(v.turned, grad_down)
        given(0)
        for s in (sq.next, sq.own):
            give_back(s, outer, big, 2 * wide_f, wide_f, v.parts_y)
    fetch(0)
    own(0)
    mid_load.wait()
    given(1)
    qkvs_load = load(3, v.qkvs_all.at[layer], big)
    merged_load = load(4, v.merged, outer)
    for copy in early:
        copy.wait()
    settle(0)
    for push in gives:
        push.wait_recv()

    def through_mid(block):
        upstream = collected(block, parts, landed)
        normed, scale = norm_parts(v.middle_v[block])
        grad_rows = v.grad_out[block].astype(f32) + norm_grad(normed, scale, upstream, gain_mid)
        v.grad_middle[block] = grad_rows
        sq.chunk(grad_branch)[block] = grad_rows.astype(bf16)
        terms[1:2] = terms[1:2] + jnp.sum(upstream * normed, axis=0, keepdims=True)

    row_blocks(rows, through_mid)
    mids = sq.spread(grad_branch, v.s_send, v.s_recv)
    given(2)
    fetch(1)
    own(1)
    unit_load.wait()
    bend_load.wait()
    settle(1)

    def through_heads(s):
        tokens = grad_branch[s]
        for head in range(heads):
            cols_k = slice(head * HEAD_K, (head + 1) * HEAD_K)
            cols_v = slice(head * HEAD_V, (head + 1) * HEAD_V)
            grad_merged = mm(tokens, out_t[:, cols_v])
            unit_rows = wide_a[s, :, cols_v].astype(f32)
            first = 2 * wide_k + wide_v + head * HEAD_V
            grad_qkvs[s, :, first : first + HEAD_V] = (
                grad_merged * unit_rows * wide_b[s, :, cols_v].astype(f32)
            ).astype(bf16)
            grad_unit = grad_merged * wide_c[s, :, cols_v].astype(f32)
            grad_mixed = (
                v.inverse_v[s, head]
                * (
                    grad_unit
                    - jnp.mean(grad_unit, axis=-1, keepdims=True)
                    - unit_rows * jnp.mean(grad_unit * unit_rows, axis=-1, keepdims=True)
                )
            ).astype(bf16)
            query, key, val = query_v[s, :, cols_k], key_v[s, :, cols_k], value_v[s, :, cols_v]
            mask = masks[s, head]
            weight = (mm_nt(query, key) * mask).astype(bf16)
            grad_product = (mm_nt(grad_mixed, val) * mask).astype(bf16)
            first = 2 * wide_k + head * HEAD_V
            grad_qkvs[s, :, first : first + HEAD_V] = mm_tn(weight, grad_mixed).astype(bf16)
            grad_qkvs[s, :, cols_k] = turn_back(mm(grad_product, key), tables[0], tables[1], tables[2]).astype(bf16)
            first = wide_k + head * HEAD_K
            grad_qkvs[s, :, first : first + HEAD_K] = turn_back(
                mm_tn(grad_product, query), tables[0], tables[1], tables[3]
            ).astype(bf16)

    mids[0].wait_recv()
    through_heads(sq.own)
    mids[1].wait_recv()
    mids[2].wait_recv()
    if not final_layer:
        gives_y = [sq.give(v.parts_y, v.landed_y, v.g_send.at[2], v.g_recv.at[2], j) for j in range(3)]
    through_heads(sq.next)
    qkvs_load.wait()
    for push in gives:
        push.wait_send()
    ends = exchange(grad_qkvs, big, 0, grad_qkvs.shape[-1], parts, landed, 1)
    fetch(2)
    own(2)
    in_load = load(5, v.normed_in_t, v.normed_t)
    transpose_into(v.turned, grad_branch)
    settle(2)
    merged_load.wait()
    given(3)
    in_load.wait()
    given(4)
    fetch(3)
    own(3)
    if final_layer:
        reduce_for(1, v.later_chip, 0, 1)
        reduce_for(0, v.chip, 0, 1)
    settle(3)
    for push in ends:
        push.wait_recv()

    def through_in(block):
        upstream = collected(block, parts, landed)
        normed, scale = norm_parts(v.x_v[block].astype(f32))
        v.grad_in[block] = (v.grad_middle[block] + norm_grad(normed, scale, upstream, gain_in)).astype(bf16)
        terms[0:1] = terms[0:1] + jnp.sum(upstream * normed, axis=0, keepdims=True)

    row_blocks(rows, through_in)
    if final_layer:

        @pl.when(at.section == 1)
        def _():
            remote(v.grad_in, v.taken_grads, v.row_send.at[1], v.row_recv.at[1], across).start()

    else:
        downs = sq.spread_from(v.grad_in, v.next_down, v.d_send, v.d_recv, v.d_sem)

    given(5)
    fetch(4)
    own(4)
    given(6)
    settle(4)
    fetch(5)
    own(5)
    if not final_layer:
        for push in gives_y:
            push.wait_recv()

        def last(block):
            v.result[block] = (
                v.middle_v[block] + collected(block, v.parts_y, v.landed_y)
            ).astype(bf16)

        row_blocks(rows, last)
    fetch(6)
    own(6)
    settle(6)
    for push in mids + ends:
        push.wait_send()
    for e in (5, 6):
        given_copies[e].wait_send()
    if not final_layer:
        for push in gives_y:
            push.wait_send()
        for push in downs:
            push.wait()
        return

    reduce_for(1, v.later_chip, 1, GROUPS)
    reduce_for(0, v.chip, 1, GROUPS)

    held, hop_land, mine = v.held, v.hop_land, v.held.at[at.section]
    held[0] = terms[...]
    held[1] = v.later_terms[...]
    hop = remote(held, hop_land.at[0], v.t_send.at[0], v.t_recv.at[0], sibling)
    hop.start()
    hop.wait()
    held[...] = held[...] + hop_land[0]
    hop = remote(held.at[other], hop_land.at[1, other], v.t_send.at[1], v.t_recv.at[1], across)
    hop.start()
    hop.wait_send()
    remote(held.at[other], hop_land.at[1, at.section], v.t_send.at[1], v.t_recv.at[1], across).wait_recv()
    mine[...] = mine[...] + hop_land[1, at.section]
    for h, device in ((2, place(tensor=1 - at.tensor)), (3, place(dp=at.dp_at(0, 1)))):
        hop = remote(mine, hop_land.at[h, 0], v.t_send.at[h], v.t_recv.at[h], device)
        hop.start()
        hop.wait()
        mine[...] = mine[...] + hop_land[h, 0]
    hops = []
    for k in range(1, at.groups):
        hop = remote(mine, hop_land.at[3 + k, 0], v.t_send.at[3 + k], v.t_recv.at[3 + k], place(dp=at.dp_at(k, 0)))
        hop.start()
        hops.append(hop)
    total = mine[...]
    for k, hop in zip(range(1, at.groups), hops):
        hop.wait()
        total = total + hop_land[3 + k, 0]
    v.gain_sums[...] = total

    for which, rows_sent in ((0, v.second_rows), (1, v.grad_in)):
        target = v.taken_rows if which == 0 else v.taken_grads
        copy = remote(rows_sent, target, v.row_send.at[which], v.row_recv.at[which], across)
        copy.wait_recv()
        copy.wait_send()

    home_copy(0).wait()
    for j in range(slices - 1):
        z_copy(GROUPS - 1, j).wait_send()

        @pl.loop(0, GROUPS)
        def _(e):
            z_copy(e, j).wait_recv()

    @pl.loop(0, GROUPS)
    def _(e):
        @pl.loop(0, slices)
        def _(j):
            x_copy(e, j, v.chip).wait_send()


def backward_layer(layer, grad_out, down, x, gains, tables, masks, saved, gathered, dp_size, later=None, rows_out=None):
    rows, width = x.shape
    length = masks.shape[-1]
    (middle, normed_in_t, query_rot, key_rot, value, unit, inverse, opened, slope_open, merged, normed_mid_t, act, slope,
     hidden) = saved
    vmem = pl.BlockSpec(memory_space=pltpu.VMEM)
    any_spec = pl.BlockSpec(memory_space=pl.ANY)
    final_layer = layer == 0
    slices = dp_size // 2
    slice_rows = width // dp_size
    size = hidden.shape[-1]
    assert value.shape[-1] == size and 2 * query_rot.shape[-1] == size
    block = (slices, slice_rows, size)

    def held(*shape, kind=bf16):
        return pltpu.VMEM(shape, kind)

    def stored(*shape, kind=bf16):
        return jax.ShapeDtypeStruct(shape, kind)

    dma = pltpu.SemaphoreType.DMA
    operands = [grad_out, gains, tables, masks]
    operands += [x, middle, normed_in_t, query_rot, key_rot, value, unit, inverse, opened, slope_open, merged, normed_mid_t,
                 act, slope, hidden]
    operands += [*gathered, down]
    in_specs = [vmem] * 4 + [any_spec] * (len(operands) - 4)
    out_shape = [stored(rows, width), stored(GROUPS, *block), stored(GROUPS, *block)]
    out_specs = [vmem, any_spec, any_spec]
    if final_layer:
        later_chip, later_terms = later
        operands += [later_chip, later_terms, *rows_out]
        in_specs += [any_spec, vmem, any_spec, any_spec]
        out_shape += [stored(GROUPS, *block), stored(GROUPS, dp_size // 4, 2, slice_rows, size), stored(2, width, kind=f32),
                      stored(rows, width), stored(rows, width)]
        out_specs += [any_spec, any_spec, vmem, any_spec, any_spec]
    else:
        out_shape += [stored(2, width, kind=f32), stored(rows, width), stored(2, length, width)]
        out_specs += [vmem, vmem, any_spec]
    scratch = [
        held(width, 3 * size),
        held(width, size),
        held(*query_rot.shape),
        held(*key_rot.shape),
        held(*value.shape),
        held(2, length, size),
        held(2, length, size),
        held(2, length, size),
        held(*inverse.shape, kind=f32),
        held(rows, width),
        held(rows, width, kind=f32),
        held(width, 2 * length),
        held(2, length, size),
        held(2, length, width),
        held(2, length, 2 * size),
        held(2, length, width),
        held(2, length, 3 * size),
        held(width, 2 * length),
        held(2, length, width),
        held(3, rows, width),
        held(rows, width, kind=f32),
        held(2, *block),
        held(*block),
        held(*block),
        dma((15,)),
        dma((3,)),
        dma((3,)),
        dma((3, 3)),
        dma((3, 3)),
        dma((GROUPS,)),
        dma((GROUPS,)),
        dma((2,)),
    ]
    if final_layer:
        hops = 3 + dp_size // 4
        scratch += [
            held(2, slice_rows, size),
            held(2, slice_rows, size),
            held(*block),
            dma((3, 2)),
            dma((GROUPS, slices)),
            dma((GROUPS, slices)),
            dma((GROUPS, slices - 1)),
            dma((GROUPS, slices - 1)),
            held(2, width, kind=f32),
            held(2, 2, width, kind=f32),
            held(hops, 2, 2, width, kind=f32),
            dma((hops,)),
            dma((hops,)),
            dma((2,)),
            dma((2,)),
        ]
    else:
        scratch += [held(2, length, width), held(3, rows, width), dma((3,)), dma((3,)), dma]
    return pl.pallas_call(
        functools.partial(backward_kernel, dp_size, layer),
        out_shape=out_shape,
        in_specs=in_specs,
        out_specs=out_specs,
        scratch_shapes=scratch,
        compiler_params=pltpu.CompilerParams(
            collective_id=4 + layer, has_side_effects=True, vmem_limit_bytes=VMEM_LIMIT
        ),
        name="backward_layer",
    )(*operands)


def nested(outs):
    return (*outs[:5], outs[5:-2], *outs[-2:])


def on_device(
    dp_size,
    layer_input,
    segment_ids,
    output_grad,
    query_weight,
    key_weight,
    value_weight,
    swish_weight,
    output_weight,
    gate_weight,
    up_weight,
    down_weight,
    mixer_gain,
    ffn_gain,
):
    at = Place(dp_size)
    section_first = at.section == 0
    rows_here, width = layer_input.shape[1:]
    length = segment_ids.shape[1]
    score_scale = HEAD_K ** (-0.5)

    quarter_k = query_weight.shape[2] // 2
    quarter_v = value_weight.shape[2] // 2
    quarter_f = gate_weight.shape[2] // 2
    heads_here = quarter_k // HEAD_K
    first_head = (at.tensor * 2 + at.low) * heads_here
    cosine, sine, growth = rotation_tables(length, HEAD_K // 2)

    ids_mine = lax.dynamic_index_in_dim(segment_ids, at.section, 0, keepdims=False)
    ids_pair = lax.ppermute(ids_mine, "dp", [(i, i ^ 2) for i in range(dp_size)])
    ids = jnp.where(at.low == 0, jnp.stack([ids_mine, ids_pair]), jnp.stack([ids_pair, ids_mine]))
    masks = decay_mask(ids, first_head, heads_here) * score_scale
    tables = jnp.stack([cosine, sine, growth, 1.0 / growth])

    first_in = lax.dynamic_index_in_dim(layer_input, at.section, 0, keepdims=False)
    out_grad = lax.dynamic_index_in_dim(output_grad, at.section, 0, keepdims=False)
    shards = (query_weight[0], key_weight[0], value_weight[0], swish_weight[0], output_weight[0].T, gate_weight[0],
              up_weight[0], down_weight[0].T)
    own_gains = jnp.concatenate([mixer_gain, ffn_gain], axis=0)
    *gathered, all_gains, first_saved, second_down, first_sent = nested(
        forward_layer(0, first_in, own_gains, tables, masks, shards, dp_size, out_grad)
    )
    second_saved = forward_layer(1, first_sent, all_gains, tables, masks, gathered, dp_size)
    gathered = [g.reshape(2, width, g.shape[-1]) for g in gathered]
    second_grad, later_chip, _, later_terms, second_sent, first_down = backward_layer(
        1, out_grad, second_down, first_sent, all_gains, tables, masks, second_saved, gathered, dp_size
    )
    first_grad, _, _, _, landed, my_gains, taken_rows, taken_grads = backward_layer(
        0, second_grad, first_down, first_in, all_gains, tables, masks, first_saved, gathered, dp_size,
        (later_chip, later_terms), (first_sent, second_sent),
    )

    def by_layer(first, second, taken):
        return jnp.where(section_first, jnp.stack([first, taken]), jnp.stack([taken, second]))[None]

    def natural(e, start, size):
        part = jnp.sum(landed[e, :, :, :, start : start + size].astype(f32), axis=0)
        return part.swapaxes(0, 1).reshape(part.shape[1], -1)

    def tall(e):
        part = jnp.sum(landed[e].astype(f32), axis=0)
        return part.swapaxes(1, 2).reshape(-1, part.shape[1])

    return (
        by_layer(first_sent, second_sent, taken_rows),
        by_layer(first_grad, second_grad, taken_grads),
        natural(4, 0, quarter_k)[None],
        natural(4, quarter_k, quarter_k)[None],
        natural(5, 0, quarter_v)[None],
        natural(6, 0, quarter_v)[None],
        tall(3)[None],
        natural(1, 0, quarter_f)[None],
        natural(2, 0, quarter_f)[None],
        tall(0)[None],
        my_gains[0][None],
        my_gains[1][None],
    )


def solution(mesh):
    in_specs = (
        P(None, ("dp", "tensor"), None),
        P(None, "dp"),
        P(None, ("dp", "tensor"), None),
        P("section", "dp", "tensor"),
        P("section", "dp", "tensor"),
        P("section", "dp", "tensor"),
        P("section", "dp", "tensor"),
        P("section", "tensor", "dp"),
        P("section", "dp", "tensor"),
        P("section", "dp", "tensor"),
        P("section", "tensor", "dp"),
        P("section", None),
        P("section", None),
    )
    out_specs = (
        P("section", None, ("dp", "tensor"), None),
        P("section", None, ("dp", "tensor"), None),
        P("section", "dp", "tensor"),
        P("section", "dp", "tensor"),
        P("section", "dp", "tensor"),
        P("section", "dp", "tensor"),
        P("section", "tensor", "dp"),
        P("section", "dp", "tensor"),
        P("section", "dp", "tensor"),
        P("section", "tensor", "dp"),
        P("section", None),
        P("section", None),
    )
    return jax.shard_map(
        functools.partial(on_device, mesh.shape["dp"]),
        mesh=mesh,
        in_specs=in_specs,
        out_specs=out_specs,
        check_vma=False,
    )
```

time: 2230 us -> 1100 us (0.49)
  waiting for transfers between devices: 1520 us -> 0.01 us
  Pallas kernels: 0 us -> 1010 us
  matrix products: 383 us -> 0 us
  other arithmetic: 134 us -> 22.1 us
  blocking collectives: 57.9 us -> 0 us
  local copies, waits for them, and re-layouts: 90.1 us -> 40.9 us
    pallas_call x0 -> x4, Pallas kernels: none -> 1010 us  [the longest x2 567 us: backward_layer(): pl.pallas_call(functools.partial(backward_kernel, dp_size, layer), out_sh...]
    reduce_scatter x13 -> x0, waiting for transfers between devices: 744 us -> none  [the longest x1 495 us: on_device(): lax.psum_scatter(pack_terms(weight_terms(joined)).astype(jnp.bfloat16), '...]
    all_gather x20 -> x0, waiting for transfers between devices: 726 us -> none  [the longest x1 80.8 us: on_device(): lax.all_gather(gate_weight[0], 'dp', axis=0, tiled=True)]
    dot_general x65 -> x0, matrix products: 363 us -> none  [the longest x8 51.6 us: weight_terms(): jnp.einsum('tc,te->ce', left_rows, right_rows, preferred_element_type=jnp...]
    psum x1 -> x0, blocking collectives: 57.9 us -> none  [on_device(): mixer_sum, ffn_sum = lax.psum((mixer_total, ffn_total), ('dp', 'tensor'))]
    ppermute x4 -> x1, waiting for transfers between devices: 48.3 us -> 0.01 us  [on_device(): lax.ppermute(ids_mine, 'dp', [(i, i ^ 2) for i in range(dp_size)])]
    reduce_sum x40 -> x2, other arithmetic: 62.7 us -> 15.6 us  [the longest x1 12.2 us: tall(): part = jnp.sum(landed[e].astype(f32), axis=0)]
    unnamed x456 -> x30, local copies, waits for them, and re-layouts: 44.3 us -> 18.4 us
  transfers between devices with their start and end apart: 37 -> 1, of which waited for: 34 -> 0; matrix products, arithmetic and copies ran while one was open for 13% -> 1% of each run, Pallas kernels for 0% -> 0%
where the time goes in v1:
time: 1100 us; the launch traced here: 1080 us
  Pallas kernels  1010 us (92%)
  local copies, waits for them, and re-layouts  40.9 us (4%)
  other arithmetic  22.1 us (2%)
    pallas_call x2, Pallas kernels, backward_layer(): pl.pallas_call(functools.partial(backward_kernel, dp_size, layer), out_sh...  567 us
    pallas_call x2, Pallas kernels, forward_layer(): pl.pallas_call(functools.partial(forward_kernel, dp_size, layer), out_sha...  447 us
  transfers between devices with their start and end apart: 1, of which 0 were waited for; matrix products, arithmetic and copies ran while one was open for 1% of the time, Pallas kernels for 0%

profile of v1, /device:TPU:5, one launch (start us, length us, event | category | flops | bytes accessed | tf_op | source)
XLA Modules:
  0.0 1079.7 jit_solution(5885837031486731249)
XLA Ops:
  0.7 0.7 copy-done
  1.3 1.3 collective-permute-start
  2.7 1.3 pad_maximum_fusion.1.refs_1_
  4.2 2.4 dynamic-slice_bitcast_fusion
  6.6 0.6 multiply_cosine_fusion
  7.2 0.8 pad_maximum_fusion.refs_2_
  8.0 1.4 copy.29
  9.5 1.4 copy.30
  11.1 1.1 select_multiply_fusion.refs_3_
  12.1 369.7 %forward_layer.2 = (bf16[2,4,2,256,3072]{4,3,2,1,0:T(8,128)(2,1)}, bf16[2,4,2,256,1024]{4,3,2,1,0:T(8,128)(2,1)}, bf16[2,4,2,256,2048]{4,3,2,1,0:T(8,128)(2,1)},...) custom-call(bf16[128,2048]{1,0:T(8,128)(2,1)} %get-tuple-element.129, ...), custom_call_target="tpu_custom_call" | custom-call | tf_op jit(solution)/shard_map/forward_layer/pallas_call | solution.py:584
  381.9 77.1 %forward_layer.3 = (f32[128,2048]{1,0:T(8,128)}, bf16[2048,512]{1,0:T(8,128)(2,1)}, bf16[2,256,512]{2,1,0:T(8,128)(2,1)}, bf16[2,256,512]{2,1,0:T(8,128)(2,1)}, ...) custom-call(bf16[128,2048]{1,0:T(8,128)(2,1)} %get-tuple-element.57., ...), custom_call_target="tpu_custom_call" | custom-call | tf_op jit(solution)/shard_map/forward_layer/pallas_call | solution.py:584
  459.0 134.8 %backward_layer.2 = (bf16[128,2048]{1,0:T(8,128)(2,1)}, bf16[7,4,256,1024]{3,2,1,0:T(8,128)(2,1)}, bf16[7,4,256,1024]{3,2,1,0:T(8,128)(2,1)}, f32[2,2048]{1,0:T(...) custom-call(bf16[128,2048]{1,0:T(8,128)(2,1)} %get-tuple-element.128.refs_4_.refs_0_, ...), custom_call_target="tpu_custom_call" | custom-call | tf_op jit(solution)/shard_map/backward_layer/pallas_call | solution.py:1166
  593.8 432.5 %backward_layer.3 = (bf16[128,2048]{1,0:T(8,128)(2,1)}, bf16[7,4,256,1024]{3,2,1,0:T(8,128)(2,1)}, bf16[7,4,256,1024]{3,2,1,0:T(8,128)(2,1)}, bf16[7,4,256,1024]...) custom-call(bf16[128,2048]{1,0:T(8,128)(2,1)} %get-tuple-element.78., ...), custom_call_target="tpu_custom_call" | custom-call | tf_op jit(solution)/shard_map/backward_layer/pallas_call | solution.py:1166
  1026.3 3.4 convert_reduce_fusion.6
  1029.7 12.2 %convert_reduce_fusion = (f32[2,256,1024]{2,1,0:T(8,128)}, f32[2,256,1024]{2,1,0:T(8,128)}, f32[2,256,1024]{2,1,0:T(8,128)}, f32[2,256,1024]{2,1,0:T(8,128)}, f3...) fusion(bf16[7,2,2,256,1024]{4,3,2,1,0:T(8,128)(2,1)} %get-tuple-element.100), kind=kLoop, calls=%fused_computation | loop fusion | flops 9437184 | bytes 25165824 | tf_op jit(solution)/shard_map/reduce_sum | solution.py:1244
  1041.9 0.6 fusion
  1042.5 2.9 copy.38
  1045.4 2.9 copy.37
  1048.4 2.9 copy.44
  1051.2 1.6 copy.32
  1052.8 1.3 copy.40
  1054.1 1.6 copy.31
  1055.7 1.3 copy.39
  1057.0 2.9 copy.36
  1059.9 2.9 copy.43
  1062.8 2.9 copy.35
  1065.7 2.9 copy.34
  1068.6 2.9 copy.42
  1071.5 1.9 copy.33
  1073.4 3.0 copy.41
  1076.4 1.1 maximum_select_fusion
  1078.1 1.1 maximum_select_fusion.1
  (33 shorter events, 1.0 us)
Async XLA Ops:
  0.6 0.7 copy-start
  1.3 9.5 collective-permute-start
  4.1 3.9 copy-start.5
  6.6 2.9 copy-start.6
  1029.7 12.2 %copy-start.10 = (f32[2,2048]{1,0:T(2,128)S(1)}, f32[2,2048]{1,0:T(2,128)}, u32[]{:S(2)}) copy-start(f32[2,2048]{1,0:T(2,128)} %get-tuple-element.101) | copy-start | bytes 49156
  1073.4 3.0 copy-start.2
  1073.4 3.0 copy-start.4
  1073.4 3.0 copy-start.9
  1076.4 1.2 copy-start.3
  1076.4 1.4 copy-start.7
  1076.4 1.7 copy-start.8
  1076.4 2.9 copy-start.1

commit v2 on v1

--- a/solution.py
+++ b/solution.py
@@ -810,16 +810,18 @@
     def index(k, b):
         return ((at.group + k) % at.groups) * 2 + (at.low + b) % 2
 
+    def piece(e, k):
+        start = pl.multiple_of(at.low * wide_f, wide_f)
+        return v.final.at[e, k, :, pl.ds(start, wide_f)]
+
     def z_copy(e, j):
         k, b = steps[j]
-        return remote(
-            v.sums.at[j], v.final.at[e, k, at.low], v.z_send.at[e, j], v.z_recv.at[e, j], place(dp=at.dp_at(k, b))
-        )
+        return remote(v.sums.at[j], piece(e, k), v.z_send.at[e, j], v.z_recv.at[e, j], place(dp=at.dp_at(k, b)))
 
     def home_copy(e):
-        return pltpu.make_async_copy(v.sums.at[slices - 1], v.final.at[e, 0, at.low], v.r_sem.at[2, 0])
-
-    def reduce_group(e, source, wait_previous):
+        return pltpu.make_async_copy(v.sums.at[slices - 1], piece(e, 0), v.r_sem.at[2, 0])
+
+    def reduce_slices(e, source, first, stop, wait_previous):
         def loads(j):
             here = index(*steps[j])
             return (
@@ -832,21 +834,19 @@
             for copy in loads(j):
                 copy.start()
 
-        begin(0)
-        for j in range(slices):
-            if j + 1 < slices:
+        begin(first)
+        for j in range(first, stop):
+            if j + 1 < stop:
                 begin(j + 1)
             for copy in loads(j):
                 copy.wait()
-            if wait_previous is not None:
-                last = j == slices - 1
-
-                @pl.when(wait_previous)
-                def _():
-                    if last:
-                        home_copy(e).wait()
-                    else:
-                        z_copy(e - 1, j).wait_send()
+
+            @pl.when(wait_previous)
+            def _():
+                if j == slices - 1:
+                    home_copy(e).wait()
+                else:
+                    z_copy(e - 1, j).wait_send()
 
             v.sums[j] = (v.left[j % 2].astype(f32) + v.right[j % 2].astype(f32)).astype(bf16)
             if j == slices - 1:
@@ -854,12 +854,37 @@
             else:
                 z_copy(e, j).start()
 
-    def reduce_for(section, source, first, stop):
+    reduced = [0, 0]
+
+    def sources(section):
+        return v.later_chip if section == 1 else v.chip
+
+    def reduce_some(section, count):
+        if not final_layer:
+            return
+
         @pl.when(at.section == section)
         def _():
-            @pl.loop(first, stop)
+            done = reduced[section]
+            while done < reduced[section] + count:
+                e, first = divmod(done, slices)
+                stop = min(slices, first + reduced[section] + count - done)
+                reduce_slices(e, sources(section), first, stop, e > 0)
+                done += stop - first
+
+        reduced[section] += count
+
+    def reduce_rest(section):
+        @pl.when(at.section == section)
+        def _():
+            e, first = divmod(reduced[section], slices)
+            if first > 0:
+                reduce_slices(e, sources(section), first, slices, e > 0)
+                e += 1
+
+            @pl.loop(e, GROUPS)
             def _(e):
-                reduce_group(e, source, e > 0)
+                reduce_slices(e, sources(section), 0, slices, e > 0)
 
     token_load.wait()
     if final_layer:
@@ -884,12 +909,12 @@
     fetch(0)
     own(0)
     mid_load.wait()
+    settle(0)
     given(1)
     qkvs_load = load(3, v.qkvs_all.at[layer], big)
     merged_load = load(4, v.merged, outer)
     for copy in early:
         copy.wait()
-    settle(0)
     for push in gives:
         push.wait_recv()
 
@@ -903,12 +928,15 @@
 
     row_blocks(rows, through_mid)
     mids = sq.spread(grad_branch, v.s_send, v.s_recv)
+    reduce_some(0, 1)
     given(2)
     fetch(1)
     own(1)
     unit_load.wait()
     bend_load.wait()
     settle(1)
+    reduce_some(1, slices)
+    reduce_some(0, 1)
 
     def through_heads(s):
         tokens = grad_branch[s]
@@ -950,6 +978,7 @@
         gives_y = [sq.give(v.parts_y, v.landed_y, v.g_send.at[2], v.g_recv.at[2], j) for j in range(3)]
     through_heads(sq.next)
     qkvs_load.wait()
+    reduce_some(0, 1)
     for push in gives:
         push.wait_send()
     ends = exchange(grad_qkvs, big, 0, grad_qkvs.shape[-1], parts, landed, 1)
@@ -964,9 +993,8 @@
     given(4)
     fetch(3)
     own(3)
-    if final_layer:
-        reduce_for(1, v.later_chip, 0, 1)
-        reduce_for(0, v.chip, 0, 1)
+    reduce_some(1, slices)
+    reduce_some(0, 1)
     settle(3)
     for push in ends:
         push.wait_recv()
@@ -987,13 +1015,18 @@
     else:
         downs = sq.spread_from(v.grad_in, v.next_down, v.d_send, v.d_recv, v.d_sem)
 
+    reduce_some(0, 1)
     given(5)
     fetch(4)
     own(4)
+    reduce_some(0, 1)
     given(6)
     settle(4)
+    reduce_some(1, slices)
+    reduce_some(0, 1)
     fetch(5)
     own(5)
+    reduce_some(0, 1)
     if not final_layer:
         for push in gives_y:
             push.wait_recv()
@@ -1018,8 +1051,8 @@
             push.wait()
         return
 
-    reduce_for(1, v.later_chip, 1, GROUPS)
-    reduce_for(0, v.chip, 1, GROUPS)
+    reduce_rest(1)
+    reduce_rest(0)
 
     held, hop_land, mine = v.held, v.hop_land, v.held.at[at.section]
     held[0] = terms[...]
@@ -1102,7 +1135,7 @@
         later_chip, later_terms = later
         operands += [later_chip, later_terms, *rows_out]
         in_specs += [any_spec, vmem, any_spec, any_spec]
-        out_shape += [stored(GROUPS, *block), stored(GROUPS, dp_size // 4, 2, slice_rows, size), stored(2, width, kind=f32),
+        out_shape += [stored(GROUPS, *block), stored(GROUPS, dp_size // 4, slice_rows, 2 * size), stored(2, width, kind=f32),
                       stored(rows, width), stored(rows, width)]
         out_specs += [any_spec, any_spec, vmem, any_spec, any_spec]
     else:
@@ -1236,25 +1269,25 @@
     def by_layer(first, second, taken):
         return jnp.where(section_first, jnp.stack([first, taken]), jnp.stack([taken, second]))[None]
 
-    def natural(e, start, size):
-        part = jnp.sum(landed[e, :, :, :, start : start + size].astype(f32), axis=0)
-        return part.swapaxes(0, 1).reshape(part.shape[1], -1)
-
-    def tall(e):
-        part = jnp.sum(landed[e].astype(f32), axis=0)
-        return part.swapaxes(1, 2).reshape(-1, part.shape[1])
+    def shard(e):
+        return jnp.sum(landed[e].astype(f32), axis=0)
+
+    def columns(e, start, size):
+        step = landed.shape[-1] // 2
+        part = jnp.concatenate([landed[e, :, :, p * step + start : p * step + start + size] for p in range(2)], axis=-1)
+        return jnp.sum(part.astype(f32), axis=0)
 
     return (
         by_layer(first_sent, second_sent, taken_rows),
         by_layer(first_grad, second_grad, taken_grads),
-        natural(4, 0, quarter_k)[None],
-        natural(4, quarter_k, quarter_k)[None],
-        natural(5, 0, quarter_v)[None],
-        natural(6, 0, quarter_v)[None],
-        tall(3)[None],
-        natural(1, 0, quarter_f)[None],
-        natural(2, 0, quarter_f)[None],
-        tall(0)[None],
+        columns(4, 0, quarter_k)[None],
+        columns(4, quarter_k, quarter_k)[None],
+        shard(5)[None],
+        shard(6)[None],
+        shard(3).T[None],
+        shard(1)[None],
+        shard(2)[None],
+        shard(0).T[None],
         my_gains[0][None],
         my_gains[1][None],
     )

time: 1100 us -> 1060 us (0.964)
  local copies, waits for them, and re-layouts: 40.9 us -> 13.9 us
    transpose x8 -> x0, local copies, waits for them, and re-layouts: 19.6 us -> none  [the longest x6 13.8 us: natural(): return part.swapaxes(0, 1).reshape(part.shape[1], -1)]
where the time goes in v2:
time: 1060 us; the launch traced here: 1040 us
  Pallas kernels  1000 us (94%)
  other arithmetic  21.7 us (2%)
  local copies, waits for them, and re-layouts  13.9 us (1%)
    pallas_call x2, Pallas kernels, backward_layer(): pl.pallas_call(functools.partial(backward_kernel, dp_size, layer), out_sh...  557 us
    pallas_call x2, Pallas kernels, forward_layer(): pl.pallas_call(functools.partial(forward_kernel, dp_size, layer), out_sha...  447 us
  transfers between devices with their start and end apart: 1, of which 0 were waited for; matrix products, arithmetic and copies ran while one was open for 1% of the time, Pallas kernels for 0%

profile of v2, /device:TPU:5, one launch (start us, length us, event | category | flops | bytes accessed | tf_op | source)
XLA Modules:
  0.0 1041.8 jit_solution(311862492220823693)
XLA Ops:
  0.6 0.0 copy-start
  0.7 0.7 copy-done
  1.3 1.3 collective-permute-start
  2.7 1.3 pad_maximum_fusion.1.refs_1_
  4.1 0.1 multiply_exponential_fusion
  4.2 2.4 dynamic-slice_bitcast_fusion
  6.6 0.6 multiply_cosine_fusion
  7.2 0.8 pad_maximum_fusion.refs_2_
  8.0 0.0 copy-done.5
  8.0 1.4 copy.27
  9.5 0.0 copy-done.6
  9.5 1.4 copy.28
  10.9 0.0 collective-permute-done
  10.9 0.2 compare_and_fusion
  11.1 1.1 select_multiply_fusion.refs_3_
  12.1 369.7 %forward_layer.2 = (bf16[2,4,2,256,3072]{4,3,2,1,0:T(8,128)(2,1)}, bf16[2,4,2,256,1024]{4,3,2,1,0:T(8,128)(2,1)}, bf16[2,4,2,256,2048]{4,3,2,1,0:T(8,128)(2,1)},...) custom-call(bf16[128,2048]{1,0:T(8,128)(2,1)} %get-tuple-element.131, ...), custom_call_target="tpu_custom_call" | custom-call | tf_op jit(solution)/shard_map/forward_layer/pallas_call | solution.py:584
  381.9 77.1 %forward_layer.3 = (f32[128,2048]{1,0:T(8,128)}, bf16[2048,512]{1,0:T(8,128)(2,1)}, bf16[2,256,512]{2,1,0:T(8,128)(2,1)}, bf16[2,256,512]{2,1,0:T(8,128)(2,1)}, ...) custom-call(bf16[128,2048]{1,0:T(8,128)(2,1)} %get-tuple-element.57., ...), custom_call_target="tpu_custom_call" | custom-call | tf_op jit(solution)/shard_map/forward_layer/pallas_call | solution.py:584
  459.0 134.8 %backward_layer.2 = (bf16[128,2048]{1,0:T(8,128)(2,1)}, bf16[7,4,256,1024]{3,2,1,0:T(8,128)(2,1)}, bf16[7,4,256,1024]{3,2,1,0:T(8,128)(2,1)}, f32[2,2048]{1,0:T(...) custom-call(bf16[128,2048]{1,0:T(8,128)(2,1)} %get-tuple-element.130.refs_4_.refs_0_, ...), custom_call_target="tpu_custom_call" | custom-call | tf_op jit(solution)/shard_map/backward_layer/pallas_call | solution.py:1199
  593.8 422.0 %backward_layer.3 = (bf16[128,2048]{1,0:T(8,128)(2,1)}, bf16[7,4,256,1024]{3,2,1,0:T(8,128)(2,1)}, bf16[7,4,256,1024]{3,2,1,0:T(8,128)(2,1)}, bf16[7,4,256,1024]...) custom-call(bf16[128,2048]{1,0:T(8,128)(2,1)} %get-tuple-element.78., ...), custom_call_target="tpu_custom_call" | custom-call | tf_op jit(solution)/shard_map/backward_layer/pallas_call | solution.py:1199
  1015.8 2.7 slice_bitcast_fusion.1
  1018.5 11.6 %convert_reduce_fusion = (f32[256,2048]{1,0:T(8,128)}, f32[256,2048]{1,0:T(8,128)}, f32[256,2048]{1,0:T(8,128)}, f32[256,2048]{1,0:T(8,128)S(1)}, f32[256,2048]{1,0:T(8,128)}, /*index=5*/f32[256,2048]{1,0:T(8,128)}) fusion(bf16[7,2,256,2048]{3,2,1,0:T(8,128)(2,1)} %get-tuple-element.100), kind=kLoop, calls=%fused_computation | loop fusion | flops 9437184 | bytes 25165824 | tf_op jit(solution)/shard_map/reduce_sum | solution.py:1273
  1030.0 0.0 copy-done.10
  1030.1 0.6 fusion
  1030.7 2.9 copy.30
  1033.5 1.8 copy.29
  1035.4 2.6 convert_reduce_fusion.6
  1037.9 1.1 convert_reduce_fusion.7
  1039.1 0.0 copy-done.2
  1039.1 0.0 copy-done.4
  1039.1 1.1 maximum_select_fusion
  1040.2 0.0 copy-done.7
  1040.2 1.1 maximum_select_fusion.1
  (23 shorter events, 0.1 us)
Async XLA Ops:
  0.6 0.7 copy-start
  1.3 9.5 collective-permute-start
  4.1 3.9 copy-start.5
  6.6 2.9 copy-start.6
  1018.5 11.6 %copy-start.10 = (f32[2,2048]{1,0:T(2,128)S(1)}, f32[2,2048]{1,0:T(2,128)}, u32[]{:S(2)}) copy-start(f32[2,2048]{1,0:T(2,128)} %get-tuple-element.101) | copy-start | bytes 49156
  1035.4 3.7 copy-start.2
  1035.4 3.7 copy-start.4
  1035.4 3.7 copy-start.9
  1037.9 2.3 copy-start.3
  1037.9 2.3 copy-start.7
  1037.9 2.3 copy-start.8
  1039.1 2.3 copy-start.1

commit v3 on v2

--- a/solution.py
+++ b/solution.py
@@ -299,6 +299,11 @@
             slope[s, :, cols] = (slope_gelu * up).astype(bf16)
             hidden[s, :, cols] = (gelu * up).astype(bf16)
 
+    def turn_if(condition, target, source):
+        @pl.when(condition)
+        def _():
+            transpose_into(target, source)
+
     if not streams:
         for i in range(7):
             load(i)
@@ -310,6 +315,7 @@
             project(i, sq.own)
         ins[1].wait_recv()
         ins[2].wait_recv()
+        turn_if(at.core == at.section, normed_in_t, normed_in)
         for i in range(4):
             project(i, sq.next)
         retain(sq.next)
@@ -319,7 +325,7 @@
         retain(sq.own)
         give_back(sq.own, merged, out_t)
         gives += give(0, 0)
-        transpose_into(normed_in_t, normed_in)
+        turn_if(at.core != at.section, normed_in_t, normed_in)
         for push in gives:
             push.wait_recv()
         row_blocks(rows, second_norm)
@@ -453,7 +459,7 @@
     advance(7)
     for push in mids:
         push.wait_recv()
-    transpose_into(normed_mid_t, normed_mid)
+    turn_if(at.core == at.section, normed_mid_t, normed_mid)
     feed(sq.next)
     feed(sq.own)
     for push in gives:
@@ -477,6 +483,7 @@
     ends = give(1, 1)
     give_back(sq.own, hidden, down_t)
     ends += give(0, 1)
+    turn_if(at.core != at.section, normed_mid_t, normed_mid)
 
     @pl.when(at.section == 0)
     def _():
@@ -598,6 +605,7 @@
     pass
 
 
+KEPT = 5
 GROUPS = 7
 
 
@@ -608,21 +616,22 @@
      v.inverse, v.opened, v.slope_open, v.merged, v.normed_mid_t, v.act, v.slope, v.hidden,
      v.qkvs_all, v.out_all, v.gate_up_all, v.down_all, v.down_in, *refs) = refs
     if final_layer:
-        v.later_chip, v.later_terms, v.first_rows, v.second_rows, *refs = refs
+        (v.later_chip, v.later_terms, v.first_rows, v.later_normed_in_t, v.later_qkvs, v.later_hidden, v.later_middle,
+         *refs) = refs
     v.grad_in, v.chip, v.core_land, *refs = refs
     if final_layer:
-        v.x_land, v.final, v.gain_sums, v.taken_rows, v.taken_grads, *refs = refs
+        v.x_land, v.final, v.gain_sums, v.result, v.taken_rows, v.taken_grads, *refs = refs
     else:
-        v.terms, v.result, v.next_down, *refs = refs
+        v.terms, v.next_down, v.kept_qkvs, *refs = refs
     (v.big, v.out_t, v.query_v, v.key_v, v.value_v, v.wide_a, v.wide_b, v.wide_c, v.inverse_v, v.x_v, v.middle_v,
      v.normed_t, v.outer, v.grad_down, v.grad_gate_up, v.grad_branch, v.grad_qkvs, v.turned, v.parts, v.landed,
      v.grad_middle, v.stage_given, v.stage_own, v.core_part, v.load_sem, v.s_send, v.s_recv, v.g_send, v.g_recv,
      v.c_send, v.c_recv, v.local_sem, *refs) = refs
     if final_layer:
         (v.left, v.right, v.sums, v.r_sem, v.x_send, v.x_recv, v.z_send, v.z_recv, v.terms, v.held, v.hop_land,
-         v.t_send, v.t_recv, v.row_send, v.row_recv) = refs
+         v.t_send, v.t_recv, v.row_send, v.row_recv, v.landed_y) = refs
     else:
-        v.parts_y, v.landed_y, v.d_send, v.d_recv, v.d_sem = refs
+        v.d_send, v.d_recv, v.d_sem, v.kept_sem = refs
     at = Place(dp_size)
     rows, width = v.x.shape
     sq = Square(dp_size, rows)
@@ -691,25 +700,23 @@
         pl.semaphore_signal(barrier, inc=1, device_id=partner, device_id_type=MESH)
     pl.semaphore_wait(barrier, len(partners))
 
-    def x_copy(e, j, source):
-        block = source.at[e, j]
+    def x_copy(e, at_source, j, source):
+        block = source.at[at_source, j]
         return remote(block, v.x_land.at[e, j], v.x_send.at[e, j], v.x_recv.at[e, j], across)
 
-    def start_x(e, source):
+    def start_x(e, at_source, source):
         @pl.loop(0, slices)
         def _(j):
-            x_copy(e, j, source).start()
+            x_copy(e, at_source, j, source).start()
 
     row_copies = []
     if final_layer:
 
         @pl.when(at.section == 0)
         def _():
-            remote(v.second_rows, v.taken_rows, v.row_send.at[0], v.row_recv.at[0], across).start()
-
-            @pl.loop(0, GROUPS)
+            @pl.loop(0, KEPT)
             def _(e):
-                start_x(e, v.later_chip)
+                start_x(e, e, v.later_chip)
 
             remote(v.grad_out, v.taken_grads, v.row_send.at[1], v.row_recv.at[1], across).start()
 
@@ -757,6 +764,7 @@
         (v.normed_t, grad_qkvs, 2 * wide_k, wide_v),
         (v.normed_t, grad_qkvs, 2 * wide_k + wide_v, wide_v),
     ]
+    members += members[KEPT:]
     given_copies, own_copies, fetches = {}, {}, {}
 
     def product(e, dp):
@@ -789,9 +797,9 @@
         own_copies[e].wait()
         if final_layer:
 
-            @pl.when(at.section == 1)
+            @pl.when(at.section == (1 if e < GROUPS else 0))
             def _():
-                start_x(e, v.chip)
+                start_x(e if e < GROUPS else e - GROUPS + KEPT, e, v.chip)
 
     def own(e):
         if e >= 1:
@@ -821,16 +829,16 @@
     def home_copy(e):
         return pltpu.make_async_copy(v.sums.at[slices - 1], piece(e, 0), v.r_sem.at[2, 0])
 
-    def reduce_slices(e, source, first, stop, wait_previous):
+    def reduce_slices(e, at_source, source, first, stop, wait_previous):
         def loads(j):
             here = index(*steps[j])
             return (
-                pltpu.make_async_copy(source.at[e, here], v.left.at[j % 2], v.r_sem.at[0, j % 2]),
+                pltpu.make_async_copy(source.at[at_source, here], v.left.at[j % 2], v.r_sem.at[0, j % 2]),
                 pltpu.make_async_copy(v.x_land.at[e, here], v.right.at[j % 2], v.r_sem.at[1, j % 2]),
             )
 
         def begin(j):
-            x_copy(e, index(*steps[j]), source).wait_recv()
+            x_copy(e, at_source, index(*steps[j]), source).wait_recv()
             for copy in loads(j):
                 copy.start()
 
@@ -856,8 +864,10 @@
 
     reduced = [0, 0]
 
-    def sources(section):
-        return v.later_chip if section == 1 else v.chip
+    def source_of(section, e):
+        if section == 0:
+            return e, v.chip
+        return (e, v.later_chip) if e < KEPT else (e + GROUPS - KEPT, v.chip)
 
     def reduce_some(section, count):
         if not final_layer:
@@ -869,22 +879,28 @@
             while done < reduced[section] + count:
                 e, first = divmod(done, slices)
                 stop = min(slices, first + reduced[section] + count - done)
-                reduce_slices(e, sources(section), first, stop, e > 0)
+                reduce_slices(e, *source_of(section, e), first, stop, e > 0)
                 done += stop - first
 
         reduced[section] += count
 
     def reduce_rest(section):
+        e, first = divmod(reduced[section], slices)
+
         @pl.when(at.section == section)
         def _():
-            e, first = divmod(reduced[section], slices)
+            begin = e
             if first > 0:
-                reduce_slices(e, sources(section), first, slices, e > 0)
-                e += 1
-
-            @pl.loop(e, GROUPS)
-            def _(e):
-                reduce_slices(e, sources(section), 0, slices, e > 0)
+                reduce_slices(e, *source_of(section, e), first, slices, e > 0)
+                begin = e + 1
+            same = KEPT if section == 1 else GROUPS
+
+            @pl.loop(begin, same)
+            def _(i):
+                reduce_slices(i, i, source_of(section, 0)[1], 0, slices, i > 0)
+
+            for i in range(same, GROUPS):
+                reduce_slices(i, *source_of(section, i), 0, slices, True)
 
     token_load.wait()
     if final_layer:
@@ -904,8 +920,6 @@
         hidden_load.wait()
         transpose_into(v.turned, grad_down)
         given(0)
-        for s in (sq.next, sq.own):
-            give_back(s, outer, big, 2 * wide_f, wide_f, v.parts_y)
     fetch(0)
     own(0)
     mid_load.wait()
@@ -974,9 +988,10 @@
     through_heads(sq.own)
     mids[1].wait_recv()
     mids[2].wait_recv()
+    through_heads(sq.next)
     if not final_layer:
-        gives_y = [sq.give(v.parts_y, v.landed_y, v.g_send.at[2], v.g_recv.at[2], j) for j in range(3)]
-    through_heads(sq.next)
+        keep = pltpu.make_async_copy(grad_qkvs, v.kept_qkvs, v.kept_sem)
+        keep.start()
     qkvs_load.wait()
     reduce_some(0, 1)
     for push in gives:
@@ -1015,6 +1030,19 @@
     else:
         downs = sq.spread_from(v.grad_in, v.next_down, v.d_send, v.d_recv, v.d_sem)
 
+    if not final_layer:
+        fetch(4)
+        own(4)
+        settle(4)
+        for push in mids + ends:
+            push.wait_send()
+        for e in (3, 4):
+            given_copies[e].wait_send()
+        for push in downs:
+            push.wait()
+        keep.wait()
+        return
+
     reduce_some(0, 1)
     given(5)
     fetch(4)
@@ -1027,30 +1055,53 @@
     fetch(5)
     own(5)
     reduce_some(0, 1)
-    if not final_layer:
-        for push in gives_y:
-            push.wait_recv()
-
-        def last(block):
-            v.result[block] = (
-                v.middle_v[block] + collected(block, v.parts_y, v.landed_y)
-            ).astype(bf16)
-
-        row_blocks(rows, last)
     fetch(6)
     own(6)
+    in_load = load(5, v.later_normed_in_t, v.normed_t)
+    qkvs_load = load(3, v.later_qkvs, grad_qkvs)
+    hidden_load = load(4, v.later_hidden, outer)
+    middle_load = load(6, v.later_middle, v.middle_v)
+    down_load = load(0, v.down_all.at[1], big.at[:, pl.ds(2 * wide_f, wide_f)])
     settle(6)
+    reduce_some(1, slices)
+    reduce_some(0, 1)
+    in_load.wait()
+    qkvs_load.wait()
+    given(7)
+    reduce_some(0, 1)
+    given(8)
+    fetch(7)
+    own(7)
+    reduce_some(0, 1)
+    fetch(8)
+    own(8)
+    settle(7)
+    reduce_some(0, 1)
     for push in mids + ends:
         push.wait_send()
-    for e in (5, 6):
+    hidden_load.wait()
+    down_load.wait()
+    settle(8)
+    gives_y = exchange(outer, big, 2 * wide_f, wide_f, parts, v.landed_y, 2)
+    reduce_some(1, slices)
+    reduce_some(0, slices)
+    middle_load.wait()
+    for push in gives_y:
+        push.wait_recv()
+
+    def last(block):
+        v.result[block] = (v.middle_v[block] + collected(block, parts, v.landed_y)).astype(bf16)
+
+    row_blocks(rows, last)
+
+    @pl.when(at.section == 0)
+    def _():
+        remote(v.result, v.taken_rows, v.row_send.at[0], v.row_recv.at[0], across).start()
+
+    for push in gives_y:
+        push.wait_send()
+    for e in (7, 8):
         given_copies[e].wait_send()
-    if not final_layer:
-        for push in gives_y:
-            push.wait_send()
-        for push in downs:
-            push.wait()
-        return
-
     reduce_rest(1)
     reduce_rest(0)
 
@@ -1082,7 +1133,7 @@
         total = total + hop_land[3 + k, 0]
     v.gain_sums[...] = total
 
-    for which, rows_sent in ((0, v.second_rows), (1, v.grad_in)):
+    for which, rows_sent in ((0, v.result), (1, v.grad_in)):
         target = v.taken_rows if which == 0 else v.taken_grads
         copy = remote(rows_sent, target, v.row_send.at[which], v.row_recv.at[which], across)
         copy.wait_recv()
@@ -1100,10 +1151,10 @@
     def _(e):
         @pl.loop(0, slices)
         def _(j):
-            x_copy(e, j, v.chip).wait_send()
-
-
-def backward_layer(layer, grad_out, down, x, gains, tables, masks, saved, gathered, dp_size, later=None, rows_out=None):
+            x_copy(e, e, j, v.chip).wait_send()
+
+
+def backward_layer(layer, grad_out, down, x, gains, tables, masks, saved, gathered, dp_size, later=None, x_out=None):
     rows, width = x.shape
     length = masks.shape[-1]
     (middle, normed_in_t, query_rot, key_rot, value, unit, inverse, opened, slope_open, merged, normed_mid_t, act, slope,
@@ -1129,18 +1180,19 @@
                  act, slope, hidden]
     operands += [*gathered, down]
     in_specs = [vmem] * 4 + [any_spec] * (len(operands) - 4)
-    out_shape = [stored(rows, width), stored(GROUPS, *block), stored(GROUPS, *block)]
+    count = 2 * GROUPS - KEPT if final_layer else KEPT
+    out_shape = [stored(rows, width), stored(count, *block), stored(count, *block)]
     out_specs = [vmem, any_spec, any_spec]
     if final_layer:
-        later_chip, later_terms = later
-        operands += [later_chip, later_terms, *rows_out]
-        in_specs += [any_spec, vmem, any_spec, any_spec]
+        later_chip, later_terms, later_qkvs, later_saved = later
+        operands += [later_chip, later_terms, x_out, later_saved[1], later_qkvs, later_saved[-1], later_saved[0]]
+        in_specs += [any_spec, vmem] + [any_spec] * 5
         out_shape += [stored(GROUPS, *block), stored(GROUPS, dp_size // 4, slice_rows, 2 * size), stored(2, width, kind=f32),
-                      stored(rows, width), stored(rows, width)]
-        out_specs += [any_spec, any_spec, vmem, any_spec, any_spec]
+                      stored(rows, width), stored(rows, width), stored(rows, width)]
+        out_specs += [any_spec, any_spec, vmem, vmem, any_spec, any_spec]
     else:
-        out_shape += [stored(2, width, kind=f32), stored(rows, width), stored(2, length, width)]
-        out_specs += [vmem, vmem, any_spec]
+        out_shape += [stored(2, width, kind=f32), stored(2, length, width), stored(2, length, 3 * size)]
+        out_specs += [vmem, any_spec, any_spec]
     scratch = [
         held(width, 3 * size),
         held(width, size),
@@ -1171,8 +1223,8 @@
         dma((3,)),
         dma((3, 3)),
         dma((3, 3)),
-        dma((GROUPS,)),
-        dma((GROUPS,)),
+        dma((count,)),
+        dma((count,)),
         dma((2,)),
     ]
     if final_layer:
@@ -1193,9 +1245,10 @@
             dma((hops,)),
             dma((2,)),
             dma((2,)),
+            held(3, rows, width),
         ]
     else:
-        scratch += [held(2, length, width), held(3, rows, width), dma((3,)), dma((3,)), dma]
+        scratch += [dma((3,)), dma((3,)), dma, dma]
     return pl.pallas_call(
         functools.partial(backward_kernel, dp_size, layer),
         out_shape=out_shape,
@@ -1258,12 +1311,12 @@
     )
     second_saved = forward_layer(1, first_sent, all_gains, tables, masks, gathered, dp_size)
     gathered = [g.reshape(2, width, g.shape[-1]) for g in gathered]
-    second_grad, later_chip, _, later_terms, second_sent, first_down = backward_layer(
+    second_grad, later_chip, _, later_terms, first_down, later_qkvs = backward_layer(
         1, out_grad, second_down, first_sent, all_gains, tables, masks, second_saved, gathered, dp_size
     )
-    first_grad, _, _, _, landed, my_gains, taken_rows, taken_grads = backward_layer(
+    first_grad, _, _, _, landed, my_gains, second_sent, taken_rows, taken_grads = backward_layer(
         0, second_grad, first_down, first_in, all_gains, tables, masks, first_saved, gathered, dp_size,
-        (later_chip, later_terms), (first_sent, second_sent),
+        (later_chip, later_terms, later_qkvs, second_saved), first_sent,
     )
 
     def by_layer(first, second, taken):

time: 1060 us -> 1050 us (level)
  no operation moved by 1% of the time
where the time goes in v3:
time: 1050 us; the launch traced here: 1040 us
  Pallas kernels  998 us (95%)
  other arithmetic  21.7 us (2%)
  local copies, waits for them, and re-layouts  13.9 us (1%)
    pallas_call x2, Pallas kernels, backward_layer(): pl.pallas_call(functools.partial(backward_kernel, dp_size, layer), out_sh...  552 us
    pallas_call x2, Pallas kernels, forward_layer(): pl.pallas_call(functools.partial(forward_kernel, dp_size, layer), out_sha...  446 us
  transfers between devices with their start and end apart: 1, of which 0 were waited for; matrix products, arithmetic and copies ran while one was open for 1% of the time, Pallas kernels for 0%

profile of v3, /device:TPU:5, one launch (start us, length us, event | category | flops | bytes accessed | tf_op | source)
XLA Modules:
  0.0 1036.3 jit_solution(11419010971648533594)
XLA Ops:
  0.6 0.0 copy-start
  0.7 0.7 copy-done
  1.3 1.3 collective-permute-start
  2.7 1.3 pad_maximum_fusion.1.refs_1_
  4.1 0.1 multiply_exponential_fusion
  4.2 2.4 dynamic-slice_bitcast_fusion
  6.6 0.6 multiply_cosine_fusion
  7.2 0.8 pad_maximum_fusion.refs_2_
  8.0 0.0 copy-done.4
  8.0 1.4 copy.27
  9.5 0.0 copy-done.5
  9.5 1.4 copy.28
  10.9 0.0 collective-permute-done
  10.9 0.2 compare_and_fusion
  11.1 1.1 select_multiply_fusion.refs_3_
  12.1 369.1 %forward_layer.2 = (bf16[2,4,2,256,3072]{4,3,2,1,0:T(8,128)(2,1)}, bf16[2,4,2,256,1024]{4,3,2,1,0:T(8,128)(2,1)}, bf16[2,4,2,256,2048]{4,3,2,1,0:T(8,128)(2,1)},...) custom-call(bf16[128,2048]{1,0:T(8,128)(2,1)} %get-tuple-element.133, ...), custom_call_target="tpu_custom_call" | custom-call | tf_op jit(solution)/shard_map/forward_layer/pallas_call | solution.py:591
  381.2 77.2 %forward_layer.3 = (f32[128,2048]{1,0:T(8,128)}, bf16[2048,512]{1,0:T(8,128)(2,1)}, bf16[2,256,512]{2,1,0:T(8,128)(2,1)}, bf16[2,256,512]{2,1,0:T(8,128)(2,1)}, ...) custom-call(bf16[128,2048]{1,0:T(8,128)(2,1)} %get-tuple-element.58., ...), custom_call_target="tpu_custom_call" | custom-call | tf_op jit(solution)/shard_map/forward_layer/pallas_call | solution.py:591
  458.4 122.2 %backward_layer.2 = (bf16[128,2048]{1,0:T(8,128)(2,1)}, bf16[5,4,256,1024]{3,2,1,0:T(8,128)(2,1)}, bf16[5,4,256,1024]{3,2,1,0:T(8,128)(2,1)}, f32[2,2048]{1,0:T(...) custom-call(bf16[128,2048]{1,0:T(8,128)(2,1)} %get-tuple-element.132.refs_4_.refs_0_, ...), custom_call_target="tpu_custom_call" | custom-call | tf_op jit(solution)/shard_map/backward_layer/pallas_call | solution.py:1252
  580.6 429.6 %backward_layer.3 = (bf16[128,2048]{1,0:T(8,128)(2,1)}, bf16[9,4,256,1024]{3,2,1,0:T(8,128)(2,1)}, bf16[9,4,256,1024]{3,2,1,0:T(8,128)(2,1)}, bf16[7,4,256,1024]...) custom-call(bf16[128,2048]{1,0:T(8,128)(2,1)} %get-tuple-element.79., ...), custom_call_target="tpu_custom_call" | custom-call | tf_op jit(solution)/shard_map/backward_layer/pallas_call | solution.py:1252
  1010.3 2.7 slice_bitcast_fusion.1
  1013.0 11.6 %convert_reduce_fusion = (f32[256,2048]{1,0:T(8,128)}, f32[256,2048]{1,0:T(8,128)}, f32[256,2048]{1,0:T(8,128)}, f32[256,2048]{1,0:T(8,128)S(1)}, f32[256,2048]{1,0:T(8,128)}, /*index=5*/f32[256,2048]{1,0:T(8,128)}) fusion(bf16[7,2,256,2048]{3,2,1,0:T(8,128)(2,1)} %get-tuple-element.102), kind=kLoop, calls=%fused_computation | loop fusion | flops 9437184 | bytes 25165824 | tf_op jit(solution)/shard_map/reduce_sum | solution.py:1326
  1024.5 0.0 copy-done.10
  1024.5 0.6 fusion
  1025.2 2.9 copy.30
  1028.0 1.8 copy.29
  1029.8 2.6 convert_reduce_fusion.6
  1032.4 1.1 convert_reduce_fusion.7
  1033.5 0.0 copy-done.8
  1033.6 1.1 maximum_select_fusion
  1034.7 0.0 copy-done.6
  1034.7 1.1 maximum_select_fusion.1
  1035.8 0.0 copy-done.1
  (23 shorter events, 0.1 us)
Async XLA Ops:
  0.6 0.7 copy-start
  1.3 9.5 collective-permute-start
  4.1 3.9 copy-start.4
  6.6 2.9 copy-start.5
  1013.0 11.6 %copy-start.10 = (f32[2,2048]{1,0:T(2,128)S(1)}, f32[2,2048]{1,0:T(2,128)}, u32[]{:S(2)}) copy-start(f32[2,2048]{1,0:T(2,128)} %get-tuple-element.103) | copy-start | bytes 49156
  1029.8 3.7 copy-start.2
  1029.8 3.7 copy-start.8
  1029.8 3.7 copy-start.9
  1032.4 2.3 copy-start.3
  1032.4 2.3 copy-start.6
  1032.4 2.3 copy-start.7
  1033.5 2.3 copy-start.1

commit v4 on v3

--- a/solution.py
+++ b/solution.py
@@ -185,7 +185,12 @@
     if streams:
         (v.grad_down, result, *refs) = refs
     held, refs = refs[:4], refs[4:]
-    (w_sem, normed_in, normed_mid, parts, landed, s_send, s_recv, g_send, g_recv, *refs) = refs
+    (w_sem, normed_in, *refs) = refs
+    if streams:
+        (normed_mid, *refs) = refs
+    else:
+        normed_mid = normed_mid_t
+    (parts, landed, s_send, s_recv, g_send, g_recv, *refs) = refs
     x, tables, masks = v.x, v.tables, v.masks
     rows, width = x.shape
     sq = Square(dp_size, rows)
@@ -335,7 +340,6 @@
         mids[1].wait_recv()
         mids[2].wait_recv()
         feed(sq.next)
-        transpose_into(normed_mid_t, normed_mid)
         for push in ins + mids + gives:
             push.wait_send()
         return
@@ -436,7 +440,9 @@
     advance(1)
     for push in ins:
         push.wait_recv()
-    transpose_into(normed_in_t, normed_in)
+    late = jnp.logical_and(at.section == 1, at.core == 1)
+    early = jnp.logical_not(late)
+    turn_if(early, normed_in_t, normed_in)
     for i in range(2, 5):
         advance(i)
         for s in (sq.own, sq.next):
@@ -459,7 +465,7 @@
     advance(7)
     for push in mids:
         push.wait_recv()
-    turn_if(at.core == at.section, normed_mid_t, normed_mid)
+    turn_if(early, normed_mid_t, normed_mid)
     feed(sq.next)
     feed(sq.own)
     for push in gives:
@@ -479,11 +485,12 @@
 
     arrive(7)
     loads_wait(7)
+    turn_if(late, normed_in_t, normed_in)
+    turn_if(late, normed_mid_t, normed_mid)
     give_back(sq.next, hidden, down_t)
     ends = give(1, 1)
     give_back(sq.own, hidden, down_t)
     ends += give(0, 1)
-    turn_if(at.core != at.section, normed_mid_t, normed_mid)
 
     @pl.when(at.section == 0)
     def _():
@@ -546,7 +553,7 @@
         tokens(quarter_v),
         tokens(quarter_v),
         tokens(quarter_v),
-        turned,
+        turned if streams else tokens(width),
         tokens(quarter_f),
         tokens(quarter_f),
         tokens(quarter_f),
@@ -554,9 +561,7 @@
     out_specs = [vmem] * len(out_shape)
     scratch = [pltpu.VMEM((slices, 2, width // dp_size, wide), bf16) for wide in wides] + [
         dma((8,)),
-        pltpu.VMEM((2, length, width), bf16),
-        pltpu.VMEM((2, length, width), bf16),
-        pltpu.VMEM((2, length, width), bf16),
+    ] + [pltpu.VMEM((2, length, width), bf16)] * (3 if streams else 2) + [
         pltpu.VMEM((2, 3, rows, width), bf16),
         dma((2, 3)),
         dma((2, 3)),
@@ -631,7 +636,7 @@
         (v.left, v.right, v.sums, v.r_sem, v.x_send, v.x_recv, v.z_send, v.z_recv, v.terms, v.held, v.hop_land,
          v.t_send, v.t_recv, v.row_send, v.row_recv, v.landed_y) = refs
     else:
-        v.d_send, v.d_recv, v.d_sem, v.kept_sem = refs
+        v.d_send, v.d_recv, v.d_sem, v.kept_sem, v.mid_v = refs
     at = Place(dp_size)
     rows, width = v.x.shape
     sq = Square(dp_size, rows)
@@ -678,7 +683,7 @@
     slope_load = load(2, v.slope, wide_b)
     gate_load = load(3, v.gate_up_all.at[layer], big.at[:, pl.ds(0, 2 * wide_f)])
     hidden_load = load(4, v.hidden, outer)
-    mid_load = load(5, v.normed_mid_t, v.normed_t)
+    mid_load = load(5, v.normed_mid_t, v.normed_t if final_layer else v.mid_v)
     early = [
         load(6, v.middle, v.middle_v),
         load(7, v.x, v.x_v),
@@ -912,6 +917,11 @@
     slope_load.wait()
     through_down(sq.next)
     through_down(sq.own)
+    if final_layer:
+        fetch(0)
+        own(0)
+        mid_load.wait()
+        settle(0)
     unit_load = load(1, v.unit, wide_a)
     bend_load = load(2, v.slope_open, wide_b)
     gate_load.wait()
@@ -920,10 +930,11 @@
         hidden_load.wait()
         transpose_into(v.turned, grad_down)
         given(0)
-    fetch(0)
-    own(0)
-    mid_load.wait()
-    settle(0)
+        fetch(0)
+        own(0)
+        mid_load.wait()
+        transpose_into(v.normed_t, v.mid_v)
+        settle(0)
     given(1)
     qkvs_load = load(3, v.qkvs_all.at[layer], big)
     merged_load = load(4, v.merged, outer)
@@ -1248,7 +1259,7 @@
             held(3, rows, width),
         ]
     else:
-        scratch += [dma((3,)), dma((3,)), dma, dma]
+        scratch += [dma((3,)), dma((3,)), dma, dma, held(2, length, width)]
     return pl.pallas_call(
         functools.partial(backward_kernel, dp_size, layer),
         out_shape=out_shape,

time: 1050 us -> 1050 us (level); the launches traced: 1040 us -> 1050 us
  Pallas kernels: 998 us -> 1010 us
    pallas_call x2, Pallas kernels: 552 us -> 562 us  [backward_layer(): pl.pallas_call(functools.partial(backward_kernel, dp_size, layer), out_sh...]
where the time goes in v4:
time: 1050 us
  Pallas kernels  1010 us (96%)
  other arithmetic  21.7 us (2%)
  local copies, waits for them, and re-layouts  13.9 us (1%)
    pallas_call x2, Pallas kernels, backward_layer(): pl.pallas_call(functools.partial(backward_kernel, dp_size, layer), out_sh...  562 us
    pallas_call x2, Pallas kernels, forward_layer(): pl.pallas_call(functools.partial(forward_kernel, dp_size, layer), out_sha...  449 us
  transfers between devices with their start and end apart: 1, of which 0 were waited for; matrix products, arithmetic and copies ran while one was open for 1% of the time, Pallas kernels for 0%

profile of v4, /device:TPU:5, one launch (start us, length us, event | category | flops | bytes accessed | tf_op | source)
XLA Modules:
  0.0 1049.3 jit_solution(10209361489142757528)
XLA Ops:
  0.6 0.0 copy-start
  0.7 0.7 copy-done
  1.3 1.3 collective-permute-start
  2.7 1.3 pad_maximum_fusion.1.refs_1_
  4.1 0.1 multiply_exponential_fusion
  4.2 2.4 dynamic-slice_bitcast_fusion
  6.6 0.6 multiply_cosine_fusion
  7.2 0.8 pad_maximum_fusion.refs_2_
  8.0 0.0 copy-done.4
  8.0 1.4 copy.27
  9.5 0.0 copy-done.5
  9.5 1.4 copy.28
  10.9 0.0 collective-permute-done
  10.9 0.2 compare_and_fusion
  11.1 1.1 select_multiply_fusion.refs_3_
  12.1 370.1 %forward_layer.2 = (bf16[2,4,2,256,3072]{4,3,2,1,0:T(8,128)(2,1)}, bf16[2,4,2,256,1024]{4,3,2,1,0:T(8,128)(2,1)}, bf16[2,4,2,256,2048]{4,3,2,1,0:T(8,128)(2,1)},...) custom-call(bf16[128,2048]{1,0:T(8,128)(2,1)} %get-tuple-element.133, ...), custom_call_target="tpu_custom_call" | custom-call | tf_op jit(solution)/shard_map/forward_layer/pallas_call | solution.py:596
  382.3 78.8 %forward_layer.3 = (f32[128,2048]{1,0:T(8,128)}, bf16[2048,512]{1,0:T(8,128)(2,1)}, bf16[2,256,512]{2,1,0:T(8,128)(2,1)}, bf16[2,256,512]{2,1,0:T(8,128)(2,1)}, ...) custom-call(bf16[128,2048]{1,0:T(8,128)(2,1)} %get-tuple-element.58., ...), custom_call_target="tpu_custom_call" | custom-call | tf_op jit(solution)/shard_map/forward_layer/pallas_call | solution.py:596
  461.1 122.0 %backward_layer.2 = (bf16[128,2048]{1,0:T(8,128)(2,1)}, bf16[5,4,256,1024]{3,2,1,0:T(8,128)(2,1)}, bf16[5,4,256,1024]{3,2,1,0:T(8,128)(2,1)}, f32[2,2048]{1,0:T(...) custom-call(bf16[128,2048]{1,0:T(8,128)(2,1)} %get-tuple-element.132.refs_4_.refs_0_, ...), custom_call_target="tpu_custom_call" | custom-call | tf_op jit(solution)/shard_map/backward_layer/pallas_call | solution.py:1263
  583.1 440.4 %backward_layer.3 = (bf16[128,2048]{1,0:T(8,128)(2,1)}, bf16[9,4,256,1024]{3,2,1,0:T(8,128)(2,1)}, bf16[9,4,256,1024]{3,2,1,0:T(8,128)(2,1)}, bf16[7,4,256,1024]...) custom-call(bf16[128,2048]{1,0:T(8,128)(2,1)} %get-tuple-element.79., ...), custom_call_target="tpu_custom_call" | custom-call | tf_op jit(solution)/shard_map/backward_layer/pallas_call | solution.py:1263
  1023.5 2.7 slice_bitcast_fusion.1
  1026.2 11.6 %convert_reduce_fusion = (f32[256,2048]{1,0:T(8,128)}, f32[256,2048]{1,0:T(8,128)}, f32[256,2048]{1,0:T(8,128)}, f32[256,2048]{1,0:T(8,128)S(1)}, f32[256,2048]{1,0:T(8,128)}, /*index=5*/f32[256,2048]{1,0:T(8,128)}) fusion(bf16[7,2,256,2048]{3,2,1,0:T(8,128)(2,1)} %get-tuple-element.102), kind=kLoop, calls=%fused_computation | loop fusion | flops 9437184 | bytes 25165824 | tf_op jit(solution)/shard_map/reduce_sum | solution.py:1337
  1037.8 0.0 copy-done.10
  1037.8 0.6 fusion
  1038.4 2.9 copy.30
  1041.3 1.8 copy.29
  1043.1 2.6 convert_reduce_fusion.6
  1045.7 1.1 convert_reduce_fusion.7
  1046.8 0.0 copy-done.8
  1046.8 1.1 maximum_select_fusion
  1047.9 0.0 copy-done.6
  1047.9 1.1 maximum_select_fusion.1
  1049.1 0.0 copy-done.1
  (23 shorter events, 0.1 us)
Async XLA Ops:
  0.6 0.7 copy-start
  1.3 9.5 collective-permute-start
  4.1 3.9 copy-start.4
  6.6 2.9 copy-start.5
  1026.2 11.6 %copy-start.10 = (f32[2,2048]{1,0:T(2,128)S(1)}, f32[2,2048]{1,0:T(2,128)}, u32[]{:S(2)}) copy-start(f32[2,2048]{1,0:T(2,128)} %get-tuple-element.103) | copy-start | bytes 49156
  1043.1 3.7 copy-start.2
  1043.1 3.7 copy-start.8
  1043.1 3.7 copy-start.9
  1045.6 2.3 copy-start.3
  1045.7 2.3 copy-start.6
  1045.7 2.3 copy-start.7
  1046.8 2.3 copy-start.1

commit v5 on v4

--- a/solution.py
+++ b/solution.py
@@ -180,10 +180,13 @@
     else:
         (v.x, v.gains, v.tables, v.masks, *refs) = refs
         stored, refs = refs[:4], refs[4:]
-    (middle, normed_in_t, query_rot, key_rot, value, unit, inverse, opened, slope_open, merged, normed_mid_t, act, slope,
-     hidden, *refs) = refs
+    saved, refs = refs[:14], refs[14:]
     if streams:
         (v.grad_down, result, *refs) = refs
+    scratch, refs = refs[:14], refs[14:]
+    (middle, normed_in_t, query_rot, key_rot, value, unit, inverse, opened, slope_open, merged, normed_mid_t, act, slope,
+     hidden) = scratch
+    save_sem, x_v, masks, tables, in_sem, *refs = refs
     held, refs = refs[:4], refs[4:]
     (w_sem, normed_in, *refs) = refs
     if streams:
@@ -191,10 +194,25 @@
     else:
         normed_mid = normed_mid_t
     (parts, landed, s_send, s_recv, g_send, g_recv, *refs) = refs
-    x, tables, masks = v.x, v.tables, v.masks
+    x = x_v
     rows, width = x.shape
     sq = Square(dp_size, rows)
     at = sq.at
+    operand_copies = [
+        pltpu.make_async_copy(source, target, in_sem.at[i])
+        for i, (source, target) in enumerate(((v.x, x_v), (v.tables, tables), (v.masks, masks)))
+    ]
+    for copy in operand_copies:
+        copy.start()
+    operand_copies[0].wait()
+    saves = []
+
+    def save(*which):
+        for i in which:
+            copy = pltpu.make_async_copy(scratch[i], saved[i], save_sem.at[i])
+            copy.start()
+            saves.append(copy)
+
     qkvs, out_t, gate_up, down_t = held
     wide_k = query_rot.shape[-1]
     wide_v = value.shape[-1]
@@ -315,6 +333,8 @@
         row_blocks(rows, first_norm)
         sq.barrier()
         ins = sq.spread(normed_in, s_send.at[0], s_recv.at[0])
+        operand_copies[1].wait()
+        operand_copies[2].wait()
         ins[0].wait_recv()
         for i in range(4):
             project(i, sq.own)
@@ -323,6 +343,7 @@
         turn_if(at.core == at.section, normed_in_t, normed_in)
         for i in range(4):
             project(i, sq.next)
+        save(2, 3, 4, 7, 8)
         retain(sq.next)
         loads_wait(4)
         give_back(sq.next, merged, out_t)
@@ -330,18 +351,25 @@
         retain(sq.own)
         give_back(sq.own, merged, out_t)
         gives += give(0, 0)
+        save(5, 6, 9)
         turn_if(at.core != at.section, normed_in_t, normed_in)
+        save(1)
         for push in gives:
             push.wait_recv()
         row_blocks(rows, second_norm)
+        save(0)
         mids = sq.spread(normed_mid, s_send.at[1], s_recv.at[1])
         mids[0].wait_recv()
         feed(sq.own)
         mids[1].wait_recv()
         mids[2].wait_recv()
+        save(10)
         feed(sq.next)
+        save(11, 12, 13)
         for push in ins + mids + gives:
             push.wait_send()
+        for copy in saves:
+            copy.wait()
         return
 
     (z_send, z_recv, x_send, x_recv, c_send, c_recv, o_send, o_recv, here_sem, gain_send, gain_recv, d_send, d_recv,
@@ -440,9 +468,10 @@
     advance(1)
     for push in ins:
         push.wait_recv()
-    late = jnp.logical_and(at.section == 1, at.core == 1)
-    early = jnp.logical_not(late)
-    turn_if(early, normed_in_t, normed_in)
+    transpose_into(normed_in_t, normed_in)
+    save(1)
+    operand_copies[1].wait()
+    operand_copies[2].wait()
     for i in range(2, 5):
         advance(i)
         for s in (sq.own, sq.next):
@@ -465,9 +494,11 @@
     advance(7)
     for push in mids:
         push.wait_recv()
-    turn_if(early, normed_mid_t, normed_mid)
+    transpose_into(normed_mid_t, normed_mid)
+    save(0, 2, 3, 4, 5, 6, 7, 8, 9, 10)
     feed(sq.next)
     feed(sq.own)
+    save(11, 12, 13)
     for push in gives:
         push.wait_send()
 
@@ -485,8 +516,6 @@
 
     arrive(7)
     loads_wait(7)
-    turn_if(late, normed_in_t, normed_in)
-    turn_if(late, normed_mid_t, normed_mid)
     give_back(sq.next, hidden, down_t)
     ends = give(1, 1)
     give_back(sq.own, hidden, down_t)
@@ -522,6 +551,8 @@
         core_own[i].wait_send()
         core_other[i].wait_send()
     gain_copy.wait_send()
+    for copy in saves:
+        copy.wait()
 
 
 def forward_layer(layer, x, gains, tables, masks, weights, dp_size, out_grad=None):
@@ -558,8 +589,10 @@
         tokens(quarter_f),
         tokens(quarter_f),
     ]
-    out_specs = [vmem] * len(out_shape)
-    scratch = [pltpu.VMEM((slices, 2, width // dp_size, wide), bf16) for wide in wides] + [
+    out_specs = [any_spec] * len(out_shape)
+    scratch = [pltpu.VMEM(out.shape, out.dtype) for out in out_shape]
+    scratch += [dma((14,))] + [pltpu.VMEM(a.shape, a.dtype) for a in (x, masks, tables)] + [dma((3,))]
+    scratch += [pltpu.VMEM((slices, 2, width // dp_size, wide), bf16) for wide in wides] + [
         dma((8,)),
     ] + [pltpu.VMEM((2, length, width), bf16)] * (3 if streams else 2) + [
         pltpu.VMEM((2, 3, rows, width), bf16),
@@ -596,7 +629,7 @@
     return pl.pallas_call(
         functools.partial(forward_kernel, dp_size, layer),
         out_shape=out_shape,
-        in_specs=[vmem] * len(operands) + [any_spec] * len(weights),
+        in_specs=[any_spec, vmem, any_spec, any_spec] + [vmem] * (len(operands) - 4) + [any_spec] * len(weights),
         out_specs=out_specs,
         scratch_shapes=scratch,
         compiler_params=pltpu.CompilerParams(
@@ -631,7 +664,7 @@
     (v.big, v.out_t, v.query_v, v.key_v, v.value_v, v.wide_a, v.wide_b, v.wide_c, v.inverse_v, v.x_v, v.middle_v,
      v.normed_t, v.outer, v.grad_down, v.grad_gate_up, v.grad_branch, v.grad_qkvs, v.turned, v.parts, v.landed,
      v.grad_middle, v.stage_given, v.stage_own, v.core_part, v.load_sem, v.s_send, v.s_recv, v.g_send, v.g_recv,
-     v.c_send, v.c_recv, v.local_sem, *refs) = refs
+     v.c_send, v.c_recv, v.local_sem, v.masks_v, v.tables_v, v.grad_out_v, *refs) = refs
     if final_layer:
         (v.left, v.right, v.sums, v.r_sem, v.x_send, v.x_recv, v.z_send, v.z_recv, v.terms, v.held, v.hop_land,
          v.t_send, v.t_recv, v.row_send, v.row_recv, v.landed_y) = refs
@@ -640,7 +673,7 @@
     at = Place(dp_size)
     rows, width = v.x.shape
     sq = Square(dp_size, rows)
-    masks, tables, gains = v.masks, v.tables, v.gains
+    masks, tables, gains = v.masks_v, v.tables_v, v.gains
     query_v, key_v, value_v = v.query_v, v.key_v, v.value_v
     wide_a, wide_b, wide_c = v.wide_a, v.wide_b, v.wide_c
     grad_down, grad_gate_up, grad_branch, grad_qkvs = v.grad_down, v.grad_gate_up, v.grad_branch, v.grad_qkvs
@@ -693,6 +726,9 @@
         load(11, v.value, value_v),
         load(12, v.inverse, v.inverse_v),
         load(13, v.opened, wide_c),
+        load(15, v.masks, masks),
+        load(16, v.tables, tables),
+        load(17, v.grad_out, v.grad_out_v),
     ]
     terms[...] = jnp.zeros_like(terms)
 
@@ -917,11 +953,6 @@
     slope_load.wait()
     through_down(sq.next)
     through_down(sq.own)
-    if final_layer:
-        fetch(0)
-        own(0)
-        mid_load.wait()
-        settle(0)
     unit_load = load(1, v.unit, wide_a)
     bend_load = load(2, v.slope_open, wide_b)
     gate_load.wait()
@@ -930,11 +961,12 @@
         hidden_load.wait()
         transpose_into(v.turned, grad_down)
         given(0)
-        fetch(0)
-        own(0)
-        mid_load.wait()
+    fetch(0)
+    own(0)
+    mid_load.wait()
+    if not final_layer:
         transpose_into(v.normed_t, v.mid_v)
-        settle(0)
+    settle(0)
     given(1)
     qkvs_load = load(3, v.qkvs_all.at[layer], big)
     merged_load = load(4, v.merged, outer)
@@ -946,7 +978,7 @@
     def through_mid(block):
         upstream = collected(block, parts, landed)
         normed, scale = norm_parts(v.middle_v[block])
-        grad_rows = v.grad_out[block].astype(f32) + norm_grad(normed, scale, upstream, gain_mid)
+        grad_rows = v.grad_out_v[block].astype(f32) + norm_grad(normed, scale, upstream, gain_mid)
         v.grad_middle[block] = grad_rows
         sq.chunk(grad_branch)[block] = grad_rows.astype(bf16)
         terms[1:2] = terms[1:2] + jnp.sum(upstream * normed, axis=0, keepdims=True)
@@ -1190,7 +1222,7 @@
     operands += [x, middle, normed_in_t, query_rot, key_rot, value, unit, inverse, opened, slope_open, merged, normed_mid_t,
                  act, slope, hidden]
     operands += [*gathered, down]
-    in_specs = [vmem] * 4 + [any_spec] * (len(operands) - 4)
+    in_specs = [any_spec, vmem] + [any_spec] * (len(operands) - 2)
     count = 2 * GROUPS - KEPT if final_layer else KEPT
     out_shape = [stored(rows, width), stored(count, *block), stored(count, *block)]
     out_specs = [vmem, any_spec, any_spec]
@@ -1229,7 +1261,7 @@
         held(2, *block),
         held(*block),
         held(*block),
-        dma((15,)),
+        dma((18,)),
         dma((3,)),
         dma((3,)),
         dma((3, 3)),
@@ -1237,6 +1269,9 @@
         dma((count,)),
         dma((count,)),
         dma((2,)),
+        held(*masks.shape, kind=f32),
+        held(*tables.shape, kind=f32),
+        held(rows, width),
     ]
     if final_layer:
         hops = 3 + dp_size // 4

time: 1050 us -> 1040 us (level); the launches traced: 1050 us -> 1030 us
  Pallas kernels: 1010 us -> 990 us
    pallas_call x2, Pallas kernels: 562 us -> 551 us  [backward_layer(): pl.pallas_call(functools.partial(backward_kernel, dp_size, layer), out_sh...]
where the time goes in v5:
time: 1040 us; the launch traced here: 1030 us
  Pallas kernels  990 us (95%)
  other arithmetic  21.7 us (2%)
  local copies, waits for them, and re-layouts  13.9 us (1%)
    pallas_call x2, Pallas kernels, backward_layer(): pl.pallas_call(functools.partial(backward_kernel, dp_size, layer), out_sh...  551 us
    pallas_call x2, Pallas kernels, forward_layer(): pl.pallas_call(functools.partial(forward_kernel, dp_size, layer), out_sha...  438 us
  transfers between devices with their start and end apart: 1, of which 0 were waited for; matrix products, arithmetic and copies ran while one was open for 1% of the time, Pallas kernels for 0%

profile of v5, /device:TPU:5, one launch (start us, length us, event | category | flops | bytes accessed | tf_op | source)
XLA Modules:
  0.0 1027.8 jit_solution(10323348870462527105)
XLA Ops:
  0.6 0.0 copy-start
  0.7 0.7 copy-done
  1.3 1.3 collective-permute-start
  2.7 1.3 pad_maximum_fusion.1.refs_1_
  4.1 0.1 multiply_exponential_fusion
  4.2 2.4 dynamic-slice_bitcast_fusion
  6.6 0.6 multiply_cosine_fusion
  7.2 0.8 pad_maximum_fusion.refs_2_
  8.0 0.0 copy-done.4
  8.0 1.4 copy.27
  9.5 0.0 copy-done.5
  9.5 1.4 copy.28
  10.9 0.0 collective-permute-done
  10.9 0.2 compare_and_fusion
  11.1 1.1 select_multiply_fusion.refs_3_
  12.1 366.7 %forward_layer.2 = (bf16[2,4,2,256,3072]{4,3,2,1,0:T(8,128)(2,1)}, bf16[2,4,2,256,1024]{4,3,2,1,0:T(8,128)(2,1)}, bf16[2,4,2,256,2048]{4,3,2,1,0:T(8,128)(2,1)},...) custom-call(bf16[128,2048]{1,0:T(8,128)(2,1)} %get-tuple-element.133, ...), custom_call_target="tpu_custom_call" | custom-call | tf_op jit(solution)/shard_map/forward_layer/pallas_call | solution.py:629
  378.8 71.8 %forward_layer.3 = (f32[128,2048]{1,0:T(8,128)}, bf16[2048,512]{1,0:T(8,128)(2,1)}, bf16[2,256,512]{2,1,0:T(8,128)(2,1)}, bf16[2,256,512]{2,1,0:T(8,128)(2,1)}, ...) custom-call(bf16[128,2048]{1,0:T(8,128)(2,1)} %get-tuple-element.58., ...), custom_call_target="tpu_custom_call" | custom-call | tf_op jit(solution)/shard_map/forward_layer/pallas_call | solution.py:629
  450.6 123.0 %backward_layer.2 = (bf16[128,2048]{1,0:T(8,128)(2,1)}, bf16[5,4,256,1024]{3,2,1,0:T(8,128)(2,1)}, bf16[5,4,256,1024]{3,2,1,0:T(8,128)(2,1)}, f32[2,2048]{1,0:T(...) custom-call(bf16[128,2048]{1,0:T(8,128)(2,1)} %get-tuple-element.132.refs_4_.refs_0_, ...), custom_call_target="tpu_custom_call" | custom-call | tf_op jit(solution)/shard_map/backward_layer/pallas_call | solution.py:1298
  573.6 428.1 %backward_layer.3 = (bf16[128,2048]{1,0:T(8,128)(2,1)}, bf16[9,4,256,1024]{3,2,1,0:T(8,128)(2,1)}, bf16[9,4,256,1024]{3,2,1,0:T(8,128)(2,1)}, bf16[7,4,256,1024]...) custom-call(bf16[128,2048]{1,0:T(8,128)(2,1)} %get-tuple-element.79., ...), custom_call_target="tpu_custom_call" | custom-call | tf_op jit(solution)/shard_map/backward_layer/pallas_call | solution.py:1298
  1001.8 2.7 slice_bitcast_fusion.1
  1004.5 11.6 %convert_reduce_fusion = (f32[256,2048]{1,0:T(8,128)}, f32[256,2048]{1,0:T(8,128)}, f32[256,2048]{1,0:T(8,128)}, f32[256,2048]{1,0:T(8,128)S(1)}, f32[256,2048]{1,0:T(8,128)}, /*index=5*/f32[256,2048]{1,0:T(8,128)}) fusion(bf16[7,2,256,2048]{3,2,1,0:T(8,128)(2,1)} %get-tuple-element.102), kind=kLoop, calls=%fused_computation | loop fusion | flops 9437184 | bytes 25165824 | tf_op jit(solution)/shard_map/reduce_sum | solution.py:1372
  1016.0 0.0 copy-done.10
  1016.0 0.6 fusion
  1016.7 2.9 copy.30
  1019.5 1.8 copy.29
  1021.4 2.6 convert_reduce_fusion.6
  1023.9 1.1 convert_reduce_fusion.7
  1025.1 0.0 copy-done.2
  1025.1 0.0 copy-done.9
  1025.1 1.1 maximum_select_fusion
  1026.2 0.0 copy-done.7
  1026.2 1.1 maximum_select_fusion.1
  (23 shorter events, 0.1 us)
Async XLA Ops:
  0.6 0.7 copy-start
  1.3 9.5 collective-permute-start
  4.1 3.9 copy-start.4
  6.6 2.9 copy-start.5
  1004.5 11.6 %copy-start.10 = (f32[2,2048]{1,0:T(2,128)S(1)}, f32[2,2048]{1,0:T(2,128)}, u32[]{:S(2)}) copy-start(f32[2,2048]{1,0:T(2,128)} %get-tuple-element.103) | copy-start | bytes 49156
  1021.3 3.7 copy-start.2
  1021.3 3.7 copy-start.8
  1021.4 3.7 copy-start.9
  1023.9 2.3 copy-start.3
  1023.9 2.3 copy-start.6
  1023.9 2.3 copy-start.7
  1025.1 2.3 copy-start.1

commit v6 on v5

--- a/solution.py
+++ b/solution.py
@@ -24,18 +24,6 @@
     zeta = (pair_index / half_width + 0.4) / 1.4
     growth = jnp.exp(position / 512.0 * jnp.log(zeta))
     return (jnp.cos(angle), jnp.sin(angle), growth)
-
-
-def decay_mask(segments, first_head, heads):
-    length = segments.shape[-1]
-    position = jnp.arange(length)
-    earlier = position[:, None] >= position[None, :]
-    same_doc = (segments[:, :, None] == segments[:, None, :]) & earlier[None]
-    distance = jnp.maximum(position[:, None] - position[None, :], 0).astype(f32)
-    head_index = (first_head + jnp.arange(heads)).astype(f32)
-    log_rate = jnp.log(1.0 - jnp.exp2(-5.0 - head_index))
-    decay = jnp.exp(log_rate[:, None, None] * distance[None])
-    return jnp.where(same_doc[:, None], decay[None], 0.0)
 
 
 class Place:
@@ -173,16 +161,18 @@
     streams = layer == 0
     v = Refs()
     if streams:
-        (v.x, v.own_gains, v.tables, v.masks, v.out_grad, *refs) = refs
+        (v.x, v.mixer_gain, v.ffn_gain, v.ids, v.tables, v.out_grad, *refs) = refs
         shards, refs = refs[:8], refs[8:]
         stored, refs = refs[:4], refs[4:]
-        (v.gains, *refs) = refs
+        (v.gains, v.masks, *refs) = refs
     else:
-        (v.x, v.gains, v.tables, v.masks, *refs) = refs
+        (v.x, v.gains, v.tables, v.masks, v.down, *refs) = refs
         stored, refs = refs[:4], refs[4:]
     saved, refs = refs[:14], refs[14:]
     if streams:
         (v.grad_down, result, *refs) = refs
+    else:
+        (v.turned_down, *refs) = refs
     scratch, refs = refs[:14], refs[14:]
     (middle, normed_in_t, query_rot, key_rot, value, unit, inverse, opened, slope_open, merged, normed_mid_t, act, slope,
      hidden) = scratch
@@ -198,9 +188,11 @@
     rows, width = x.shape
     sq = Square(dp_size, rows)
     at = sq.at
+    sources = [(v.x.at[at.section] if streams else v.x, x_v), (v.tables, tables)]
+    if not streams:
+        sources.append((v.masks, masks))
     operand_copies = [
-        pltpu.make_async_copy(source, target, in_sem.at[i])
-        for i, (source, target) in enumerate(((v.x, x_v), (v.tables, tables), (v.masks, masks)))
+        pltpu.make_async_copy(source, target, in_sem.at[i]) for i, (source, target) in enumerate(sources)
     ]
     for copy in operand_copies:
         copy.start()
@@ -328,8 +320,21 @@
             transpose_into(target, source)
 
     if not streams:
+        (down_v, turned_v, down_sem) = refs
+        down_load = pltpu.make_async_copy(v.down, down_v, down_sem.at[0])
+        down_load.start()
+        down_save = pltpu.make_async_copy(turned_v, v.turned_down, down_sem.at[1])
+
+        def turn_down(condition):
+            @pl.when(condition)
+            def _():
+                down_load.wait()
+                transpose_into(turned_v, down_v)
+                down_save.start()
+
         for i in range(7):
             load(i)
+        turn_down(at.core == at.section)
         row_blocks(rows, first_norm)
         sq.barrier()
         ins = sq.spread(normed_in, s_send.at[0], s_recv.at[0])
@@ -354,6 +359,7 @@
         save(5, 6, 9)
         turn_if(at.core != at.section, normed_in_t, normed_in)
         save(1)
+        turn_down(at.core != at.section)
         for push in gives:
             push.wait_recv()
         row_blocks(rows, second_norm)
@@ -370,10 +376,11 @@
             push.wait_send()
         for copy in saves:
             copy.wait()
+        down_save.wait()
         return
 
     (z_send, z_recv, x_send, x_recv, c_send, c_recv, o_send, o_recv, here_sem, gain_send, gain_recv, d_send, d_recv,
-     d_sem) = refs
+     d_sem, own_gains, ids_land, id_send, id_recv, mask_sem) = refs
     steps = [(k, b) for k in range(at.groups) for b in range(2)][1:]
 
     def place(section=None, dp=None):
@@ -391,9 +398,32 @@
         pl.semaphore_signal(barrier, inc=1, device_id=partner, device_id_type=MESH)
     pl.semaphore_wait(barrier, len(partners))
 
-    gain_copy = copy(v.own_gains, v.gains.at[at.section], gain_send, gain_recv, place(section=other))
+    own_gains[0:1] = v.mixer_gain[...]
+    own_gains[1:2] = v.ffn_gain[...]
+    gain_copy = copy(own_gains, v.gains.at[at.section], gain_send, gain_recv, place(section=other))
     gain_copy.start()
-    v.gains[at.section] = v.own_gains[...]
+    v.gains[at.section] = own_gains[...]
+    id_copy = copy(v.ids, ids_land, id_send, id_recv, sq.device(1, 0))
+    id_copy.start()
+
+    def make_masks():
+        length = masks.shape[-1]
+        t = lax.broadcasted_iota(jnp.int32, (length, length), 0).astype(f32)
+        s = lax.broadcasted_iota(jnp.int32, (length, length), 1).astype(f32)
+        distance = jnp.maximum(t - s, 0.0)
+        decays = []
+        for head in range(heads):
+            number = jnp.full((1, 1), ((at.tensor * 2 + at.low) * heads + head).astype(f32))
+            rate = jnp.log(1.0 - jnp.exp2(-5.0 - number))
+            decays.append(jnp.exp(rate * distance) * HEAD_K ** (-0.5))
+        for sequence, ids in ((sq.own, v.ids), (sq.next, ids_land)):
+            row = ids[pl.ds(at.section, 1), :]
+            same = t >= s
+            for document in (1, 2):
+                start = jnp.sum(jnp.where(row < document, 1.0, 0.0), axis=1, keepdims=True)
+                same = jnp.logical_and(same, (t >= start) == (s >= start))
+            for head in range(heads):
+                masks[sequence, head] = jnp.where(same, decays[head], 0.0)
 
     def slot(i, section, dp):
         which, first, size = groups[i]
@@ -464,14 +494,17 @@
             arrive(i - 1)
 
     advance(0)
-    downs = sq.spread_from(v.out_grad, v.grad_down, d_send, d_recv, d_sem)
+    downs = sq.spread_from(v.out_grad.at[at.section], v.grad_down, d_send, d_recv, d_sem)
+    id_copy.wait_recv()
+    make_masks()
+    mask_save = pltpu.make_async_copy(masks, v.masks, mask_sem)
+    mask_save.start()
     advance(1)
     for push in ins:
         push.wait_recv()
     transpose_into(normed_in_t, normed_in)
     save(1)
     operand_copies[1].wait()
-    operand_copies[2].wait()
     for i in range(2, 5):
         advance(i)
         for s in (sq.own, sq.next):
@@ -551,14 +584,14 @@
         core_own[i].wait_send()
         core_other[i].wait_send()
     gain_copy.wait_send()
+    id_copy.wait_send()
+    mask_save.wait()
     for copy in saves:
         copy.wait()
 
 
-def forward_layer(layer, x, gains, tables, masks, weights, dp_size, out_grad=None):
-    rows, width = x.shape
-    length = masks.shape[-1]
-    heads = masks.shape[1]
+def forward_layer(layer, operands, weights, length, heads, dp_size):
+    rows, width = operands[0].shape[-2:]
     streams = layer == 0
     slices = dp_size // 2
     quarter_k = heads * HEAD_K
@@ -591,7 +624,14 @@
     ]
     out_specs = [any_spec] * len(out_shape)
     scratch = [pltpu.VMEM(out.shape, out.dtype) for out in out_shape]
-    scratch += [dma((14,))] + [pltpu.VMEM(a.shape, a.dtype) for a in (x, masks, tables)] + [dma((3,))]
+    mask_shape = (2, heads, length, length)
+    scratch += [
+        dma((14,)),
+        pltpu.VMEM((rows, width), bf16),
+        pltpu.VMEM(mask_shape, f32),
+        pltpu.VMEM((4, length, HEAD_K // 2), f32),
+        dma((3,)),
+    ]
     scratch += [pltpu.VMEM((slices, 2, width // dp_size, wide), bf16) for wide in wides] + [
         dma((8,)),
     ] + [pltpu.VMEM((2, length, width), bf16)] * (3 if streams else 2) + [
@@ -604,11 +644,11 @@
     if streams:
         out_shape = (
             [jax.ShapeDtypeStruct((2, slices, 2, width // dp_size, wide), bf16) for wide in wides]
-            + [jax.ShapeDtypeStruct((2,) + gains.shape, f32)]
+            + [jax.ShapeDtypeStruct((2, 2, width), f32), jax.ShapeDtypeStruct(mask_shape, f32)]
             + out_shape
             + [tokens(width), jax.ShapeDtypeStruct((rows, width), bf16)]
         )
-        out_specs = [any_spec] * 4 + [vmem] + out_specs + [any_spec, vmem]
+        out_specs = [any_spec] * 4 + [vmem, any_spec] + out_specs + [any_spec, vmem]
         scratch += [
             dma((8, slices - 1)),
             dma((8, slices - 1)),
@@ -624,12 +664,22 @@
             dma((3,)),
             dma((3,)),
             dma,
+            pltpu.VMEM((2, width), f32),
+            pltpu.VMEM((2, length), jnp.int32),
+            dma,
+            dma,
+            dma,
         ]
-    operands = [x, gains, tables, masks] + ([out_grad] if streams else [])
+        in_specs = [any_spec, vmem, vmem, vmem, any_spec, any_spec]
+    else:
+        out_shape = out_shape + [turned]
+        out_specs = out_specs + [any_spec]
+        scratch += [pltpu.VMEM((2, length, width), bf16), pltpu.VMEM(turned.shape, bf16), dma((2,))]
+        in_specs = [any_spec, vmem, any_spec, any_spec, any_spec]
     return pl.pallas_call(
         functools.partial(forward_kernel, dp_size, layer),
         out_shape=out_shape,
-        in_specs=[any_spec, vmem, any_spec, any_spec] + [vmem] * (len(operands) - 4) + [any_spec] * len(weights),
+        in_specs=in_specs + [any_spec] * len(weights),
         out_specs=out_specs,
         scratch_shapes=scratch,
         compiler_params=pltpu.CompilerParams(
@@ -653,6 +703,8 @@
     (v.grad_out, v.gains, v.tables, v.masks, v.x, v.middle, v.normed_in_t, v.query_rot, v.key_rot, v.value, v.unit,
      v.inverse, v.opened, v.slope_open, v.merged, v.normed_mid_t, v.act, v.slope, v.hidden,
      v.qkvs_all, v.out_all, v.gate_up_all, v.down_all, v.down_in, *refs) = refs
+    if not final_layer:
+        v.down_turned, *refs = refs
     if final_layer:
         (v.later_chip, v.later_terms, v.first_rows, v.later_normed_in_t, v.later_qkvs, v.later_hidden, v.later_middle,
          *refs) = refs
@@ -671,7 +723,7 @@
     else:
         v.d_send, v.d_recv, v.d_sem, v.kept_sem, v.mid_v = refs
     at = Place(dp_size)
-    rows, width = v.x.shape
+    rows, width = v.x.shape[-2:]
     sq = Square(dp_size, rows)
     masks, tables, gains = v.masks_v, v.tables_v, v.gains
     query_v, key_v, value_v = v.query_v, v.key_v, v.value_v
@@ -716,10 +768,12 @@
     slope_load = load(2, v.slope, wide_b)
     gate_load = load(3, v.gate_up_all.at[layer], big.at[:, pl.ds(0, 2 * wide_f)])
     hidden_load = load(4, v.hidden, outer)
+    if not final_layer:
+        turned_load = load(18, v.down_turned, v.turned)
     mid_load = load(5, v.normed_mid_t, v.normed_t if final_layer else v.mid_v)
     early = [
         load(6, v.middle, v.middle_v),
-        load(7, v.x, v.x_v),
+        load(7, v.x.at[at.section] if final_layer else v.x, v.x_v),
         load(8, v.out_all.at[layer], out_t),
         load(9, v.query_rot, query_v),
         load(10, v.key_rot, key_v),
@@ -728,7 +782,7 @@
         load(13, v.opened, wide_c),
         load(15, v.masks, masks),
         load(16, v.tables, tables),
-        load(17, v.grad_out, v.grad_out_v),
+        load(17, v.grad_out if final_layer else v.grad_out.at[at.section], v.grad_out_v),
     ]
     terms[...] = jnp.zeros_like(terms)
 
@@ -959,7 +1013,7 @@
     gives = exchange(grad_gate_up, big, 0, 2 * wide_f, parts, landed, 0)
     if not final_layer:
         hidden_load.wait()
-        transpose_into(v.turned, grad_down)
+        turned_load.wait()
         given(0)
     fetch(0)
     own(0)
@@ -1197,8 +1251,8 @@
             x_copy(e, e, j, v.chip).wait_send()
 
 
-def backward_layer(layer, grad_out, down, x, gains, tables, masks, saved, gathered, dp_size, later=None, x_out=None):
-    rows, width = x.shape
+def backward_layer(layer, grad_out, down, turned_down, x, gains, tables, masks, saved, gathered, dp_size, later=None, x_out=None):
+    rows, width = x.shape[-2:]
     length = masks.shape[-1]
     (middle, normed_in_t, query_rot, key_rot, value, unit, inverse, opened, slope_open, merged, normed_mid_t, act, slope,
      hidden) = saved
@@ -1222,6 +1276,8 @@
     operands += [x, middle, normed_in_t, query_rot, key_rot, value, unit, inverse, opened, slope_open, merged, normed_mid_t,
                  act, slope, hidden]
     operands += [*gathered, down]
+    if not final_layer:
+        operands += [turned_down]
     in_specs = [any_spec, vmem] + [any_spec] * (len(operands) - 2)
     count = 2 * GROUPS - KEPT if final_layer else KEPT
     out_shape = [stored(rows, width), stored(count, *block), stored(count, *block)]
@@ -1261,7 +1317,7 @@
         held(2, *block),
         held(*block),
         held(*block),
-        dma((18,)),
+        dma((19,)),
         dma((3,)),
         dma((3,)),
         dma((3, 3)),
@@ -1309,7 +1365,7 @@
 
 
 def nested(outs):
-    return (*outs[:5], outs[5:-2], *outs[-2:])
+    return (*outs[:6], outs[6:-2], *outs[-2:])
 
 
 def on_device(
@@ -1330,38 +1386,29 @@
 ):
     at = Place(dp_size)
     section_first = at.section == 0
-    rows_here, width = layer_input.shape[1:]
+    width = layer_input.shape[2]
     length = segment_ids.shape[1]
-    score_scale = HEAD_K ** (-0.5)
-
     quarter_k = query_weight.shape[2] // 2
-    quarter_v = value_weight.shape[2] // 2
-    quarter_f = gate_weight.shape[2] // 2
     heads_here = quarter_k // HEAD_K
-    first_head = (at.tensor * 2 + at.low) * heads_here
     cosine, sine, growth = rotation_tables(length, HEAD_K // 2)
-
-    ids_mine = lax.dynamic_index_in_dim(segment_ids, at.section, 0, keepdims=False)
-    ids_pair = lax.ppermute(ids_mine, "dp", [(i, i ^ 2) for i in range(dp_size)])
-    ids = jnp.where(at.low == 0, jnp.stack([ids_mine, ids_pair]), jnp.stack([ids_pair, ids_mine]))
-    masks = decay_mask(ids, first_head, heads_here) * score_scale
     tables = jnp.stack([cosine, sine, growth, 1.0 / growth])
 
-    first_in = lax.dynamic_index_in_dim(layer_input, at.section, 0, keepdims=False)
-    out_grad = lax.dynamic_index_in_dim(output_grad, at.section, 0, keepdims=False)
     shards = (query_weight[0], key_weight[0], value_weight[0], swish_weight[0], output_weight[0].T, gate_weight[0],
               up_weight[0], down_weight[0].T)
-    own_gains = jnp.concatenate([mixer_gain, ffn_gain], axis=0)
-    *gathered, all_gains, first_saved, second_down, first_sent = nested(
-        forward_layer(0, first_in, own_gains, tables, masks, shards, dp_size, out_grad)
+    *gathered, all_gains, masks, first_saved, second_down, first_sent = nested(
+        forward_layer(
+            0, (layer_input, mixer_gain, ffn_gain, segment_ids, tables, output_grad), shards, length, heads_here, dp_size
+        )
     )
-    second_saved = forward_layer(1, first_sent, all_gains, tables, masks, gathered, dp_size)
+    *second_saved, turned_down = forward_layer(
+        1, (first_sent, all_gains, tables, masks, second_down), gathered, length, heads_here, dp_size
+    )
     gathered = [g.reshape(2, width, g.shape[-1]) for g in gathered]
     second_grad, later_chip, _, later_terms, first_down, later_qkvs = backward_layer(
-        1, out_grad, second_down, first_sent, all_gains, tables, masks, second_saved, gathered, dp_size
+        1, output_grad, second_down, turned_down, first_sent, all_gains, tables, masks, second_saved, gathered, dp_size
     )
     first_grad, _, _, _, landed, my_gains, second_sent, taken_rows, taken_grads = backward_layer(
-        0, second_grad, first_down, first_in, all_gains, tables, masks, first_saved, gathered, dp_size,
+        0, second_grad, first_down, None, layer_input, all_gains, tables, masks, first_saved, gathered, dp_size,
         (later_chip, later_terms, later_qkvs, second_saved), first_sent,
     )
 

time: 1040 us -> 1030 us (level)
  transfers between devices with their start and end apart: 1 -> 0, of which waited for: 0 -> 0; matrix products, arithmetic and copies ran while one was open for 1% -> 0% of each run, Pallas kernels for 0% -> 0%
where the time goes in v6:
time: 1030 us; the launch traced here: 1010 us
  Pallas kernels  986 us (96%)
  other arithmetic  17.1 us (2%)
    pallas_call x2, Pallas kernels, backward_layer(): pl.pallas_call(functools.partial(backward_kernel, dp_size, layer), out_sh...  545 us
    pallas_call x2, Pallas kernels, forward_layer(): pl.pallas_call(functools.partial(forward_kernel, dp_size, layer), out_sha...  441 us

profile of v6, /device:TPU:5, one launch (start us, length us, event | category | flops | bytes accessed | tf_op | source)
XLA Modules:
  0.0 1013.8 jit_solution(3681705107494100640)
XLA Ops:
  0.6 0.0 copy-start.2
  0.7 0.0 copy-start.3
  0.7 0.6 multiply_cosine_fusion
  1.3 0.8 pad_maximum_fusion.refs_4_.refs_2_
  2.1 0.0 copy-done.2
  2.1 1.4 copy.27
  3.5 0.0 copy-done.3
  3.5 1.4 copy.28
  4.9 367.8 %forward_layer.2 = (bf16[2,4,2,256,3072]{4,3,2,1,0:T(8,128)(2,1)}, bf16[2,4,2,256,1024]{4,3,2,1,0:T(8,128)(2,1)}, bf16[2,4,2,256,2048]{4,3,2,1,0:T(8,128)(2,1)},...) custom-call(bf16[2,128,2048]{2,1,0:T(8,128)(2,1)} %refs_4_.1, ...), custom_call_target="tpu_custom_call" | custom-call | tf_op jit(solution)/shard_map/forward_layer/pallas_call | solution.py:679
  372.8 72.7 %forward_layer.3 = (f32[128,2048]{1,0:T(8,128)}, bf16[2048,512]{1,0:T(8,128)(2,1)}, bf16[2,256,512]{2,1,0:T(8,128)(2,1)}, bf16[2,256,512]{2,1,0:T(8,128)(2,1)}, ...) custom-call(bf16[128,2048]{1,0:T(8,128)(2,1)} %get-tuple-element.60., ...), custom_call_target="tpu_custom_call" | custom-call | tf_op jit(solution)/shard_map/forward_layer/pallas_call | solution.py:679
  445.5 126.1 %backward_layer.2 = (bf16[128,2048]{1,0:T(8,128)(2,1)}, bf16[5,4,256,1024]{3,2,1,0:T(8,128)(2,1)}, bf16[5,4,256,1024]{3,2,1,0:T(8,128)(2,1)}, f32[2,2048]{1,0:T(...) custom-call(bf16[2,128,2048]{2,1,0:T(8,128)(2,1)} %refs_0_.3, ...), custom_call_target="tpu_custom_call" | custom-call | tf_op jit(solution)/shard_map/backward_layer/pallas_call | solution.py:1354
  571.6 419.1 %backward_layer.3 = (bf16[128,2048]{1,0:T(8,128)(2,1)}, bf16[9,4,256,1024]{3,2,1,0:T(8,128)(2,1)}, bf16[9,4,256,1024]{3,2,1,0:T(8,128)(2,1)}, bf16[7,4,256,1024]...) custom-call(bf16[128,2048]{1,0:T(8,128)(2,1)} %get-tuple-element.83., ...), custom_call_target="tpu_custom_call" | custom-call | tf_op jit(solution)/shard_map/backward_layer/pallas_call | solution.py:1354
  990.7 11.1 %convert_reduce_fusion = (f32[256,2048]{1,0:T(8,128)S(1)}, f32[256,2048]{1,0:T(8,128)}, f32[256,2048]{1,0:T(8,128)}, f32[256,2048]{1,0:T(8,128)}, f32[256,2048]{1,0:T(8,128)}, /*index=5*/f32[256,2048]{1,0:T(8,128)}) fusion(bf16[7,2,256,2048]{3,2,1,0:T(8,128)(2,1)} %get-tuple-element.106), kind=kLoop, calls=%fused_computation | loop fusion | flops 9437184 | bytes 25165824 | tf_op jit(solution)/shard_map/reduce_sum | solution.py:1419
  1001.8 2.9 copy.29
  1004.7 1.8 copy.30
  1006.5 1.7 slice_bitcast_fusion.1
  1008.2 0.0 copy-start.1
  1008.2 0.0 copy-start.6
  1008.2 0.0 copy-start.7
  1008.2 1.1 convert_reduce_fusion.6
  1009.3 0.0 copy-start
  1009.3 1.1 convert_reduce_fusion.7
  1010.5 0.0 copy-done.1
  1010.5 0.0 copy-done.6
  1010.5 0.0 copy-done.7
  1010.5 1.1 maximum_select_fusion.1
  1011.6 0.0 copy-done
  1011.6 0.0 copy-done.4
  1011.6 0.0 copy-done.5
  1011.6 1.1 maximum_select_fusion
  1012.8 0.0 copy-done.8
  1012.8 0.6 fusion
  (7 shorter events, 0.0 us)
Async XLA Ops:
  0.6 1.5 copy-start.2
  0.7 2.9 copy-start.3
  1008.2 2.3 copy-start.1
  1008.2 2.3 copy-start.6
  1008.2 2.3 copy-start.7
  1009.3 2.3 copy-start
  1009.3 2.3 copy-start.4
  1009.3 2.3 copy-start.5
  1010.5 2.3 copy-start.8

commit v7 on v6

--- a/solution.py
+++ b/solution.py
@@ -91,28 +91,62 @@
             device_id_type=MESH,
         )
 
-    def spread(self, ref, send, recv):
-        pushes = []
-        for j, step in enumerate(SQUARE):
-            push = self.copy(self.chunk(ref), self.chunk(ref), send.at[j], recv.at[j], step)
-            push.start()
-            pushes.append(push)
-        return pushes
-
-    def spread_from(self, own, ref, send, recv, here):
-        local = pltpu.make_async_copy(own, self.chunk(ref), here)
-        local.start()
-        pushes = [local]
-        for j, step in enumerate(SQUARE):
-            push = self.copy(own, self.chunk(ref), send.at[j], recv.at[j], step)
-            push.start()
-            pushes.append(push)
-        return pushes
+    def spread(self, ref, send, recv, own=None, here=None):
+        return Spread(self, ref, send, recv, own, here)
 
     def give(self, parts, landed, send, recv, j):
         push = self.copy(self.chunk(parts, *SQUARE[j]), landed.at[j], send.at[j], recv.at[j], SQUARE[j])
         push.start()
         return push
+
+
+class Spread:
+    def __init__(self, sq, ref, send, recv, own, here):
+        self.sq, self.ref, self.send, self.recv = sq, ref, send, recv
+        self.half = sq.rows // 2
+        source = sq.chunk(ref) if own is None else own
+        self.local = None
+        if own is not None:
+            self.local = pltpu.make_async_copy(own, sq.chunk(ref), here)
+            self.local.start()
+        beside, below = (0, 1), (1, 0)
+        self.first = [
+            self.push(source, sq.chunk(ref), half, j, step)
+            for j, (half, step) in enumerate(((0, beside), (1, below), (1, beside), (0, below)))
+        ]
+        from_beside, from_below = sq.chunk(ref, *beside), sq.chunk(ref, *below)
+        self.onward = [
+            self.push(from_beside, from_beside, 0, 4, below, start=False),
+            self.push(from_below, from_below, 1, 5, beside, start=False),
+        ]
+
+    def push(self, source, target, half, j, step, start=True):
+        block = pl.ds(half * self.half, self.half)
+        copy = self.sq.copy(source.at[block], target.at[block], self.send.at[j], self.recv.at[j], step)
+        if start:
+            copy.start()
+        return copy
+
+    def wait_own(self):
+        for came, onward in zip(self.first[:2], self.onward):
+            came.wait_recv()
+            onward.start()
+        self.first[2].wait_recv()
+
+    def wait_next(self):
+        self.first[3].wait_recv()
+        for onward in self.onward:
+            onward.wait_recv()
+
+    def wait_recv(self):
+        self.wait_own()
+        self.wait_next()
+
+    def wait_send(self):
+        for copy in self.first + self.onward:
+            copy.wait_send()
+        if self.local is not None:
+            self.local.wait()
 
 
 def row_blocks(rows, body, block=32):
@@ -314,11 +348,6 @@
             slope[s, :, cols] = (slope_gelu * up).astype(bf16)
             hidden[s, :, cols] = (gelu * up).astype(bf16)
 
-    def turn_if(condition, target, source):
-        @pl.when(condition)
-        def _():
-            transpose_into(target, source)
-
     if not streams:
         (down_v, turned_v, down_sem) = refs
         down_load = pltpu.make_async_copy(v.down, down_v, down_sem.at[0])
@@ -340,12 +369,10 @@
         ins = sq.spread(normed_in, s_send.at[0], s_recv.at[0])
         operand_copies[1].wait()
         operand_copies[2].wait()
-        ins[0].wait_recv()
+        ins.wait_own()
         for i in range(4):
             project(i, sq.own)
-        ins[1].wait_recv()
-        ins[2].wait_recv()
-        turn_if(at.core == at.section, normed_in_t, normed_in)
+        ins.wait_next()
         for i in range(4):
             project(i, sq.next)
         save(2, 3, 4, 7, 8)
@@ -357,7 +384,7 @@
         give_back(sq.own, merged, out_t)
         gives += give(0, 0)
         save(5, 6, 9)
-        turn_if(at.core != at.section, normed_in_t, normed_in)
+        transpose_into(normed_in_t, normed_in)
         save(1)
         turn_down(at.core != at.section)
         for push in gives:
@@ -365,14 +392,13 @@
         row_blocks(rows, second_norm)
         save(0)
         mids = sq.spread(normed_mid, s_send.at[1], s_recv.at[1])
-        mids[0].wait_recv()
+        mids.wait_own()
         feed(sq.own)
-        mids[1].wait_recv()
-        mids[2].wait_recv()
+        mids.wait_next()
         save(10)
         feed(sq.next)
         save(11, 12, 13)
-        for push in ins + mids + gives:
+        for push in [ins, mids] + gives:
             push.wait_send()
         for copy in saves:
             copy.wait()
@@ -494,14 +520,14 @@
             arrive(i - 1)
 
     advance(0)
-    downs = sq.spread_from(v.out_grad.at[at.section], v.grad_down, d_send, d_recv, d_sem)
+    downs = sq.spread(v.grad_down, d_send, d_recv, v.out_grad.at[at.section], d_sem)
     id_copy.wait_recv()
     make_masks()
     mask_save = pltpu.make_async_copy(masks, v.masks, mask_sem)
     mask_save.start()
+    ins.wait_recv()
     advance(1)
-    for push in ins:
-        push.wait_recv()
+    downs.wait_recv()
     transpose_into(normed_in_t, normed_in)
     save(1)
     operand_copies[1].wait()
@@ -524,9 +550,8 @@
         push.wait_recv()
     row_blocks(rows, second_norm)
     mids = sq.spread(normed_mid, s_send.at[1], s_recv.at[1])
+    mids.wait_recv()
     advance(7)
-    for push in mids:
-        push.wait_recv()
     transpose_into(normed_mid_t, normed_mid)
     save(0, 2, 3, 4, 5, 6, 7, 8, 9, 10)
     feed(sq.next)
@@ -576,9 +601,7 @@
         for i in range(8):
             core_own[i].wait_recv()
 
-    for push in downs:
-        push.wait()
-    for push in ins + mids + ends + list(z_copies.values()) + list(x_copies.values()):
+    for push in [downs, ins, mids] + ends + list(z_copies.values()) + list(x_copies.values()):
         push.wait_send()
     for i in range(8):
         core_own[i].wait_send()
@@ -636,8 +659,8 @@
         dma((8,)),
     ] + [pltpu.VMEM((2, length, width), bf16)] * (3 if streams else 2) + [
         pltpu.VMEM((2, 3, rows, width), bf16),
-        dma((2, 3)),
-        dma((2, 3)),
+        dma((2, 6)),
+        dma((2, 6)),
         dma((2, 3)),
         dma((2, 3)),
     ]
@@ -661,8 +684,8 @@
             dma((8,)),
             dma,
             dma,
-            dma((3,)),
-            dma((3,)),
+            dma((6,)),
+            dma((6,)),
             dma,
             pltpu.VMEM((2, width), f32),
             pltpu.VMEM((2, length), jnp.int32),
@@ -1081,10 +1104,9 @@
                 mm_tn(grad_product, query), tables[0], tables[1], tables[3]
             ).astype(bf16)
 
-    mids[0].wait_recv()
+    mids.wait_own()
     through_heads(sq.own)
-    mids[1].wait_recv()
-    mids[2].wait_recv()
+    mids.wait_next()
     through_heads(sq.next)
     if not final_layer:
         keep = pltpu.make_async_copy(grad_qkvs, v.kept_qkvs, v.kept_sem)
@@ -1125,18 +1147,18 @@
             remote(v.grad_in, v.taken_grads, v.row_send.at[1], v.row_recv.at[1], across).start()
 
     else:
-        downs = sq.spread_from(v.grad_in, v.next_down, v.d_send, v.d_recv, v.d_sem)
+        downs = sq.spread(v.next_down, v.d_send, v.d_recv, v.grad_in, v.d_sem)
 
     if not final_layer:
         fetch(4)
+        downs.wait_own()
         own(4)
         settle(4)
-        for push in mids + ends:
+        downs.wait_next()
+        for push in [downs, mids] + ends:
             push.wait_send()
         for e in (3, 4):
             given_copies[e].wait_send()
-        for push in downs:
-            push.wait()
         keep.wait()
         return
 
@@ -1174,7 +1196,7 @@
     own(8)
     settle(7)
     reduce_some(0, 1)
-    for push in mids + ends:
+    for push in [mids] + ends:
         push.wait_send()
     hidden_load.wait()
     down_load.wait()
@@ -1318,8 +1340,8 @@
         held(*block),
         held(*block),
         dma((19,)),
-        dma((3,)),
-        dma((3,)),
+        dma((6,)),
+        dma((6,)),
         dma((3, 3)),
         dma((3, 3)),
         dma((count,)),
@@ -1350,7 +1372,7 @@
             held(3, rows, width),
         ]
     else:
-        scratch += [dma((3,)), dma((3,)), dma, dma, held(2, length, width)]
+        scratch += [dma((6,)), dma((6,)), dma, dma, held(2, length, width)]
     return pl.pallas_call(
         functools.partial(backward_kernel, dp_size, layer),
         out_shape=out_shape,

time: 1030 us -> 1090 us (1.058)
  Pallas kernels: 986 us -> 1050 us
    pallas_call x2, Pallas kernels: 441 us -> 485 us  [forward_layer(): pl.pallas_call(functools.partial(forward_kernel, dp_size, layer), out_sha...]
    pallas_call x2, Pallas kernels: 545 us -> 564 us  [backward_layer(): pl.pallas_call(functools.partial(backward_kernel, dp_size, layer), out_sh...]
where the time goes in v7:
time: 1090 us; the launch traced here: 1080 us
  Pallas kernels  1050 us (96%)
  other arithmetic  17.1 us (2%)
    pallas_call x2, Pallas kernels, backward_layer(): pl.pallas_call(functools.partial(backward_kernel, dp_size, layer), out_sh...  564 us
    pallas_call x2, Pallas kernels, forward_layer(): pl.pallas_call(functools.partial(forward_kernel, dp_size, layer), out_sha...  485 us

profile of v7, /device:TPU:5, one launch (start us, length us, event | category | flops | bytes accessed | tf_op | source)
XLA Modules:
  0.0 1077.3 jit_solution(8086117613849290053)
XLA Ops:
  0.6 0.0 copy-start.2
  0.7 0.0 copy-start.3
  0.7 0.6 multiply_cosine_fusion
  1.3 0.8 pad_maximum_fusion.refs_4_.refs_2_
  2.1 0.0 copy-done.2
  2.1 1.4 copy.27
  3.5 0.0 copy-done.3
  3.5 1.4 copy.28
  4.9 411.3 %forward_layer.2 = (bf16[2,4,2,256,3072]{4,3,2,1,0:T(8,128)(2,1)}, bf16[2,4,2,256,1024]{4,3,2,1,0:T(8,128)(2,1)}, bf16[2,4,2,256,2048]{4,3,2,1,0:T(8,128)(2,1)},...) custom-call(bf16[2,128,2048]{2,1,0:T(8,128)(2,1)} %refs_4_.1, ...), custom_call_target="tpu_custom_call" | custom-call | tf_op jit(solution)/shard_map/forward_layer/pallas_call | solution.py:702
  416.2 74.0 %forward_layer.3 = (f32[128,2048]{1,0:T(8,128)}, bf16[2048,512]{1,0:T(8,128)(2,1)}, bf16[2,256,512]{2,1,0:T(8,128)(2,1)}, bf16[2,256,512]{2,1,0:T(8,128)(2,1)}, ...) custom-call(bf16[128,2048]{1,0:T(8,128)(2,1)} %get-tuple-element.60., ...), custom_call_target="tpu_custom_call" | custom-call | tf_op jit(solution)/shard_map/forward_layer/pallas_call | solution.py:702
  490.3 104.2 %backward_layer.2 = (bf16[128,2048]{1,0:T(8,128)(2,1)}, bf16[5,4,256,1024]{3,2,1,0:T(8,128)(2,1)}, bf16[5,4,256,1024]{3,2,1,0:T(8,128)(2,1)}, f32[2,2048]{1,0:T(...) custom-call(bf16[2,128,2048]{2,1,0:T(8,128)(2,1)} %refs_0_.3, ...), custom_call_target="tpu_custom_call" | custom-call | tf_op jit(solution)/shard_map/backward_layer/pallas_call | solution.py:1376
  594.5 459.7 %backward_layer.3 = (bf16[128,2048]{1,0:T(8,128)(2,1)}, bf16[9,4,256,1024]{3,2,1,0:T(8,128)(2,1)}, bf16[9,4,256,1024]{3,2,1,0:T(8,128)(2,1)}, bf16[7,4,256,1024]...) custom-call(bf16[128,2048]{1,0:T(8,128)(2,1)} %get-tuple-element.83., ...), custom_call_target="tpu_custom_call" | custom-call | tf_op jit(solution)/shard_map/backward_layer/pallas_call | solution.py:1376
  1054.2 11.1 %convert_reduce_fusion = (f32[256,2048]{1,0:T(8,128)S(1)}, f32[256,2048]{1,0:T(8,128)}, f32[256,2048]{1,0:T(8,128)}, f32[256,2048]{1,0:T(8,128)}, f32[256,2048]{1,0:T(8,128)}, /*index=5*/f32[256,2048]{1,0:T(8,128)}) fusion(bf16[7,2,256,2048]{3,2,1,0:T(8,128)(2,1)} %get-tuple-element.106), kind=kLoop, calls=%fused_computation | loop fusion | flops 9437184 | bytes 25165824 | tf_op jit(solution)/shard_map/reduce_sum | solution.py:1441
  1065.3 2.9 copy.29
  1068.2 1.8 copy.30
  1070.0 1.7 slice_bitcast_fusion.1
  1071.6 0.0 copy-start.1
  1071.7 0.0 copy-start.6
  1071.7 0.0 copy-start.7
  1071.7 1.1 convert_reduce_fusion.6
  1072.8 0.0 copy-start
  1072.8 1.1 convert_reduce_fusion.7
  1074.0 0.0 copy-done.1
  1074.0 0.0 copy-done.6
  1074.0 0.0 copy-done.7
  1074.0 1.1 maximum_select_fusion.1
  1075.1 0.0 copy-done
  1075.1 0.0 copy-done.4
  1075.1 0.0 copy-done.5
  1075.1 1.1 maximum_select_fusion
  1076.2 0.0 copy-done.8
  1076.2 0.6 fusion
  (7 shorter events, 0.0 us)
Async XLA Ops:
  0.6 1.5 copy-start.2
  0.7 2.9 copy-start.3
  1071.6 2.3 copy-start.1
  1071.7 2.3 copy-start.6
  1071.7 2.3 copy-start.7
  1072.8 2.3 copy-start
  1072.8 2.3 copy-start.4
  1072.8 2.3 copy-start.5
  1074.0 2.3 copy-start.8

commit v8 on v7

--- a/solution.py
+++ b/solution.py
@@ -91,8 +91,8 @@
             device_id_type=MESH,
         )
 
-    def spread(self, ref, send, recv, own=None, here=None):
-        return Spread(self, ref, send, recv, own, here)
+    def spread(self, ref, send, recv, direct, own=None, here=None):
+        return (DirectSpread if direct else Spread)(self, ref, send, recv, own, here)
 
     def give(self, parts, landed, send, recv, j):
         push = self.copy(self.chunk(parts, *SQUARE[j]), landed.at[j], send.at[j], recv.at[j], SQUARE[j])
@@ -104,11 +104,7 @@
     def __init__(self, sq, ref, send, recv, own, here):
         self.sq, self.ref, self.send, self.recv = sq, ref, send, recv
         self.half = sq.rows // 2
-        source = sq.chunk(ref) if own is None else own
-        self.local = None
-        if own is not None:
-            self.local = pltpu.make_async_copy(own, sq.chunk(ref), here)
-            self.local.start()
+        source = self.source(own, here)
         beside, below = (0, 1), (1, 0)
         self.first = [
             self.push(source, sq.chunk(ref), half, j, step)
@@ -120,6 +116,14 @@
             self.push(from_below, from_below, 1, 5, beside, start=False),
         ]
 
+    def source(self, own, here):
+        self.local = None
+        if own is None:
+            return self.sq.chunk(self.ref)
+        self.local = pltpu.make_async_copy(own, self.sq.chunk(self.ref), here)
+        self.local.start()
+        return own
+
     def push(self, source, target, half, j, step, start=True):
         block = pl.ds(half * self.half, self.half)
         copy = self.sq.copy(source.at[block], target.at[block], self.send.at[j], self.recv.at[j], step)
@@ -147,6 +151,24 @@
             copy.wait_send()
         if self.local is not None:
             self.local.wait()
+
+
+class DirectSpread(Spread):
+    def __init__(self, sq, ref, send, recv, own, here):
+        self.sq, self.ref = sq, ref
+        source = self.source(own, here)
+        self.first, self.onward = [], []
+        for j, step in enumerate(SQUARE):
+            copy = sq.copy(source, sq.chunk(ref), send.at[j], recv.at[j], step)
+            copy.start()
+            self.first.append(copy)
+
+    def wait_own(self):
+        self.first[0].wait_recv()
+
+    def wait_next(self):
+        self.first[1].wait_recv()
+        self.first[2].wait_recv()
 
 
 def row_blocks(rows, body, block=32):
@@ -366,7 +388,7 @@
         turn_down(at.core == at.section)
         row_blocks(rows, first_norm)
         sq.barrier()
-        ins = sq.spread(normed_in, s_send.at[0], s_recv.at[0])
+        ins = sq.spread(normed_in, s_send.at[0], s_recv.at[0], False)
         operand_copies[1].wait()
         operand_copies[2].wait()
         ins.wait_own()
@@ -391,7 +413,7 @@
             push.wait_recv()
         row_blocks(rows, second_norm)
         save(0)
-        mids = sq.spread(normed_mid, s_send.at[1], s_recv.at[1])
+        mids = sq.spread(normed_mid, s_send.at[1], s_recv.at[1], False)
         mids.wait_own()
         feed(sq.own)
         mids.wait_next()
@@ -509,7 +531,7 @@
         push_own(i)
     gain_copy.wait_recv()
     row_blocks(rows, first_norm)
-    ins = sq.spread(normed_in, s_send.at[0], s_recv.at[0])
+    ins = sq.spread(normed_in, s_send.at[0], s_recv.at[0], True)
 
     def advance(i):
         pass_on(i)
@@ -520,14 +542,13 @@
             arrive(i - 1)
 
     advance(0)
-    downs = sq.spread(v.grad_down, d_send, d_recv, v.out_grad.at[at.section], d_sem)
+    downs = sq.spread(v.grad_down, d_send, d_recv, True, v.out_grad.at[at.section], d_sem)
     id_copy.wait_recv()
     make_masks()
     mask_save = pltpu.make_async_copy(masks, v.masks, mask_sem)
     mask_save.start()
+    advance(1)
     ins.wait_recv()
-    advance(1)
-    downs.wait_recv()
     transpose_into(normed_in_t, normed_in)
     save(1)
     operand_copies[1].wait()
@@ -549,9 +570,9 @@
     for push in gives:
         push.wait_recv()
     row_blocks(rows, second_norm)
-    mids = sq.spread(normed_mid, s_send.at[1], s_recv.at[1])
+    mids = sq.spread(normed_mid, s_send.at[1], s_recv.at[1], True)
+    advance(7)
     mids.wait_recv()
-    advance(7)
     transpose_into(normed_mid_t, normed_mid)
     save(0, 2, 3, 4, 5, 6, 7, 8, 9, 10)
     feed(sq.next)
@@ -601,6 +622,7 @@
         for i in range(8):
             core_own[i].wait_recv()
 
+    downs.wait_recv()
     for push in [downs, ins, mids] + ends + list(z_copies.values()) + list(x_copies.values()):
         push.wait_send()
     for i in range(8):
@@ -1061,7 +1083,7 @@
         terms[1:2] = terms[1:2] + jnp.sum(upstream * normed, axis=0, keepdims=True)
 
     row_blocks(rows, through_mid)
-    mids = sq.spread(grad_branch, v.s_send, v.s_recv)
+    mids = sq.spread(grad_branch, v.s_send, v.s_recv, final_layer)
     reduce_some(0, 1)
     given(2)
     fetch(1)
@@ -1147,7 +1169,7 @@
             remote(v.grad_in, v.taken_grads, v.row_send.at[1], v.row_recv.at[1], across).start()
 
     else:
-        downs = sq.spread(v.next_down, v.d_send, v.d_recv, v.grad_in, v.d_sem)
+        downs = sq.spread(v.next_down, v.d_send, v.d_recv, False, v.grad_in, v.d_sem)
 
     if not final_layer:
         fetch(4)

time: 1090 us -> 992 us (0.910)
  Pallas kernels: 1050 us -> 952 us
    pallas_call x2, Pallas kernels: 564 us -> 515 us  [backward_layer(): pl.pallas_call(functools.partial(backward_kernel, dp_size, layer), out_sh...]
    pallas_call x2, Pallas kernels: 485 us -> 437 us  [forward_layer(): pl.pallas_call(functools.partial(forward_kernel, dp_size, layer), out_sha...]
where the time goes in v8:
time: 992 us; the launch traced here: 980 us
  Pallas kernels  952 us (96%)
  other arithmetic  17.1 us (2%)
    pallas_call x2, Pallas kernels, backward_layer(): pl.pallas_call(functools.partial(backward_kernel, dp_size, layer), out_sh...  515 us
    pallas_call x2, Pallas kernels, forward_layer(): pl.pallas_call(functools.partial(forward_kernel, dp_size, layer), out_sha...  437 us

profile of v8, /device:TPU:5, one launch (start us, length us, event | category | flops | bytes accessed | tf_op | source)
XLA Modules:
  0.0 980.1 jit_solution(10636515298358729137)
XLA Ops:
  0.6 0.0 copy-start.2
  0.7 0.0 copy-start.3
  0.7 0.6 multiply_cosine_fusion
  1.3 0.8 pad_maximum_fusion.refs_4_.refs_2_
  2.1 0.0 copy-done.2
  2.1 1.4 copy.27
  3.5 0.0 copy-done.3
  3.5 1.4 copy.28
  4.9 368.0 %forward_layer.2 = (bf16[2,4,2,256,3072]{4,3,2,1,0:T(8,128)(2,1)}, bf16[2,4,2,256,1024]{4,3,2,1,0:T(8,128)(2,1)}, bf16[2,4,2,256,2048]{4,3,2,1,0:T(8,128)(2,1)},...) custom-call(bf16[2,128,2048]{2,1,0:T(8,128)(2,1)} %refs_4_.1, ...), custom_call_target="tpu_custom_call" | custom-call | tf_op jit(solution)/shard_map/forward_layer/pallas_call | solution.py:724
  372.9 68.8 %forward_layer.3 = (f32[128,2048]{1,0:T(8,128)}, bf16[2048,512]{1,0:T(8,128)(2,1)}, bf16[2,256,512]{2,1,0:T(8,128)(2,1)}, bf16[2,256,512]{2,1,0:T(8,128)(2,1)}, ...) custom-call(bf16[128,2048]{1,0:T(8,128)(2,1)} %get-tuple-element.60., ...), custom_call_target="tpu_custom_call" | custom-call | tf_op jit(solution)/shard_map/forward_layer/pallas_call | solution.py:724
  441.8 106.0 %backward_layer.2 = (bf16[128,2048]{1,0:T(8,128)(2,1)}, bf16[5,4,256,1024]{3,2,1,0:T(8,128)(2,1)}, bf16[5,4,256,1024]{3,2,1,0:T(8,128)(2,1)}, f32[2,2048]{1,0:T(...) custom-call(bf16[2,128,2048]{2,1,0:T(8,128)(2,1)} %refs_0_.3, ...), custom_call_target="tpu_custom_call" | custom-call | tf_op jit(solution)/shard_map/backward_layer/pallas_call | solution.py:1398
  547.8 409.2 %backward_layer.3 = (bf16[128,2048]{1,0:T(8,128)(2,1)}, bf16[9,4,256,1024]{3,2,1,0:T(8,128)(2,1)}, bf16[9,4,256,1024]{3,2,1,0:T(8,128)(2,1)}, bf16[7,4,256,1024]...) custom-call(bf16[128,2048]{1,0:T(8,128)(2,1)} %get-tuple-element.83., ...), custom_call_target="tpu_custom_call" | custom-call | tf_op jit(solution)/shard_map/backward_layer/pallas_call | solution.py:1398
  957.0 11.1 %convert_reduce_fusion = (f32[256,2048]{1,0:T(8,128)S(1)}, f32[256,2048]{1,0:T(8,128)}, f32[256,2048]{1,0:T(8,128)}, f32[256,2048]{1,0:T(8,128)}, f32[256,2048]{1,0:T(8,128)}, /*index=5*/f32[256,2048]{1,0:T(8,128)}) fusion(bf16[7,2,256,2048]{3,2,1,0:T(8,128)(2,1)} %get-tuple-element.106), kind=kLoop, calls=%fused_computation | loop fusion | flops 9437184 | bytes 25165824 | tf_op jit(solution)/shard_map/reduce_sum | solution.py:1463
  968.1 2.9 copy.29
  971.0 1.8 copy.30
  972.8 1.7 slice_bitcast_fusion.1
  974.4 0.0 copy-start.1
  974.5 0.0 copy-start.6
  974.5 0.0 copy-start.7
  974.5 1.1 convert_reduce_fusion.6
  975.6 0.0 copy-start
  975.6 1.1 convert_reduce_fusion.7
  976.7 0.0 copy-done.1
  976.8 0.0 copy-done.6
  976.8 0.0 copy-done.7
  976.8 1.1 maximum_select_fusion.1
  977.9 0.0 copy-done
  977.9 0.0 copy-done.4
  977.9 0.0 copy-done.5
  977.9 1.1 maximum_select_fusion
  979.0 0.0 copy-done.8
  979.0 0.6 fusion
  (7 shorter events, 0.0 us)
Async XLA Ops:
  0.6 1.5 copy-start.2
  0.7 2.9 copy-start.3
  974.4 2.3 copy-start.1
  974.5 2.3 copy-start.6
  974.5 2.3 copy-start.7
  975.6 2.3 copy-start
  975.6 2.3 copy-start.4
  975.6 2.3 copy-start.5
  976.8 2.3 copy-start.8

commit v9 on v8

--- a/solution.py
+++ b/solution.py
@@ -169,6 +169,47 @@
     def wait_next(self):
         self.first[1].wait_recv()
         self.first[2].wait_recv()
+
+
+class Collect:
+    def __init__(self, sq, parts, landed, send, recv):
+        self.sq, self.parts, self.landed, self.send, self.recv = sq, parts, landed, send, recv
+        self.half = sq.rows // 2
+        self.pushes = []
+
+    def push(self, source, half, slot, target_half, j, step):
+        copy = self.sq.copy(
+            source.at[pl.ds(half * self.half, self.half)],
+            self.landed.at[slot, pl.ds(target_half * self.half, self.half)],
+            self.send.at[j],
+            self.recv.at[j],
+            step,
+        )
+        copy.start()
+        self.pushes.append(copy)
+
+    def after_next(self):
+        across = self.sq.chunk(self.parts, 1, 1)
+        self.push(across, 0, 2, 0, 0, (0, 1))
+        self.push(across, 1, 2, 1, 1, (1, 0))
+        self.push(self.sq.chunk(self.parts, 1, 0), 1, 1, 1, 2, (1, 0))
+
+    def after_own(self):
+        beside, below = self.sq.chunk(self.parts, 0, 1), self.sq.chunk(self.parts, 1, 0)
+        self.push(beside, 0, 0, 0, 3, (0, 1))
+        for half, chunk, slot, j, step in ((0, below, 1, 4, (1, 0)), (1, beside, 0, 5, (0, 1))):
+            self.pushes[half].wait_recv()
+            rows = pl.ds(half * self.half, self.half)
+            chunk[rows] = (chunk[rows].astype(f32) + self.landed[2, rows].astype(f32)).astype(bf16)
+            self.push(chunk, half, slot, half, j, step)
+
+    def wait_recv(self):
+        for copy in self.pushes[2:]:
+            copy.wait_recv()
+
+    def wait_send(self):
+        for copy in self.pushes:
+            copy.wait_send()
 
 
 def row_blocks(rows, body, block=32):
@@ -337,7 +378,7 @@
 
     def collected(block, which):
         total = sq.chunk(parts)[block].astype(f32)
-        for j in range(len(SQUARE)):
+        for j in range(3 if streams else 2):
             total = total + landed[which, j, block].astype(f32)
         return total
 
@@ -401,10 +442,12 @@
         retain(sq.next)
         loads_wait(4)
         give_back(sq.next, merged, out_t)
-        gives = give(1, 0)
+        collect = Collect(sq, parts, landed.at[0], g_send.at[0], g_recv.at[0])
+        collect.after_next()
         retain(sq.own)
         give_back(sq.own, merged, out_t)
-        gives += give(0, 0)
+        collect.after_own()
+        gives = [collect]
         save(5, 6, 9)
         transpose_into(normed_in_t, normed_in)
         save(1)
@@ -683,8 +726,8 @@
         pltpu.VMEM((2, 3, rows, width), bf16),
         dma((2, 6)),
         dma((2, 6)),
-        dma((2, 3)),
-        dma((2, 3)),
+        dma((2, 6)),
+        dma((2, 6)),
     ]
     if streams:
         out_shape = (
@@ -883,13 +926,19 @@
 
     def collected(block, given, land):
         total = sq.chunk(given)[block].astype(f32)
-        for j in range(len(SQUARE)):
+        for j in range(3 if final_layer else 2):
             total = total + land[j, block].astype(f32)
         return total
 
     def exchange(source, weight, first, size, target, land, which):
         give_back(sq.next, source, weight, first, size, target)
         send, recv = v.g_send.at[which], v.g_recv.at[which]
+        if not final_layer:
+            collect = Collect(sq, target, land, send, recv)
+            collect.after_next()
+            give_back(sq.own, source, weight, first, size, target)
+            collect.after_own()
+            return [collect]
         pushes = [sq.give(target, land, send, recv, j) for j in (1, 2)]
         give_back(sq.own, source, weight, first, size, target)
         pushes.append(sq.give(target, land, send, recv, 0))
@@ -1364,8 +1413,8 @@
         dma((19,)),
         dma((6,)),
         dma((6,)),
-        dma((3, 3)),
-        dma((3, 3)),
+        dma((3, 6)),
+        dma((3, 6)),
         dma((count,)),
         dma((count,)),
         dma((2,)),

time: 992 us -> 989 us (level)
  no operation moved by 1% of the time
where the time goes in v9:
time: 989 us; the launch traced here: 976 us
  Pallas kernels  948 us (96%)
  other arithmetic  17.1 us (2%)
    pallas_call x2, Pallas kernels, backward_layer(): pl.pallas_call(functools.partial(backward_kernel, dp_size, layer), out_sh...  520 us
    pallas_call x2, Pallas kernels, forward_layer(): pl.pallas_call(functools.partial(forward_kernel, dp_size, layer), out_sha...  428 us

profile of v9, /device:TPU:5, one launch (start us, length us, event | category | flops | bytes accessed | tf_op | source)
XLA Modules:
  0.0 976.2 jit_solution(4782873758469806921)
XLA Ops:
  0.6 0.0 copy-start.2
  0.7 0.0 copy-start.3
  0.7 0.6 multiply_cosine_fusion
  1.3 0.8 pad_maximum_fusion.refs_4_.refs_2_
  2.1 0.0 copy-done.2
  2.1 1.4 copy.27
  3.5 0.0 copy-done.3
  3.5 1.4 copy.28
  4.9 368.1 %forward_layer.2 = (bf16[2,4,2,256,3072]{4,3,2,1,0:T(8,128)(2,1)}, bf16[2,4,2,256,1024]{4,3,2,1,0:T(8,128)(2,1)}, bf16[2,4,2,256,2048]{4,3,2,1,0:T(8,128)(2,1)},...) custom-call(bf16[2,128,2048]{2,1,0:T(8,128)(2,1)} %refs_4_.1, ...), custom_call_target="tpu_custom_call" | custom-call | tf_op jit(solution)/shard_map/forward_layer/pallas_call | solution.py:767
  373.0 59.7 %forward_layer.3 = (f32[128,2048]{1,0:T(8,128)}, bf16[2048,512]{1,0:T(8,128)(2,1)}, bf16[2,256,512]{2,1,0:T(8,128)(2,1)}, bf16[2,256,512]{2,1,0:T(8,128)(2,1)}, ...) custom-call(bf16[128,2048]{1,0:T(8,128)(2,1)} %get-tuple-element.60., ...), custom_call_target="tpu_custom_call" | custom-call | tf_op jit(solution)/shard_map/forward_layer/pallas_call | solution.py:767
  432.8 113.0 %backward_layer.2 = (bf16[128,2048]{1,0:T(8,128)(2,1)}, bf16[5,4,256,1024]{3,2,1,0:T(8,128)(2,1)}, bf16[5,4,256,1024]{3,2,1,0:T(8,128)(2,1)}, f32[2,2048]{1,0:T(...) custom-call(bf16[2,128,2048]{2,1,0:T(8,128)(2,1)} %refs_0_.3, ...), custom_call_target="tpu_custom_call" | custom-call | tf_op jit(solution)/shard_map/backward_layer/pallas_call | solution.py:1447
  545.8 407.3 %backward_layer.3 = (bf16[128,2048]{1,0:T(8,128)(2,1)}, bf16[9,4,256,1024]{3,2,1,0:T(8,128)(2,1)}, bf16[9,4,256,1024]{3,2,1,0:T(8,128)(2,1)}, bf16[7,4,256,1024]...) custom-call(bf16[128,2048]{1,0:T(8,128)(2,1)} %get-tuple-element.83., ...), custom_call_target="tpu_custom_call" | custom-call | tf_op jit(solution)/shard_map/backward_layer/pallas_call | solution.py:1447
  953.1 11.1 %convert_reduce_fusion = (f32[256,2048]{1,0:T(8,128)S(1)}, f32[256,2048]{1,0:T(8,128)}, f32[256,2048]{1,0:T(8,128)}, f32[256,2048]{1,0:T(8,128)}, f32[256,2048]{1,0:T(8,128)}, /*index=5*/f32[256,2048]{1,0:T(8,128)}) fusion(bf16[7,2,256,2048]{3,2,1,0:T(8,128)(2,1)} %get-tuple-element.106), kind=kLoop, calls=%fused_computation | loop fusion | flops 9437184 | bytes 25165824 | tf_op jit(solution)/shard_map/reduce_sum | solution.py:1512
  964.2 2.9 copy.29
  967.1 1.8 copy.30
  968.9 1.7 slice_bitcast_fusion.1
  970.6 0.0 copy-start.1
  970.6 0.0 copy-start.6
  970.6 0.0 copy-start.7
  970.6 1.1 convert_reduce_fusion.6
  971.7 0.0 copy-start
  971.7 1.1 convert_reduce_fusion.7
  972.9 0.0 copy-done.1
  972.9 0.0 copy-done.6
  972.9 0.0 copy-done.7
  972.9 1.1 maximum_select_fusion.1
  974.0 0.0 copy-done
  974.0 0.0 copy-done.4
  974.0 0.0 copy-done.5
  974.0 1.1 maximum_select_fusion
  975.2 0.0 copy-done.8
  975.2 0.6 fusion
  (7 shorter events, 0.0 us)
Async XLA Ops:
  0.6 1.5 copy-start.2
  0.7 2.9 copy-start.3
  970.6 2.3 copy-start.1
  970.6 2.3 copy-start.6
  970.6 2.3 copy-start.7
  971.7 2.3 copy-start
  971.7 2.3 copy-start.4
  971.7 2.3 copy-start.5
  972.9 2.3 copy-start.8
